TPU v7x, 256 devices: a whole 4x4x8 slice. The times are simulated.
256 devices in a mesh: tile: 64 (over z, y, core), slot: 4 (over x).
Axes of the slice: x: 4, y: 4, z: 8, core: 2. Of those that a mesh axis runs over, the one named last changes fastest.
Arguments:
- departure: bfloat16 [24576, 100], P(('tile', 'slot')), may hold values from -6 to 6
- inv_var: float32 [100], replicated, may hold values from 0.25 to 4
- k_matrix: bfloat16 [24576, 100, 411], P(('tile', 'slot')), may hold values from -0.625 to 0.625
- frac_row: bfloat16 [24576], P(('tile', 'slot')), may hold values from 0 to 1
- frac_col: bfloat16 [24576], P(('tile', 'slot')), may hold values from 0 to 1
- dest_tile: int32 [24576, 1], P(('tile', 'slot')), may hold values from 0 to 63; in each aligned block of 96 rows (0 to 95, 96 to 191, ...) at most 4 rows name the same one
- cell_row: int32 [24576], P(('tile', 'slot')), may hold values from 0 to 31
- cell_col: int32 [24576], P(('tile', 'slot')), may hold values from 0 to 254
- predictors: bfloat16 [24576, 8], P(('tile', 'slot')), may hold values from -6 to 6
- scan_pos: int32 [24576], P(('tile', 'slot')), may hold values from 0 to 119
Outputs:
- grid_adjoint: float32 [2048, 256, 411], P(('tile', 'slot'))
- bias_grad: float32 [100, 128], replicated
Inputs may be any that keep to these rules, and one draw needn't show every extreme that they name: `dest_tile`: among the observations of one device, no tile is named by more than 4 of them, a bound that some block reaches.
All inputs are finite; a program needn't handle non-finite values.
Results may differ from a plain program's by a relative error of at most 0.004.
Values may be sent and summed in bfloat16 or wider, within the bound.
No kernel may reach another device: no remote copies, remote signals or barrier semaphores. Data moves between devices by JAX's collectives and lax.ppermute only.
A program may use at most 128 MiB of HBM per device.

v0:
```python
import math

import jax
import jax.numpy as jnp
from jax import lax
from jax.sharding import PartitionSpec as P

NSCAN = 120
GR = 32
GC = 256


def from_behind(value, axis, steps):
    count = lax.axis_size(axis)
    pairs = [(source, (source + steps) % count) for source in range(count)]
    return lax.ppermute(value, axis, pairs)


def spread(rows_in, coords, height, width):
    levels = rows_in.shape[1]
    row_frac = coords[:, 0].astype(jnp.float32)
    col_frac = coords[:, 1].astype(jnp.float32)
    row_at = coords[:, 2].astype(jnp.int32)
    col_at = coords[:, 3].astype(jnp.int32)
    anchor = row_at * width + col_at
    indices = jnp.concatenate([anchor, anchor + 1, anchor + width, anchor + width + 1])
    weights = jnp.concatenate(
        [
            (1.0 - row_frac) * (1.0 - col_frac),
            (1.0 - row_frac) * col_frac,
            row_frac * (1.0 - col_frac),
            row_frac * col_frac,
        ]
    )
    widened = rows_in.astype(jnp.float32)
    values = weights[:, None] * jnp.concatenate([widened, widened, widened, widened], 0)
    column_grid = jnp.zeros(((height + 1) * width, levels), jnp.float32).at[indices].add(values)
    return column_grid.reshape(height + 1, width, levels)


def placement_of(target, buckets, capacity):
    matches = (target[:, None] == jnp.arange(buckets, dtype=jnp.int32)[None, :]).astype(jnp.int32)
    ahead = jnp.cumsum(matches, 0) - matches
    ranked = jnp.sum(ahead * matches, 1)
    return target * capacity + ranked


def per_device(
    departure,
    inv_var,
    k_matrix,
    frac_row,
    frac_col,
    dest_tile,
    cell_row,
    cell_col,
    predictors,
    scan_pos,
):
    n_tile = lax.axis_size("tile")
    n_slot = lax.axis_size("slot")
    obs_dev = departure.shape[0]
    levels = k_matrix.shape[2]
    weighted = (departure.astype(jnp.float32) * inv_var[None, :]).astype(jnp.bfloat16)
    profile = jnp.einsum(
        "oc,ocv->ov", weighted, k_matrix, preferred_element_type=jnp.float32
    ).astype(jnp.bfloat16)
    capacity = max(2, 8 * obs_dev // (3 * n_tile))
    target = dest_tile[:, 0]
    placed = placement_of(target, n_tile, capacity)
    coords = jnp.stack(
        [frac_row, frac_col, cell_row.astype(jnp.bfloat16), cell_col.astype(jnp.bfloat16)], 1
    )
    send_rows = (
        jnp.zeros((n_tile * capacity, levels), jnp.bfloat16)
        .at[placed]
        .set(profile)
        .reshape(n_tile, capacity, levels)
    )
    send_coords = (
        jnp.zeros((n_tile * capacity, 4), jnp.bfloat16)
        .at[placed]
        .set(coords)
        .reshape(n_tile, capacity, 4)
    )
    got_rows, got_coords = (
        lax.all_to_all(send_rows, "tile", split_axis=0, concat_axis=0, tiled=True),
        lax.all_to_all(send_coords, "tile", split_axis=0, concat_axis=0, tiled=True),
    )
    got_rows = got_rows.reshape(-1, levels)
    got_coords = got_coords.reshape(-1, 4)
    column_grid = spread(got_rows, got_coords, GR, GC)
    arrived = from_behind(column_grid[GR], "tile", 1)
    interior = column_grid[:GR].at[0].add(arrived)
    result = lax.psum_scatter(interior, "slot", scatter_dimension=0, tiled=True)
    indicator = (scan_pos[:, None] == jnp.arange(NSCAN, dtype=jnp.int32)[None, :]).astype(
        jnp.bfloat16
    )
    basis_rows = jnp.concatenate([predictors, indicator], 1)
    local_bias = lax.dot_general(
        weighted, basis_rows, (((0,), (0,)), ((), ())), preferred_element_type=jnp.float32
    )
    summed = lax.psum(local_bias, ("tile", "slot"))
    return (result, summed / math.sqrt(obs_dev * n_tile * n_slot))


def solution(mesh):
    placed = (
        P(("tile", "slot"), None),
        P(),
        P(("tile", "slot"), None, None),
        P(("tile", "slot")),
        P(("tile", "slot")),
        P(("tile", "slot"), None),
        P(("tile", "slot")),
        P(("tile", "slot")),
        P(("tile", "slot"), None),
        P(("tile", "slot")),
    )
    return jax.shard_map(
        per_device,
        mesh=mesh,
        in_specs=placed,
        out_specs=(P(("tile", "slot"), None, None), P()),
        check_vma=False,
    )
```

profile of v0, /device:TPU:1, one launch (start us, length us, event | category | flops | bytes accessed | tf_op | source)
XLA Modules:
  0.0 257.6 jit_solution(12144196481266234520)
XLA Ops:
  7.2 0.7 convert_bitcast_fusion
  7.8 0.7 pad_maximum_fusion.1
  8.5 0.1 copy.25
  8.7 0.7 fusion.18
  9.4 0.1 reduce_window_sum.11
  9.5 0.8 select_reduce_fusion
  10.4 0.7 fusion.29
  11.0 0.8 scatter_custom_fusion
  11.9 1.1 copy.26
  13.0 13.2 %all-to-all-start = ((bf16[64,4,4]{1,2,0:T(4,128)(2,1)}), bf16[64,4,4]{1,2,0:T(4,128)(2,1)S(1)}, u32[]{:S(2)}, u32[]{:S(2)}) async-start(bf16[64,4,4]{1,2,0:T(4,128)(2,1)} %copy.26), calls=%async_computation | async-start | bytes 131072 | tf_op jit(solution)/shard_map/all_to_all | solution.py:88
  26.2 0.8 fusion.26
  26.9 14.6 %fusion = f32[96,1,411]{2,1,0:T(1,128)S(1)} fusion(bf16[96,100,411]{2,0,1:T(8,128)(2,1)} %param.14, bf16[96,100,1]{1,0,2:T(8,128)(2,1)S(1)} %fusion.26), kind=kOutput, calls=%fused_computation.3 | convolution fusion | flops 7891200 | bytes 8068224 | tf_op jit(solution)/shard_map/oc,ocv->ov/dot_general | solution.py:65
  41.5 1.0 scatter_custom_fusion.1
  42.6 0.8 reshape.184
  43.4 10.5 %all-to-all-start.1 = ((bf16[64,4,411]{2,1,0:T(4,128)(2,1)}), bf16[64,4,411]{2,1,0:T(4,128)(2,1)S(1)}, u32[]{:S(2)}, u32[]{:S(2)}) async-start(bf16[64,4,411]{2,1,0:T(4,128)(2,1)} %reshape.184), calls=%async_computation.1 | async-start | bytes 524288 | tf_op jit(solution)/shard_map/all_to_all | solution.py:87
  53.9 0.1 reshape.183
  54.1 12.9 %all-to-all-done.1 = bf16[64,4,411]{2,1,0:T(4,128)(2,1)S(1)} async-done(((bf16[64,4,411]{2,1,0:T(4,128)(2,1)}), bf16[64,4,411]{2,1,0:T(4,128)(2,1)S(1)}, u32[]{:S(2)}, u32[]{:S(2)}) %all-to-all-start.1) | async-done | bytes 210464 | tf_op jit(solution)/shard_map/all_to_all | solution.py:87
  67.0 0.1 convert_element_type.63
  67.1 15.4 %scatter_custom_fusion.2 = f32[8448,411]{1,0:T(8,128)} fusion(s32[1024]{0:T(1024)S(1)} %bitcast.31, f32[]{:T(128)} %constant.45.clone.1, bf16[256,411]{1,0:T(8,128)(2,1)S(1)} %convert_element_type.63, bf16[]{:T(256)} %constant.64, f32[1024]{0:T(1024)S(1)} %pad_maximum_fusion), kind=kCustom, calls=%fused_computation.5 | custom fusion | flops 4208640 | bytes 14154758 | tf_op jit(solution)/shard_map/scatter-add | solution.py:37
  82.6 1.1 slice.60
  83.6 0.8 collective-permute-start
  84.4 11.6 %slice.58 = f32[8192,411]{1,0:T(8,128)} slice(f32[8448,411]{1,0:T(8,128)} %scatter_custom_fusion.2), slice={[0:8192], [0:411]} | slice | bytes 26935296 | tf_op jit(solution)/shard_map/slice | solution.py:94
  96.0 19.2 %copy.29 = f32[32,256,411]{1,0,2:T(8,128)} copy(f32[32,256,411]{2,1,0:T(8,128)} %bitcast.29) | data formatting | bytes 26935296 | tf_op jit(solution)/shard_map/slice | solution.py:94
  115.2 1.2 fusion.14
  116.3 0.5 copy.30
  116.9 10.6 %scatter-add.13 = f32[32,256,411]{1,0,2:T(8,128)} dynamic-update-slice(f32[32,256,411]{1,0,2:T(8,128)} %copy.29, f32[1,256,411]{1,0,2:T(1,128)S(1)} %copy.30, s32[]{:T(128)} %constant.48.clone.1, s32[]{:T(128)} %constant.48.clone.1, s32[]{:T(128)} %constant.48.clone.1) | dynamic-update-slice | bytes 841732 | tf_op jit(solution)/shard_map/scatter-add | solution.py:94
  127.5 0.1 copy.31
  127.6 0.1 fusion.19
  127.7 0.2 fusion.22
  127.9 78.9 %psum.7 = f32[100,128]{1,0:T(8,128)S(1)} all-reduce(f32[100,128]{1,0:T(8,128)S(1)} %fusion.22), channel_id=1, replica_groups=mesh['tile'=64,'slot'=4] {'tile','slot'}, use_global_device_ids=true, to_apply=%region_6.7 | all-reduce | flops 12800 | bytes 102400 | tf_op jit(solution)/shard_map/psum | solution.py:103
  206.8 0.6 broadcast_multiply_fusion
  207.4 43.3 %reduce-scatter.2.cloned.1.call-done = f32[8,256,411]{1,0,2:T(8,128)} async-done(((f32[32,256,411]{1,0,2:T(8,128)}), f32[8,256,411]{1,0,2:T(8,128)}) %reduce-scatter.2.cloned.1.call-update) | async-done | bytes 3366928 | tf_op jit(solution)/shard_map/reduce_scatter | solution.py:95
  (19 shorter events, 0.1 us)
Async XLA Ops:
  13.0 30.4 %all-to-all-start = ((bf16[64,4,4]{1,2,0:T(4,128)(2,1)}), bf16[64,4,4]{1,2,0:T(4,128)(2,1)S(1)}, u32[]{:S(2)}, u32[]{:S(2)}) async-start(bf16[64,4,4]{1,2,0:T(4,128)(2,1)} %copy.26), calls=%async_computation | async-start | bytes 131072 | tf_op jit(solution)/shard_map/all_to_all | solution.py:88
  43.4 23.6 %all-to-all-start.1 = ((bf16[64,4,411]{2,1,0:T(4,128)(2,1)}), bf16[64,4,411]{2,1,0:T(4,128)(2,1)S(1)}, u32[]{:S(2)}, u32[]{:S(2)}) async-start(bf16[64,4,411]{2,1,0:T(4,128)(2,1)} %reshape.184), calls=%async_computation.1 | async-start | bytes 524288 | tf_op jit(solution)/shard_map/all_to_all | solution.py:87
  53.8 196.9 %reduce-scatter.2.cloned.1.call-start = ((), (), s32[]{:S(2)}) async-start(), calls=%async_computation.3 | async-start | bytes 16834560 | tf_op jit(solution)/shard_map/reduce_scatter | solution.py:95
  83.6 31.5 %collective-permute-start = (f32[256,411]{1,0:T(8,128)S(1)}, f32[256,411]{1,0:T(8,128)S(1)}, u32[]{:S(2)}, u32[]{:S(2)}) collective-permute-start(f32[256,411]{1,0:T(8,128)S(1)} %slice.60), channel_id=1, source_target_pairs={{0,4},{4,8},{8,12},{12,16},{16,20},{20,24},{24,28},{28,32},{32,36}... | collective-permute-start | bytes 1262600 | tf_op jit(solution)/shard_map/ppermute | solution.py:16
  115.1 12.3 %copy-start.2 = (bf16[96,8]{0,1:T(8,128)(2,1)S(1)}, bf16[96,8]{0,1:T(8,128)(2,1)}, u32[]{:S(2)}) copy-start(bf16[96,8]{0,1:T(8,128)(2,1)} %param.20) | copy-start | bytes 4612
  115.1 12.4 %copy-start.3 = (s32[96]{0:T(128)S(1)}, s32[96]{0:T(128)}, u32[]{:S(2)}) copy-start(s32[96]{0:T(128)} %param.21) | copy-start | bytes 1156
  115.1 12.5 %copy-start = (bf16[96,100]{1,0:T(8,128)(2,1)S(1)}, bf16[96,100]{1,0:T(8,128)(2,1)}, u32[]{:S(2)}) copy-start(bf16[96,100]{1,0:T(8,128)(2,1)} %param.12) | copy-start | bytes 57604
  115.1 12.5 %copy-start.1 = (f32[100]{0:T(128)S(1)}, f32[100]{0:T(128)}, u32[]{:S(2)}) copy-start(f32[100]{0:T(128)} %param.13) | copy-start | bytes 1204
Sparse Core Ops, SparseCore 0:
  127.6 123.1 reduce-scatter.1
where the time goes:
time: 259 us; the launch traced here: 258 us
  blocking collectives  78.9 us (30%)
  waiting for transfers between devices  56.2 us (22%)
  local copies, waits for them, and re-layouts  47.2 us (18%)
  starting transfers between devices  24.4 us (9%)
  other arithmetic  21.8 us (8%)
  matrix products  14.8 us (6%)
  between operations  14.2 us (5%)
    psum x1, blocking collectives, per_device(): summed = lax.psum(local_bias, ('tile', 'slot'))  78.9 us
    reduce_scatter x1, waiting for transfers between devices, per_device(): result = lax.psum_scatter(interior, 'slot', scatter_dimension=0, tiled=True)  43.3 us
    slice x2, local copies, waits for them, and re-layouts, per_device(): interior = column_grid[:GR].at[0].add(arrived)  30.7 us
    scatter-add x1, other arithmetic, spread(): jnp.zeros(((height + 1) * width, levels), jnp.float32).at[indices]  15.4 us
    dot_general x1, matrix products, per_device(): jnp.einsum('oc,ocv->ov', weighted, k_matrix, preferred_element_type=jnp.f...  14.6 us
    all_to_all x1, starting transfers between devices, per_device(): lax.all_to_all(send_coords, 'tile', split_axis=0, concat_axis=0, tiled=True)  13.2 us
    all_to_all x1, waiting for transfers between devices, per_device(): lax.all_to_all(send_rows, 'tile', split_axis=0, concat_axis=0, tiled=True)  12.9 us
    scatter-add x1, local copies, waits for them, and re-layouts, per_device(): interior = column_grid[:GR].at[0].add(arrived)  10.6 us
  transfers between devices with their start and end apart: 4, of which 2 were waited for; matrix products, arithmetic and copies ran while one was open for 19% of the time, Pallas kernels for 0%

commit v1 on v0

v1 whole, which is shorter than its diff:
```python
import functools
import math

import jax
import jax.numpy as jnp
from jax import lax
from jax.experimental import pallas as pl
from jax.experimental.pallas import tpu as pltpu
from jax.sharding import PartitionSpec as P

F32 = jnp.float32
BF16 = jnp.bfloat16
NT = (((1,), (1,)), ((), ()))
NN = (((1,), (0,)), ((), ()))

CAP = 4
GR = 32
GC = 256
LANES = 512
VROWS = 432
VCHUNK = 48
CHUNK_ROW = 416
BLOCK = 8
VMEM = 48 * 1024 * 1024


def iota(shape, dim):
    return lax.broadcasted_iota(jnp.int32, shape, dim)


def dot(a, b, dims):
    return lax.dot_general(a, b, dims, preferred_element_type=F32)


def ones_where(mask):
    return jnp.where(mask, 1.0, 0.0).astype(BF16)


def send_kernel(dep, inv, k_hbm, tile, frow, fcol, crow, ccol, predt, scan, out, kbuf, acc, sems, *, steps):
    chans, obs, levels = k_hbm.shape
    per = chans // steps
    copies = [
        pltpu.make_async_copy(k_hbm.at[pl.ds(i * per, per)], kbuf.at[pl.ds(i * per, per)], sems.at[i])
        for i in range(steps)
    ]
    for copy in copies:
        copy.start()
    slots = out.shape[0]
    wbf = (dep[...].astype(F32) * inv[...]).astype(BF16)
    w = wbf.astype(F32)

    tr = jnp.broadcast_to(tile[...].astype(F32), (obs, obs))
    ri, ci = iota((obs, obs), 0), iota((obs, obs), 1)
    tc = jnp.sum(jnp.where(ri == ci, tr, 0.0), 1, keepdims=True)
    rank = jnp.sum(jnp.where((tc == tr) & (ri < ci), 1.0, 0.0), 0, keepdims=True)
    slot = (tile[...].astype(F32) * CAP + rank).astype(jnp.int32)
    sel = ones_where(iota((slots, obs), 0) == slot)

    base = levels - (LANES - 128)
    rows = iota((128, obs), 0)
    place = jnp.where(rows == base, frow[...].astype(F32), 0.0)
    place = jnp.where(rows == base + 1, fcol[...].astype(F32), place)
    place = jnp.where(rows == base + 2, crow[...].astype(F32), place)
    place = jnp.where(rows == base + 3, ccol[...].astype(F32), place)
    extra = dot(sel, place.astype(BF16), NT)

    npred = predt.shape[0]
    kinds = 128
    ind = jnp.where(iota((kinds - npred, obs), 0) == scan[...], 1.0, 0.0)
    basist = jnp.concatenate([predt[...].astype(F32), ind], 0).astype(BF16)
    biast = dot(basist, wbf, NN)
    hi = biast.astype(BF16)
    lo = (biast - hi.astype(F32)).astype(BF16)
    half = chans // 2
    first = base + 4
    er, ec = iota((chans, 128), 0), iota((chans, 128), 1)
    parts = []
    for h in range(2):
        e = ones_where((ec == er - h * half + first) & (er >= h * half) & (er < (h + 1) * half))
        f = ones_where((ec == er - h * half + first + half) & (er >= h * half) & (er < (h + 1) * half))
        parts.append(dot(hi, e, NN) + dot(lo, f, NN))
    extra = extra + jnp.concatenate(parts, 0)

    acc[...] = jnp.zeros(acc.shape, F32)
    for i in range(steps):
        copies[i].wait()
        for r in range(0, obs, 16):
            total = acc[r : r + 16, 0:levels]
            for c in range(i * per, (i + 1) * per):
                total = total + w[r : r + 16, c : c + 1] * kbuf[c, r : r + 16, :].astype(F32)
            acc[r : r + 16, 0:levels] = total
    placed = dot(sel, acc[...].astype(BF16), NN)
    out[:, 0 : LANES - 128] = placed[:, 0 : LANES - 128].astype(BF16)
    out[:, LANES - 128 : LANES] = (placed[:, LANES - 128 : LANES] + extra).astype(BF16)


def turn_kernel(got, out, *, levels, half):
    slots = got.shape[0]
    out[0:CHUNK_ROW, :] = jnp.transpose(got[...].astype(F32))[0:CHUNK_ROW, :].astype(BF16)
    pick = ones_where(iota((8, slots), 1) % CAP == iota((8, slots), 0))
    total = dot(pick, got[:, LANES - 128 : LANES], NN)
    first = levels - (LANES - 128) + 4
    lane = iota((8, 128), 1)
    kept = 128 - first - half
    chunk = jnp.where(lane < half, pltpu.roll(total, 128 - first, 1), 0.0)
    chunk = chunk + jnp.where(lane < kept, pltpu.roll(total, 128 - first - half, 1), 0.0)
    high = chunk.astype(BF16).astype(F32)
    both = jnp.concatenate([high, chunk - high], 0)
    out[CHUNK_ROW:VROWS, 0:128] = both.astype(BF16)
    out[CHUNK_ROW:VROWS, 128:slots] = jnp.zeros((VROWS - CHUNK_ROW, slots - 128), BF16)


def coords_of(refs, levels, k):
    tops = [ref[CHUNK_ROW - 16 : CHUNK_ROW, :].astype(F32) for ref in refs]
    at = levels + k - (CHUNK_ROW - 16)
    return jnp.concatenate([top[at : at + 1, :] for top in tops], 1)


def prep_kernel(first_row, a0, a1, a2, a3, spill, colw, roww, chunk, *, levels):
    refs = (a0, a1, a2, a3)
    total = sum([r[CHUNK_ROW : CHUNK_ROW + 16, 0:128].astype(F32) for r in refs])
    chunk[...] = total[0:8, :] + total[8:16, :]
    fr, fc, cr, cc = [coords_of(refs, levels, k) for k in range(4)]
    n = fr.shape[1]
    cols = iota((GC, n), 0)
    at = cc.astype(jnp.int32)
    cw = jnp.where(cols == at, 1.0 - fc, 0.0) + jnp.where(cols == at + 1, fc, 0.0)
    cw = cw.astype(BF16)
    colw[...] = cw
    row = cr.astype(jnp.int32)
    rel = iota((BLOCK, n), 0) + first_row[0]
    roww[...] = jnp.where(rel == row, 1.0 - fr, 0.0) + jnp.where(rel == row + 1, fr, 0.0)
    last = jnp.where(row == GR - 1, fr, 0.0)
    part = a0.shape[1]
    out = jnp.zeros((CHUNK_ROW, GC), F32)
    for j, ref in enumerate(refs):
        lhs = (ref[0:CHUNK_ROW, :].astype(F32) * last[:, j * part : (j + 1) * part]).astype(BF16)
        out = out + dot(lhs, cw[:, j * part : (j + 1) * part], NT)
    spill[0:CHUNK_ROW, :] = out.astype(BF16)
    spill[CHUNK_ROW:VROWS, :] = jnp.zeros((VROWS - CHUNK_ROW, GC), BF16)


def grid_kernel(a0, a1, a2, a3, colw, roww, spill, out):
    part = a0.shape[1]
    total = jnp.zeros((VCHUNK * BLOCK, GC), F32)
    for j, ref in enumerate((a0, a1, a2, a3)):
        cols = slice(j * part, (j + 1) * part)
        lhs = ref[...].astype(F32)[:, None, :] * roww[:, cols][None, :, :]
        lhs = lhs.reshape(VCHUNK * BLOCK, part).astype(BF16)
        total = total + dot(lhs, colw[:, cols], NT)
    total = total.reshape(VCHUNK, BLOCK, GC)
    first = iota((VCHUNK, BLOCK, GC), 1) == 0
    out[...] = total + jnp.where(first, spill[...].astype(F32)[:, None, :], 0.0)


def bias_kernel(got, out, *, half, scale):
    t = jnp.transpose(got[...])
    n = got.shape[0] // 2
    out[0:half, :] = t[0:half, 0:n] * scale
    out[half : 2 * half, :] = t[0:half, n : 2 * n] * scale


def whole(shape):
    return pl.BlockSpec(shape, lambda *_: (0,) * len(shape))


VM = pl.BlockSpec(memory_space=pltpu.VMEM)


def per_device(
    departure, inv_var, k_matrix, frac_row, frac_col, dest_tile, cell_row, cell_col, predictors, scan_pos
):
    n_tile = lax.axis_size("tile")
    n_slot = lax.axis_size("slot")
    obs, chans, levels = k_matrix.shape
    slots = n_tile * CAP
    params = pltpu.CompilerParams(vmem_limit_bytes=VMEM)
    steps = 10
    flat = lambda x: x.reshape(1, obs)
    send = pl.pallas_call(
        functools.partial(send_kernel, steps=steps),
        out_shape=jax.ShapeDtypeStruct((slots, LANES), BF16),
        in_specs=[VM, VM, pl.BlockSpec(memory_space=pl.ANY)] + [VM] * 7,
        out_specs=VM,
        scratch_shapes=[
            pltpu.VMEM((chans, obs, levels), BF16),
            pltpu.VMEM((obs, LANES), F32),
            pltpu.SemaphoreType.DMA((steps,)),
        ],
        compiler_params=params,
        name="send",
    )(
        departure,
        inv_var.reshape(1, chans),
        jnp.transpose(k_matrix, (1, 0, 2)),
        flat(dest_tile),
        flat(frac_row),
        flat(frac_col),
        flat(cell_row),
        flat(cell_col),
        predictors.T,
        flat(scan_pos),
    )
    got = lax.all_to_all(send.reshape(n_tile, CAP, LANES), "tile", 0, 0, tiled=True)
    turned = pl.pallas_call(
        functools.partial(turn_kernel, levels=levels, half=chans // 2),
        out_shape=jax.ShapeDtypeStruct((VROWS, slots), BF16),
        in_specs=[VM],
        out_specs=VM,
        compiler_params=params,
        name="turn",
    )(got.reshape(slots, LANES))
    blocks = [turned] + [
        lax.ppermute(turned, "slot", [(i, (i + d) % n_slot) for i in range(n_slot)]) for d in (1, 3, 2)
    ]
    total = n_slot * slots
    first_row = (lax.axis_index("slot") * BLOCK).astype(jnp.int32).reshape(1)
    spill, colw, roww, chunk = pl.pallas_call(
        functools.partial(prep_kernel, levels=levels),
        out_shape=(
            jax.ShapeDtypeStruct((VROWS, GC), BF16),
            jax.ShapeDtypeStruct((GC, total), BF16),
            jax.ShapeDtypeStruct((BLOCK, total), F32),
            jax.ShapeDtypeStruct((8, 128), F32),
        ),
        in_specs=[pl.BlockSpec(memory_space=pltpu.SMEM)] + [VM] * 4,
        out_specs=(VM,) * 4,
        compiler_params=params,
        name="prep",
    )(first_row, *blocks)
    pairs = [(t * n_slot, ((t + 1) % n_tile) * n_slot) for t in range(n_tile)]
    arrived = lax.ppermute(spill, ("tile", "slot"), pairs)
    chunks = jnp.broadcast_to(chunk[None, 0:CAP, :], (n_tile, CAP, 128))
    chunks = lax.all_to_all(chunks, "tile", 0, 0, tiled=True).reshape(slots, 128)
    grid = pl.pallas_call(
        grid_kernel,
        grid=(VROWS // VCHUNK,),
        out_shape=jax.ShapeDtypeStruct((levels, BLOCK, GC), F32),
        in_specs=[pl.BlockSpec((VCHUNK, slots), lambda i: (i, 0))] * 4
        + [whole((GC, total)), whole((BLOCK, total)), pl.BlockSpec((VCHUNK, GC), lambda i: (i, 0))],
        out_specs=pl.BlockSpec((VCHUNK, BLOCK, GC), lambda i: (i, 0, 0)),
        compiler_params=params,
        name="grid",
    )(*blocks, colw, roww, arrived)
    bias = pl.pallas_call(
        functools.partial(bias_kernel, half=chans // 2, scale=1.0 / math.sqrt(obs * n_tile * n_slot)),
        out_shape=jax.ShapeDtypeStruct((chans, 128), F32),
        in_specs=[VM],
        out_specs=VM,
        compiler_params=params,
        name="bias",
    )(chunks)
    return jnp.transpose(grid, (1, 2, 0)), bias


def solution(mesh):
    both = ("tile", "slot")
    placed = (
        P(both, None),
        P(),
        P(both, None, None),
        P(both),
        P(both),
        P(both, None),
        P(both),
        P(both),
        P(both, None),
        P(both),
    )
    return jax.shard_map(
        per_device,
        mesh=mesh,
        in_specs=placed,
        out_specs=(P(both, None, None), P()),
        check_vma=False,
    )
```

time: 259 us -> 73.5 us (0.28)
  the two profiles are of different devices: /device:TPU:1 before, /device:TPU:32 now
where the time goes in v1:
time: 73.5 us; the launch traced here: 73.2 us
  blocking collectives  23.7 us (32%)
  waiting for transfers between devices  17.9 us (24%)
  starting transfers between devices  12.3 us (17%)
  Pallas kernels  11.8 us (16%)
  local copies, waits for them, and re-layouts  6.81 us (9%)
    all_to_all x1, blocking collectives, per_device(): lax.all_to_all(send.reshape(n_tile, CAP, LANES), 'tile', 0, 0, tiled=True)  23.7 us
    ppermute x3, waiting for transfers between devices, per_device(): lax.ppermute(turned, 'slot', [(i, (i + d) % n_slot) for i in range(n_slot)])  9.74 us
    ppermute x1, waiting for transfers between devices, per_device(): arrived = lax.ppermute(spill, ('tile', 'slot'), pairs)  8.11 us
    unnamed x18, local copies, waits for them, and re-layouts  5.99 us
    pallas_call x1, Pallas kernels, per_device(): pl.pallas_call(grid_kernel, grid=(VROWS // VCHUNK,), out_shape=jax.ShapeD...  5.77 us
    all_to_all x1, starting transfers between devices, per_device(): lax.all_to_all(chunks, 'tile', 0, 0, tiled=True).reshape(slots, 128)  5.16 us
    ppermute x3, starting transfers between devices, per_device(): lax.ppermute(turned, 'slot', [(i, (i + d) % n_slot) for i in range(n_slot)])  5.08 us
    pallas_call x1, Pallas kernels, per_device(): pl.pallas_call(functools.partial(send_kernel, steps=steps), out_shape=jax...  4.54 us
  transfers between devices with their start and end apart: 5, of which 4 were waited for; matrix products, arithmetic and copies ran while one was open for 0% of the time, Pallas kernels for 8%

profile of v1, /device:TPU:32, one launch (start us, length us, event | category | flops | bytes accessed | tf_op | source)
XLA Modules:
  0.0 73.2 jit_solution(4075299440374030411)
XLA Ops:
  0.6 0.0 copy-start
  0.6 0.7 copy-done
  1.4 0.0 copy-start.1
  1.4 0.7 copy-done.1
  2.1 0.0 copy-start.2
  2.1 0.7 copy-done.2
  2.7 0.0 copy-start.3
  2.7 0.7 copy-done.3
  3.4 0.7 copy-done.4
  4.0 0.7 copy-done.5
  4.7 0.7 copy-done.6
  5.3 0.7 copy-done.7
  6.0 0.7 copy-done.8
  6.6 4.5 %send.1 = bf16[256,512]{1,0:T(8,128)(2,1)S(1)} custom-call(bf16[96,100]{1,0:T(8,128)(2,1)S(1)} %copy-done, f32[1,100]{1,0:T(1,128)S(1)} %bitcast.14, bf16[100,96,411]{2,1,0:T(8,128)(2,1)} %bitcast.21, s32[1,96]{1,0:T(1,128)S(1)} %bitcast.15, bf16[1,96]{1,0:T(2,128)(2,1)S(1)} %bitcast.16, bf16[1,96]{1,0:T(2,128)(2,1)S(1)} %bitcast.17, s32[1,96]{1,0:T(1,128)S(1)} %bitcast.18, ...), custom_call_target="tpu_custom_call" | custom-call | tf_op jit(solution)/shard_map/send/pallas_call | solution.py:180
  11.2 0.1 reshape.45
  11.3 23.7 %all_to_all.10 = bf16[64,4,512]{2,1,0:T(4,128)(2,1)S(1)} all-to-all(bf16[64,4,512]{2,1,0:T(4,128)(2,1)S(1)} %reshape.45), channel_id=1, replica_groups=mesh['tile'=64,'slot'=4] {'tile'}, dimensions={0} | all-to-all | bytes 524288 | tf_op jit(solution)/shard_map/all_to_all | solution.py:204
  35.0 0.1 reshape.46.got
  35.0 0.2 turn.1.a0
  35.2 1.5 %collective-permute-start = (bf16[432,256]{1,0:T(8,128)(2,1)S(1)}, bf16[432,256]{1,0:T(8,128)(2,1)S(1)}, u32[]{:S(2)}, u32[]{:S(2)}) collective-permute-start(bf16[432,256]{1,0:T(8,128)(2,1)S(1)} %turn.1.a0), channel_id=1, source_target_pairs={{0,1},{1,2},{2,3},{3,0},{4,5},{5,6},{6,7},{7,4},{8,9},{9,10},{10,1... | collective-permute-start | bytes 663560 | tf_op jit(solution)/shard_map/ppermute | solution.py:214
  36.8 1.7 %collective-permute-start.1 = (bf16[432,256]{1,0:T(8,128)(2,1)S(1)}, bf16[432,256]{1,0:T(8,128)(2,1)S(1)}, u32[]{:S(2)}, u32[]{:S(2)}) collective-permute-start(bf16[432,256]{1,0:T(8,128)(2,1)S(1)} %turn.1.a0), channel_id=1, source_target_pairs={{0,3},{1,0},{2,1},{3,2},{4,7},{5,4},{6,5},{7,6},{8,11},{9,8},{10,9... | collective-permute-start | bytes 663560 | tf_op jit(solution)/shard_map/ppermute | solution.py:214
  38.5 1.8 %collective-permute-start.2 = (bf16[432,256]{1,0:T(8,128)(2,1)S(1)}, bf16[432,256]{1,0:T(8,128)(2,1)S(1)}, u32[]{:S(2)}, u32[]{:S(2)}) collective-permute-start(bf16[432,256]{1,0:T(8,128)(2,1)S(1)} %turn.1.a0), channel_id=1, source_target_pairs={{0,2},{1,3},{2,0},{3,1},{4,6},{5,7},{6,4},{7,5},{8,10},{9,11},{10,... | collective-permute-start | bytes 663560 | tf_op jit(solution)/shard_map/ppermute | solution.py:214
  40.3 4.0 %collective-permute-done.a1 = bf16[432,256]{1,0:T(8,128)(2,1)S(1)} collective-permute-done((bf16[432,256]{1,0:T(8,128)(2,1)S(1)}, bf16[432,256]{1,0:T(8,128)(2,1)S(1)}, u32[]{:S(2)}, u32[]{:S(2)}) %collective-permute-start) | collective-permute-done | bytes 221216 | tf_op jit(solution)/shard_map/ppermute | solution.py:214
  44.4 4.0 %collective-permute-done.1.a2 = bf16[432,256]{1,0:T(8,128)(2,1)S(1)} collective-permute-done((bf16[432,256]{1,0:T(8,128)(2,1)S(1)}, bf16[432,256]{1,0:T(8,128)(2,1)S(1)}, u32[]{:S(2)}, u32[]{:S(2)}) %collective-permute-start.1) | collective-permute-done | bytes 221216 | tf_op jit(solution)/shard_map/ppermute | solution.py:214
  48.4 1.7 %collective-permute-done.2.a3 = bf16[432,256]{1,0:T(8,128)(2,1)S(1)} collective-permute-done((bf16[432,256]{1,0:T(8,128)(2,1)S(1)}, bf16[432,256]{1,0:T(8,128)(2,1)S(1)}, u32[]{:S(2)}, u32[]{:S(2)}) %collective-permute-start.2) | collective-permute-done | bytes 221216 | tf_op jit(solution)/shard_map/ppermute | solution.py:214
  50.1 0.6 prep.1
  50.7 0.7 broadcast_in_dim.2
  51.3 5.2 %all-to-all-start.1 = ((f32[64,4,128]{2,1,0:T(4,128)}), f32[64,4,128]{2,1,0:T(4,128)S(1)}, u32[]{:S(2)}, u32[]{:S(2)}) async-start(f32[64,4,128]{2,1,0:T(4,128)} %broadcast_in_dim.2), calls=%async_computation.1 | async-start | bytes 262144 | tf_op jit(solution)/shard_map/all_to_all | solution.py:234
  56.5 2.1 %collective-permute-start.3 = (bf16[432,256]{1,0:T(8,128)(2,1)S(1)}, bf16[432,256]{1,0:T(8,128)(2,1)S(1)}, u32[]{:S(2)}, u32[]{:S(2)}) collective-permute-start(bf16[432,256]{1,0:T(8,128)(2,1)S(1)} %get-tuple-element.8), channel_id=1, source_target_pairs={{0,4},{4,8},{8,12},{12,16},{16,20},{20,24},{24,28},{28,32},{32,36}... | collective-permute-start | bytes 663560 | tf_op jit(solution)/shard_map/ppermute | solution.py:232
  58.6 8.1 %collective-permute-done.3.spill = bf16[432,256]{1,0:T(8,128)(2,1)S(1)} collective-permute-done((bf16[432,256]{1,0:T(8,128)(2,1)S(1)}, bf16[432,256]{1,0:T(8,128)(2,1)S(1)}, u32[]{:S(2)}, u32[]{:S(2)}) %collective-permute-start.3) | collective-permute-done | bytes 221216 | tf_op jit(solution)/shard_map/ppermute | solution.py:232
  66.7 5.8 %grid.1 = f32[411,8,256]{2,1,0:T(8,128)} custom-call(bf16[432,256]{1,0:T(8,128)(2,1)S(1)} %turn.1.a0, bf16[432,256]{1,0:T(8,128)(2,1)S(1)} %collective-permute-done.a1, bf16[432,256]{1,0:T(8,128)(2,1)S(1)} %collective-permute-done.1.a2, bf16[432,256]{1,0:T(8,128)(2,1)S(1)} %collective-permute-done.2.a3, bf16[256,1024]{1,0:T(8,128)(2,1)S(1)} %get-tuple-element.6.colw, ...), custom_call_target="tpu_custom_call" | custom-call | tf_op jit(solution)/shard_map/grid/pallas_call | solution.py:235
  72.5 0.0 all-to-all-done.1
  72.5 0.7 bias.1
  (6 shorter events, 0.0 us)
Async XLA Ops:
  0.6 0.7 %copy-start = (bf16[96,100]{1,0:T(8,128)(2,1)S(1)}, bf16[96,100]{1,0:T(8,128)(2,1)}, u32[]{:S(2)}) copy-start(bf16[96,100]{1,0:T(8,128)(2,1)} %dep.1) | copy-start | bytes 57604
  1.4 0.7 copy-start.1
  2.1 0.7 copy-start.2
  2.7 0.7 copy-start.3
  3.4 0.7 copy-start.4
  4.0 0.7 copy-start.5
  4.7 0.7 copy-start.6
  5.3 0.7 copy-start.7
  6.0 0.7 copy-start.8
  35.2 9.1 %collective-permute-start = (bf16[432,256]{1,0:T(8,128)(2,1)S(1)}, bf16[432,256]{1,0:T(8,128)(2,1)S(1)}, u32[]{:S(2)}, u32[]{:S(2)}) collective-permute-start(bf16[432,256]{1,0:T(8,128)(2,1)S(1)} %turn.1.a0), channel_id=1, source_target_pairs={{0,1},{1,2},{2,3},{3,0},{4,5},{5,6},{6,7},{7,4},{8,9},{9,10},{10,1... | collective-permute-start | bytes 663560 | tf_op jit(solution)/shard_map/ppermute | solution.py:214
  36.8 11.6 %collective-permute-start.1 = (bf16[432,256]{1,0:T(8,128)(2,1)S(1)}, bf16[432,256]{1,0:T(8,128)(2,1)S(1)}, u32[]{:S(2)}, u32[]{:S(2)}) collective-permute-start(bf16[432,256]{1,0:T(8,128)(2,1)S(1)} %turn.1.a0), channel_id=1, source_target_pairs={{0,3},{1,0},{2,1},{3,2},{4,7},{5,4},{6,5},{7,6},{8,11},{9,8},{10,9... | collective-permute-start | bytes 663560 | tf_op jit(solution)/shard_map/ppermute | solution.py:214
  38.5 11.6 %collective-permute-start.2 = (bf16[432,256]{1,0:T(8,128)(2,1)S(1)}, bf16[432,256]{1,0:T(8,128)(2,1)S(1)}, u32[]{:S(2)}, u32[]{:S(2)}) collective-permute-start(bf16[432,256]{1,0:T(8,128)(2,1)S(1)} %turn.1.a0), channel_id=1, source_target_pairs={{0,2},{1,3},{2,0},{3,1},{4,6},{5,7},{6,4},{7,5},{8,10},{9,11},{10,... | collective-permute-start | bytes 663560 | tf_op jit(solution)/shard_map/ppermute | solution.py:214
  51.3 21.1 %all-to-all-start.1 = ((f32[64,4,128]{2,1,0:T(4,128)}), f32[64,4,128]{2,1,0:T(4,128)S(1)}, u32[]{:S(2)}, u32[]{:S(2)}) async-start(f32[64,4,128]{2,1,0:T(4,128)} %broadcast_in_dim.2), calls=%async_computation.1 | async-start | bytes 262144 | tf_op jit(solution)/shard_map/all_to_all | solution.py:234
  56.5 10.2 %collective-permute-start.3 = (bf16[432,256]{1,0:T(8,128)(2,1)S(1)}, bf16[432,256]{1,0:T(8,128)(2,1)S(1)}, u32[]{:S(2)}, u32[]{:S(2)}) collective-permute-start(bf16[432,256]{1,0:T(8,128)(2,1)S(1)} %get-tuple-element.8), channel_id=1, source_target_pairs={{0,4},{4,8},{8,12},{12,16},{16,20},{20,24},{24,28},{28,32},{32,36}... | collective-permute-start | bytes 663560 | tf_op jit(solution)/shard_map/ppermute | solution.py:232

commit v2 on v1

v2 whole, which is shorter than its diff:
```python
import functools
import math

import jax
import jax.numpy as jnp
from jax import lax
from jax.experimental import pallas as pl
from jax.experimental.pallas import tpu as pltpu
from jax.sharding import PartitionSpec as P

F32 = jnp.float32
BF16 = jnp.bfloat16
NT = (((1,), (1,)), ((), ()))
NN = (((1,), (0,)), ((), ()))

CAP = 4
GR = 32
GC = 256
LANES = 512
VROWS = 416
VCHUNK = 104
BLOCK = 8
VMEM = 48 * 1024 * 1024


def iota(shape, dim):
    return lax.broadcasted_iota(jnp.int32, shape, dim)


def dot(a, b, dims):
    return lax.dot_general(a, b, dims, preferred_element_type=F32)


def ones_where(mask):
    return jnp.where(mask, 1.0, 0.0).astype(BF16)


def send_kernel(*refs, steps):
    k_hbm, small_hbm, out, small, kbuf, acc, sems, small_sems = refs[0], refs[1:10], *refs[10:11], refs[11:20], *refs[20:]
    chans, obs, levels = k_hbm.shape
    per = chans // steps
    small_copies = [
        pltpu.make_async_copy(src, dst, small_sems.at[i]) for i, (src, dst) in enumerate(zip(small_hbm, small))
    ]
    for copy in small_copies:
        copy.start()
    copies = [
        pltpu.make_async_copy(k_hbm.at[pl.ds(i * per, per)], kbuf.at[pl.ds(i * per, per)], sems.at[i])
        for i in range(steps)
    ]
    for copy in copies:
        copy.start()
    for copy in small_copies:
        copy.wait()
    dep, inv, tile, frow, fcol, crow, ccol, predt, scan = small
    slots = out.shape[0]
    wbf = (dep[...].astype(F32) * inv[...]).astype(BF16)
    w = wbf.astype(F32)

    tr = jnp.broadcast_to(tile[...].astype(F32), (obs, obs))
    ri, ci = iota((obs, obs), 0), iota((obs, obs), 1)
    tc = jnp.sum(jnp.where(ri == ci, tr, 0.0), 1, keepdims=True)
    rank = jnp.sum(jnp.where((tc == tr) & (ri < ci), 1.0, 0.0), 0, keepdims=True)
    slot = (tile[...].astype(F32) * CAP + rank).astype(jnp.int32)
    sel = ones_where(iota((slots, obs), 0) == slot)

    base = levels - (LANES - 128)
    rows = iota((128, obs), 0)
    place = jnp.where(rows == base, frow[...].astype(F32), 0.0)
    place = jnp.where(rows == base + 1, fcol[...].astype(F32), place)
    place = jnp.where(rows == base + 2, crow[...].astype(F32), place)
    place = jnp.where(rows == base + 3, ccol[...].astype(F32), place)
    extra = dot(sel, place.astype(BF16), NT)

    npred = predt.shape[0]
    kinds = 128
    ind = jnp.where(iota((kinds - npred, obs), 0) == scan[...], 1.0, 0.0)
    basist = jnp.concatenate([predt[...].astype(F32), ind], 0).astype(BF16)
    biast = dot(basist, wbf, NN)
    hi = biast.astype(BF16)
    lo = (biast - hi.astype(F32)).astype(BF16)
    half = chans // 2
    first = base + 4
    er, ec = iota((chans, 128), 0), iota((chans, 128), 1)
    parts = []
    for h in range(2):
        e = ones_where((ec == er - h * half + first) & (er >= h * half) & (er < (h + 1) * half))
        f = ones_where((ec == er - h * half + first + half) & (er >= h * half) & (er < (h + 1) * half))
        parts.append(dot(hi, e, NN) + dot(lo, f, NN))
    extra = extra + jnp.concatenate(parts, 0)

    acc[...] = jnp.zeros(acc.shape, F32)
    for i in range(steps):
        copies[i].wait()
        for r in range(0, obs, 16):
            total = acc[r : r + 16, 0:levels]
            for c in range(i * per, (i + 1) * per):
                total = total + w[r : r + 16, c : c + 1] * kbuf[c, r : r + 16, :].astype(F32)
            acc[r : r + 16, 0:levels] = total
    placed = dot(sel, acc[...].astype(BF16), NN)
    out[:, 0 : LANES - 128] = placed[:, 0 : LANES - 128].astype(BF16)
    out[:, LANES - 128 : LANES] = (placed[:, LANES - 128 : LANES] + extra).astype(BF16)


def turn_kernel(got, out, chunk, *, levels, half):
    slots = got.shape[0]
    out[...] = jnp.transpose(got[...].astype(F32))[0:VROWS, :].astype(BF16)
    pick = ones_where(iota((slots, slots), 1) % CAP == iota((slots, slots), 0) % CAP)
    total = dot(pick, got[:, LANES - 128 : LANES], NN)
    first = levels - (LANES - 128) + 4
    lane = iota((slots, 128), 1)
    kept = 128 - first - half
    sums = jnp.where(lane < half, pltpu.roll(total, 128 - first, 1), 0.0)
    chunk[...] = sums + jnp.where(lane < kept, pltpu.roll(total, 128 - first - half, 1), 0.0)


def prep_kernel(first_row, a0, a1, a2, a3, spill, colw, roww, *, levels):
    refs = (a0, a1, a2, a3)
    tops = jnp.concatenate([ref[VROWS - 16 : VROWS, :].astype(F32) for ref in refs], 1)
    at = levels - (VROWS - 16)
    fr, cr = tops[at : at + 1, :], tops[at + 2 : at + 3, :]
    n = fr.shape[1]
    turned = jnp.transpose(tops)
    fc, cc = turned[:, at + 1 : at + 2], turned[:, at + 3 : at + 4].astype(jnp.int32)
    cols = iota((n, GC), 1)
    cw = jnp.where(cols == cc, 1.0 - fc, jnp.where(cols == cc + 1, fc, 0.0)).astype(BF16)
    colw[...] = cw
    row = cr.astype(jnp.int32)
    rel = iota((BLOCK, n), 0) + first_row[0]
    roww[...] = jnp.where(rel == row, 1.0 - fr, 0.0) + jnp.where(rel == row + 1, fr, 0.0)
    last = jnp.where(row == GR - 1, fr, 0.0)
    part = a0.shape[1]
    out = jnp.zeros((VROWS, GC), F32)
    for j, ref in enumerate(refs):
        lhs = (ref[...].astype(F32) * last[:, j * part : (j + 1) * part]).astype(BF16)
        out = out + dot(lhs, cw[j * part : (j + 1) * part, :], NN)
    spill[...] = out.astype(BF16)


def grid_kernel(a0, a1, a2, a3, colw, roww, spill, out):
    part = a0.shape[1]
    total = jnp.zeros((VCHUNK * BLOCK, GC), F32)
    for j, ref in enumerate((a0, a1, a2, a3)):
        cols = slice(j * part, (j + 1) * part)
        lhs = ref[...].astype(F32)[:, None, :] * roww[:, cols][None, :, :]
        lhs = lhs.reshape(VCHUNK * BLOCK, part).astype(BF16)
        total = total + dot(lhs, colw[cols, :], NN)
    total = total.reshape(VCHUNK, BLOCK, GC)
    first = iota((VCHUNK, BLOCK, GC), 1) == 0
    out[...] = total + jnp.where(first, spill[...].astype(F32)[:, None, :], 0.0)


def slot_bias_kernel(got, out, *, half):
    t = jnp.transpose(got[...])
    n = got.shape[0] // 2
    out[0:half, :] = t[0:half, 0:n]
    out[half : 2 * half, :] = t[0:half, n : 2 * n]


def bias_kernel(b0, b1, b2, b3, out, *, scale):
    out[...] = ((b0[...] + b1[...]) + (b2[...] + b3[...])) * scale


def whole(shape):
    return pl.BlockSpec(shape, lambda *_: (0,) * len(shape))


VM = pl.BlockSpec(memory_space=pltpu.VMEM)
HBM = pl.BlockSpec(memory_space=pltpu.HBM)


def per_device(
    departure, inv_var, k_matrix, frac_row, frac_col, dest_tile, cell_row, cell_col, predictors, scan_pos
):
    n_tile = lax.axis_size("tile")
    n_slot = lax.axis_size("slot")
    obs, chans, levels = k_matrix.shape
    slots = n_tile * CAP
    params = pltpu.CompilerParams(vmem_limit_bytes=VMEM)
    tight = pltpu.CompilerParams(vmem_limit_bytes=56 * 1024 * 1024)
    steps = 10
    flat = lambda x: x.reshape(1, obs)
    small = (
        departure,
        inv_var.reshape(1, chans),
        flat(dest_tile),
        flat(frac_row),
        flat(frac_col),
        flat(cell_row),
        flat(cell_col),
        predictors.T,
        flat(scan_pos),
    )
    send = pl.pallas_call(
        functools.partial(send_kernel, steps=steps),
        out_shape=jax.ShapeDtypeStruct((slots, LANES), BF16),
        in_specs=[HBM] * (1 + len(small)),
        out_specs=VM,
        scratch_shapes=[pltpu.VMEM(x.shape, x.dtype) for x in small]
        + [
            pltpu.VMEM((chans, obs, levels), BF16),
            pltpu.VMEM((obs, LANES), F32),
            pltpu.SemaphoreType.DMA((steps,)),
            pltpu.SemaphoreType.DMA((len(small),)),
        ],
        compiler_params=tight,
        name="send",
    )(jnp.transpose(k_matrix, (1, 0, 2)), *small)
    got = lax.all_to_all(send.reshape(n_tile, CAP, LANES), "tile", 0, 0, tiled=True)
    turned, chunk = pl.pallas_call(
        functools.partial(turn_kernel, levels=levels, half=chans // 2),
        out_shape=(jax.ShapeDtypeStruct((VROWS, slots), BF16), jax.ShapeDtypeStruct((slots, 128), F32)),
        in_specs=[VM],
        out_specs=(VM, VM),
        compiler_params=params,
        name="turn",
    )(got.reshape(slots, LANES))

    def around(x):
        return [x] + [lax.ppermute(x, "slot", [(i, (i + d) % n_slot) for i in range(n_slot)]) for d in (1, 3, 2)]

    blocks = around(turned)
    chunks = lax.all_to_all(chunk.reshape(n_tile, CAP, 128), "tile", 0, 0, tiled=True).reshape(slots, 128)
    total = n_slot * slots
    first_row = (lax.axis_index("slot") * BLOCK).astype(jnp.int32).reshape(1)
    spill, colw, roww = pl.pallas_call(
        functools.partial(prep_kernel, levels=levels),
        out_shape=(
            jax.ShapeDtypeStruct((VROWS, GC), BF16),
            jax.ShapeDtypeStruct((total, GC), BF16),
            jax.ShapeDtypeStruct((BLOCK, total), F32),
        ),
        in_specs=[pl.BlockSpec(memory_space=pltpu.SMEM)] + [VM] * 4,
        out_specs=(VM,) * 3,
        compiler_params=params,
        name="prep",
    )(first_row, *blocks)
    pairs = [(t * n_slot, ((t + 1) % n_tile) * n_slot) for t in range(n_tile)]
    arrived = lax.ppermute(spill, ("tile", "slot"), pairs)
    slot_bias = pl.pallas_call(
        functools.partial(slot_bias_kernel, half=chans // 2),
        out_shape=jax.ShapeDtypeStruct((chans, 128), F32),
        in_specs=[VM],
        out_specs=VM,
        compiler_params=params,
        name="slot_bias",
    )(chunks)
    biases = around(slot_bias)
    grid = pl.pallas_call(
        grid_kernel,
        grid=(VROWS // VCHUNK,),
        out_shape=jax.ShapeDtypeStruct((levels, BLOCK, GC), F32),
        in_specs=[pl.BlockSpec((VCHUNK, slots), lambda i: (i, 0))] * 4
        + [whole((total, GC)), whole((BLOCK, total)), pl.BlockSpec((VCHUNK, GC), lambda i: (i, 0))],
        out_specs=pl.BlockSpec((VCHUNK, BLOCK, GC), lambda i: (i, 0, 0)),
        compiler_params=params,
        cost_estimate=pl.CostEstimate(
            flops=2 * levels * BLOCK * GC * total, bytes_accessed=16 * levels * BLOCK * GC, transcendentals=0
        ),
        name="grid",
    )(*blocks, colw, roww, arrived)
    *biases, grid = lax.optimization_barrier((*biases, grid))
    bias = pl.pallas_call(
        functools.partial(bias_kernel, scale=1.0 / math.sqrt(obs * n_tile * n_slot)),
        out_shape=jax.ShapeDtypeStruct((chans, 128), F32),
        in_specs=[VM] * 4,
        out_specs=VM,
        compiler_params=params,
        name="bias",
    )(*biases)
    return jnp.transpose(grid, (1, 2, 0)), bias


def solution(mesh):
    both = ("tile", "slot")
    placed = (
        P(both, None),
        P(),
        P(both, None, None),
        P(both),
        P(both),
        P(both, None),
        P(both),
        P(both),
        P(both, None),
        P(both),
    )
    return jax.shard_map(
        per_device,
        mesh=mesh,
        in_specs=placed,
        out_specs=(P(both, None, None), P()),
        check_vma=False,
    )
```

time: 73.5 us -> 65.4 us (0.89)
  the two profiles are of different devices: /device:TPU:32 before, /device:TPU:1 now
where the time goes in v2:
time: 65.4 us; the launch traced here: 65.1 us
  blocking collectives  26.1 us (40%)
  starting transfers between devices  16 us (24%)
  Pallas kernels  13.9 us (21%)
  waiting for transfers between devices  7.3 us (11%)
  local copies, waits for them, and re-layouts  1.08 us (2%)
  between operations  0.71 us (1%)
    all_to_all x1, blocking collectives, per_device(): lax.all_to_all(send.reshape(n_tile, CAP, LANES), 'tile', 0, 0, tiled=True)  26.1 us
    pallas_call x1, Pallas kernels, per_device(): pl.pallas_call(functools.partial(send_kernel, steps=steps), out_shape=jax...  7.5 us
    ppermute x6, starting transfers between devices, around(): lax.ppermute(x, 'slot', [(i, (i + d) % n_slot) for i in range(n_slot)])  7.19 us
    all_to_all x1, starting transfers between devices, per_device(): lax.all_to_all(chunk.reshape(n_tile, CAP, 128), 'tile', 0, 0, tiled=True)  5.55 us
    ppermute x6, waiting for transfers between devices, around(): lax.ppermute(x, 'slot', [(i, (i + d) % n_slot) for i in range(n_slot)])  4.1 us
    pallas_call x1, Pallas kernels, per_device(): pl.pallas_call(grid_kernel, grid=(VROWS // VCHUNK,), out_shape=jax.ShapeD...  3.72 us
    ppermute x1, starting transfers between devices, per_device(): arrived = lax.ppermute(spill, ('tile', 'slot'), pairs)  3.29 us
    all_to_all x1, waiting for transfers between devices, per_device(): lax.all_to_all(chunk.reshape(n_tile, CAP, 128), 'tile', 0, 0, tiled=True)  3.2 us
  transfers between devices with their start and end apart: 8, of which 3 were waited for; matrix products, arithmetic and copies ran while one was open for 0% of the time, Pallas kernels for 7%

profile of v2, /device:TPU:1, one launch (start us, length us, event | category | flops | bytes accessed | tf_op | source)
XLA Modules:
  0.0 65.1 jit_solution(5033162523711823166)
XLA Ops:
  0.6 7.5 %send.1 = bf16[256,512]{1,0:T(8,128)(2,1)} custom-call(bf16[100,96,411]{2,1,0:T(8,128)(2,1)} %bitcast.14, bf16[96,100]{1,0:T(8,128)(2,1)} %refs_1_.1, f32[1,100]{1,0:T(1,128)} %bitcast.16, s32[1,96]{1,0:T(1,128)} %bitcast.17, bf16[1,96]{1,0:T(2,128)(2,1)} %bitcast.18, bf16[1,96]{1,0:T(2,128)(2,1)} %bitcast.19, s32[1,96]{1,0:T(1,128)} %bitcast.20, ...), custom_call_target="tpu_custom_call" | custom-call | tf_op jit(solution)/shard_map/send/pallas_call | solution.py:194
  8.1 1.0 %reshape.47 = bf16[64,4,512]{2,1,0:T(4,128)(2,1)S(1)} reshape(bf16[256,512]{1,0:T(8,128)(2,1)} %send.1) | data formatting | bytes 524288 | tf_op jit(solution)/shard_map/reshape | solution.py:209
  9.2 26.1 %all_to_all.10 = bf16[64,4,512]{2,1,0:T(4,128)(2,1)S(1)} all-to-all(bf16[64,4,512]{2,1,0:T(4,128)(2,1)S(1)} %reshape.47), channel_id=1, replica_groups=mesh['tile'=64,'slot'=4] {'tile'}, dimensions={0} | all-to-all | bytes 524288 | tf_op jit(solution)/shard_map/all_to_all | solution.py:209
  35.3 0.1 reshape.48.got
  35.4 0.9 %turn.1 = (bf16[416,256]{1,0:T(8,128)(2,1)S(1)}, f32[256,128]{1,0:T(8,128)}) custom-call(bf16[256,512]{1,0:T(8,128)(2,1)S(1)} %reshape.48.got), custom_call_target="tpu_custom_call" | custom-call | tf_op jit(solution)/shard_map/turn/pallas_call | solution.py:210
  36.3 1.2 %collective-permute-start.3 = (bf16[416,256]{1,0:T(8,128)(2,1)S(1)}, bf16[416,256]{1,0:T(8,128)(2,1)S(1)}, u32[]{:S(2)}, u32[]{:S(2)}) collective-permute-start(bf16[416,256]{1,0:T(8,128)(2,1)S(1)} %get-tuple-element.13.a0), channel_id=1, source_target_pairs={{0,1},{1,2},{2,3},{3,0},{4,5},{5,6},{6,7},{7,4},{8,9},{9,10},{10,1... | collective-permute-start | bytes 638984 | tf_op jit(solution)/shard_map/ppermute | solution.py:220
  37.5 1.5 %collective-permute-start.4 = (bf16[416,256]{1,0:T(8,128)(2,1)S(1)}, bf16[416,256]{1,0:T(8,128)(2,1)S(1)}, u32[]{:S(2)}, u32[]{:S(2)}) collective-permute-start(bf16[416,256]{1,0:T(8,128)(2,1)S(1)} %get-tuple-element.13.a0), channel_id=1, source_target_pairs={{0,3},{1,0},{2,1},{3,2},{4,7},{5,4},{6,5},{7,6},{8,11},{9,8},{10,9... | collective-permute-start | bytes 638984 | tf_op jit(solution)/shard_map/ppermute | solution.py:220
  39.0 1.5 %collective-permute-start.5 = (bf16[416,256]{1,0:T(8,128)(2,1)S(1)}, bf16[416,256]{1,0:T(8,128)(2,1)S(1)}, u32[]{:S(2)}, u32[]{:S(2)}) collective-permute-start(bf16[416,256]{1,0:T(8,128)(2,1)S(1)} %get-tuple-element.13.a0), channel_id=1, source_target_pairs={{0,2},{1,3},{2,0},{3,1},{4,6},{5,7},{6,4},{7,5},{8,10},{9,11},{10,... | collective-permute-start | bytes 638984 | tf_op jit(solution)/shard_map/ppermute | solution.py:220
  40.5 5.6 %all-to-all-start.1 = ((f32[64,4,128]{2,1,0:T(4,128)}), f32[64,4,128]{2,1,0:T(4,128)S(1)}, u32[]{:S(2)}, u32[]{:S(2)}) async-start(f32[64,4,128]{2,1,0:T(4,128)} %bitcast.9), calls=%async_computation.1 | async-start | bytes 262144 | tf_op jit(solution)/shard_map/all_to_all | solution.py:223
  46.1 0.0 collective-permute-done.3.a1
  46.1 0.0 collective-permute-done.4.a2
  46.1 3.6 %collective-permute-done.5.a3 = bf16[416,256]{1,0:T(8,128)(2,1)S(1)} collective-permute-done((bf16[416,256]{1,0:T(8,128)(2,1)S(1)}, bf16[416,256]{1,0:T(8,128)(2,1)S(1)}, u32[]{:S(2)}, u32[]{:S(2)}) %collective-permute-start.5) | collective-permute-done | bytes 213024 | tf_op jit(solution)/shard_map/ppermute | solution.py:220
  49.7 1.0 %prep.1 = (bf16[416,256]{1,0:T(8,128)(2,1)S(1)}, bf16[1024,256]{1,0:T(8,128)(2,1)S(1)}, f32[8,1024]{1,0:T(8,128)S(1)}) custom-call(s32[1]{0:T(128)} %bitcast.11.first_row, bf16[416,256]{1,0:T(8,128)(2,1)S(1)} %get-tuple-element.13.a0, bf16[416,256]{1,0:T(8,128)(2,1)S(1)} %collective-permute-done.3.a1, bf16[416,256]{1,0:T(8,128)(2,1)S(1)} %collective-permute-done.4.a2, ...), custom_call_target="tpu_custom_call" | custom-call | tf_op jit(solution)/shard_map/prep/pallas_call | solution.py:226
  50.7 3.3 %collective-permute-start.6 = (bf16[416,256]{1,0:T(8,128)(2,1)S(1)}, bf16[416,256]{1,0:T(8,128)(2,1)S(1)}, u32[]{:S(2)}, u32[]{:S(2)}) collective-permute-start(bf16[416,256]{1,0:T(8,128)(2,1)S(1)} %get-tuple-element.16), channel_id=1, source_target_pairs={{0,4},{4,8},{8,12},{12,16},{16,20},{20,24},{24,28},{28,32},{32,36}... | collective-permute-start | bytes 638984 | tf_op jit(solution)/shard_map/ppermute | solution.py:239
  54.0 3.2 %all-to-all-done.1 = f32[64,4,128]{2,1,0:T(4,128)S(1)} async-done(((f32[64,4,128]{2,1,0:T(4,128)}), f32[64,4,128]{2,1,0:T(4,128)S(1)}, u32[]{:S(2)}, u32[]{:S(2)}) %all-to-all-start.1) | async-done | bytes 131104 | tf_op jit(solution)/shard_map/all_to_all | solution.py:223
  57.2 0.1 slot_bias.1.b0
  57.3 0.4 collective-permute-start
  57.7 2.4 %collective-permute-start.1 = (f32[100,128]{1,0:T(8,128)S(1)}, f32[100,128]{1,0:T(8,128)S(1)}, u32[]{:S(2)}, u32[]{:S(2)}) collective-permute-start(f32[100,128]{1,0:T(8,128)S(1)} %slot_bias.1.b0), channel_id=1, source_target_pairs={{0,3},{1,0},{2,1},{3,2},{4,7},{5,4},{6,5},{7,6},{8,11},{9,8},{10,9... | collective-permute-start | bytes 153608 | tf_op jit(solution)/shard_map/ppermute | solution.py:220
  60.0 0.2 collective-permute-start.2
  60.2 0.0 collective-permute-done.6.spill
  60.3 3.7 %grid.1 = f32[411,8,256]{2,1,0:T(8,128)} custom-call(bf16[416,256]{1,0:T(8,128)(2,1)S(1)} %get-tuple-element.13.a0, bf16[416,256]{1,0:T(8,128)(2,1)S(1)} %collective-permute-done.3.a1, bf16[416,256]{1,0:T(8,128)(2,1)S(1)} %collective-permute-done.4.a2, bf16[416,256]{1,0:T(8,128)(2,1)S(1)} %collective-permute-done.5.a3, ...), custom_call_target="tpu_custom_call" | custom-call | flops 1723858944 | bytes 13467648 | tf_op jit(solution)/shard_map/grid/pallas_call | solution.py:249
  64.0 0.0 collective-permute-done.b1
  64.0 0.0 collective-permute-done.1.b2
  64.0 0.5 collective-permute-done.2.b3
  64.5 0.6 bias.1
Async XLA Ops:
  36.3 9.8 %collective-permute-start.3 = (bf16[416,256]{1,0:T(8,128)(2,1)S(1)}, bf16[416,256]{1,0:T(8,128)(2,1)S(1)}, u32[]{:S(2)}, u32[]{:S(2)}) collective-permute-start(bf16[416,256]{1,0:T(8,128)(2,1)S(1)} %get-tuple-element.13.a0), channel_id=1, source_target_pairs={{0,1},{1,2},{2,3},{3,0},{4,5},{5,6},{6,7},{7,4},{8,9},{9,10},{10,1... | collective-permute-start | bytes 638984 | tf_op jit(solution)/shard_map/ppermute | solution.py:220
  37.5 8.6 %collective-permute-start.4 = (bf16[416,256]{1,0:T(8,128)(2,1)S(1)}, bf16[416,256]{1,0:T(8,128)(2,1)S(1)}, u32[]{:S(2)}, u32[]{:S(2)}) collective-permute-start(bf16[416,256]{1,0:T(8,128)(2,1)S(1)} %get-tuple-element.13.a0), channel_id=1, source_target_pairs={{0,3},{1,0},{2,1},{3,2},{4,7},{5,4},{6,5},{7,6},{8,11},{9,8},{10,9... | collective-permute-start | bytes 638984 | tf_op jit(solution)/shard_map/ppermute | solution.py:220
  39.0 10.7 %collective-permute-start.5 = (bf16[416,256]{1,0:T(8,128)(2,1)S(1)}, bf16[416,256]{1,0:T(8,128)(2,1)S(1)}, u32[]{:S(2)}, u32[]{:S(2)}) collective-permute-start(bf16[416,256]{1,0:T(8,128)(2,1)S(1)} %get-tuple-element.13.a0), channel_id=1, source_target_pairs={{0,2},{1,3},{2,0},{3,1},{4,6},{5,7},{6,4},{7,5},{8,10},{9,11},{10,... | collective-permute-start | bytes 638984 | tf_op jit(solution)/shard_map/ppermute | solution.py:220
  40.5 16.7 %all-to-all-start.1 = ((f32[64,4,128]{2,1,0:T(4,128)}), f32[64,4,128]{2,1,0:T(4,128)S(1)}, u32[]{:S(2)}, u32[]{:S(2)}) async-start(f32[64,4,128]{2,1,0:T(4,128)} %bitcast.9), calls=%async_computation.1 | async-start | bytes 262144 | tf_op jit(solution)/shard_map/all_to_all | solution.py:223
  50.7 9.6 %collective-permute-start.6 = (bf16[416,256]{1,0:T(8,128)(2,1)S(1)}, bf16[416,256]{1,0:T(8,128)(2,1)S(1)}, u32[]{:S(2)}, u32[]{:S(2)}) collective-permute-start(bf16[416,256]{1,0:T(8,128)(2,1)S(1)} %get-tuple-element.16), channel_id=1, source_target_pairs={{0,4},{4,8},{8,12},{12,16},{16,20},{20,24},{24,28},{28,32},{32,36}... | collective-permute-start | bytes 638984 | tf_op jit(solution)/shard_map/ppermute | solution.py:239
  57.3 6.7 %collective-permute-start = (f32[100,128]{1,0:T(8,128)S(1)}, f32[100,128]{1,0:T(8,128)S(1)}, u32[]{:S(2)}, u32[]{:S(2)}) collective-permute-start(f32[100,128]{1,0:T(8,128)S(1)} %slot_bias.1.b0), channel_id=1, source_target_pairs={{0,1},{1,2},{2,3},{3,0},{4,5},{5,6},{6,7},{7,4},{8,9},{9,10},{10,1... | collective-permute-start | bytes 153608 | tf_op jit(solution)/shard_map/ppermute | solution.py:220
  57.7 6.3 %collective-permute-start.1 = (f32[100,128]{1,0:T(8,128)S(1)}, f32[100,128]{1,0:T(8,128)S(1)}, u32[]{:S(2)}, u32[]{:S(2)}) collective-permute-start(f32[100,128]{1,0:T(8,128)S(1)} %slot_bias.1.b0), channel_id=1, source_target_pairs={{0,3},{1,0},{2,1},{3,2},{4,7},{5,4},{6,5},{7,6},{8,11},{9,8},{10,9... | collective-permute-start | bytes 153608 | tf_op jit(solution)/shard_map/ppermute | solution.py:220
  60.0 4.5 %collective-permute-start.2 = (f32[100,128]{1,0:T(8,128)S(1)}, f32[100,128]{1,0:T(8,128)S(1)}, u32[]{:S(2)}, u32[]{:S(2)}) collective-permute-start(f32[100,128]{1,0:T(8,128)S(1)} %slot_bias.1.b0), channel_id=1, source_target_pairs={{0,2},{1,3},{2,0},{3,1},{4,6},{5,7},{6,4},{7,5},{8,10},{9,11},{10,... | collective-permute-start | bytes 153608 | tf_op jit(solution)/shard_map/ppermute | solution.py:220

commit v3 on v2

v3 whole, which is shorter than its diff:
```python
import functools
import math

import jax
import jax.numpy as jnp
from jax import lax
from jax.experimental import pallas as pl
from jax.experimental.pallas import tpu as pltpu
from jax.sharding import PartitionSpec as P

F32 = jnp.float32
BF16 = jnp.bfloat16
NT = (((1,), (1,)), ((), ()))
NN = (((1,), (0,)), ((), ()))

CAP = 4
GR = 32
GC = 256
LANES = 512
WIDE = LANES // 2
VROWS = 416
VCHUNK = 104
BLOCK = 8
VMEM = 24 * 1024 * 1024


def iota(shape, dim):
    return lax.broadcasted_iota(jnp.int32, shape, dim)


def dot(a, b, dims):
    return lax.dot_general(a, b, dims, preferred_element_type=F32)


def ones_where(mask):
    return jnp.where(mask, 1.0, 0.0).astype(BF16)


def send_kernel(*refs, steps):
    k_hbm, small_hbm, out, small, kbuf, acc, sems, small_sems = refs[0], refs[1:10], *refs[10:11], refs[11:20], *refs[20:]
    chans, obs, levels = k_hbm.shape
    per = chans // steps
    small_copies = [
        pltpu.make_async_copy(src, dst, small_sems.at[i]) for i, (src, dst) in enumerate(zip(small_hbm, small))
    ]
    copies = [
        pltpu.make_async_copy(k_hbm.at[pl.ds(i * per, per)], kbuf.at[pl.ds(i * per, per)], sems.at[i])
        for i in range(steps)
    ]
    for copy in small_copies[:2] + copies[:2] + small_copies[2:] + copies[2:]:
        copy.start()
    dep, inv, tile, frow, fcol, crow, ccol, predt, scan = small
    rows_out = out.shape[0]
    for copy in small_copies[:2]:
        copy.wait()
    wbf = (dep[...].astype(F32) * inv[...]).astype(BF16)
    w = wbf.astype(F32)

    def sums(i):
        copies[i].wait()
        for r in range(0, obs, 16):
            total = acc[r : r + 16, 0:levels]
            for c in range(i * per, (i + 1) * per):
                total = total + w[r : r + 16, c : c + 1] * kbuf[c, r : r + 16, :].astype(F32)
            acc[r : r + 16, 0:levels] = total

    acc[...] = jnp.zeros(acc.shape, F32)
    for i in range(steps // 2):
        sums(i)
    for copy in small_copies[2:]:
        copy.wait()

    tr = jnp.broadcast_to(tile[...].astype(F32), (obs, obs))
    ri, ci = iota((obs, obs), 0), iota((obs, obs), 1)
    tc = jnp.sum(jnp.where(ri == ci, tr, 0.0), 1, keepdims=True)
    rank = jnp.sum(jnp.where((tc == tr) & (ri < ci), 1.0, 0.0), 0, keepdims=True)
    slot = (tile[...].astype(F32) * (2 * CAP) + rank).astype(jnp.int32)
    at = iota((rows_out, obs), 0)
    first_half, second_half = ones_where(at == slot), ones_where(at == slot + CAP)

    base = levels - (LANES - 128)
    rows = iota((128, obs), 0)
    place = jnp.where(rows == base, frow[...].astype(F32), 0.0)
    place = jnp.where(rows == base + 1, fcol[...].astype(F32), place)
    place = jnp.where(rows == base + 2, crow[...].astype(F32), place)
    place = jnp.where(rows == base + 3, ccol[...].astype(F32), place)
    extra = dot(second_half, place.astype(BF16), NT)

    npred = predt.shape[0]
    kinds = 128
    ind = jnp.where(iota((kinds - npred, obs), 0) == scan[...], 1.0, 0.0)
    basist = jnp.concatenate([predt[...].astype(F32), ind], 0).astype(BF16)
    biast = dot(basist, wbf, NN)
    hi = biast.astype(BF16)
    lo = (biast - hi.astype(F32)).astype(BF16)
    half = chans // 2
    first = base + 4
    er, ec = iota((chans, 128), 0), iota((chans, 128), 1)
    qr, qk = iota((rows_out, kinds), 0), iota((rows_out, kinds), 1)
    for h in range(2):
        mine = (er >= h * half) & (er < (h + 1) * half)
        e = ones_where((ec == er - h * half + first) & mine)
        f = ones_where((ec == er - h * half + first + half) & mine)
        part = (dot(hi, e, NN) + dot(lo, f, NN)).astype(BF16)
        q = qk + h * kinds
        extra = extra + dot(ones_where(qr == (q // CAP) * (2 * CAP) + CAP + q % CAP), part, NN)

    for i in range(steps // 2, steps):
        sums(i)
    rows = acc[...].astype(BF16)
    placed = dot(first_half, rows[:, 0:WIDE], NN) + dot(second_half, rows[:, WIDE:LANES], NN)
    out[:, 0 : WIDE - 128] = placed[:, 0 : WIDE - 128].astype(BF16)
    out[:, WIDE - 128 : WIDE] = (placed[:, WIDE - 128 : WIDE] + extra).astype(BF16)


def picks(slots, offset):
    q, r = iota((slots, 2 * slots), 0), iota((slots, 2 * slots), 1)
    return ones_where(r == (q // CAP) * (2 * CAP) + q % CAP + offset)


def head_kernel(got, head, *, levels, half):
    slots = got.shape[0] // 2
    lanes = got[:, WIDE - 128 : WIDE]
    rest = jnp.transpose(dot(picks(slots, CAP), lanes, NN))
    at = VROWS - 16 - (LANES - 128)
    head[0:16, :] = rest[at : at + 16, :].astype(BF16)
    q, r = iota((8, 2 * slots), 0), iota((8, 2 * slots), 1)
    pick = ones_where(r % (2 * CAP) == q + CAP)
    total = dot(pick, lanes, NN)
    first = levels - (LANES - 128) + 4
    lane = iota((8, 128), 1)
    kept = 128 - first - half
    chunk = jnp.where(lane < half, pltpu.roll(total, 128 - first, 1), 0.0)
    chunk = chunk + jnp.where(lane < kept, pltpu.roll(total, 128 - first - half, 1), 0.0)
    high = chunk.astype(BF16).astype(F32)
    head[16:32, 0:128] = jnp.concatenate([high, chunk - high], 0).astype(BF16)
    head[16:32, 128:slots] = jnp.zeros((16, slots - 128), BF16)


def turn_kernel(got, out):
    slots = got.shape[0] // 2
    out[0:WIDE, :] = jnp.transpose(dot(picks(slots, 0), got[...], NN)).astype(BF16)
    rest = jnp.transpose(dot(picks(slots, CAP), got[...], NN))
    out[WIDE:VROWS, :] = rest[0 : VROWS - WIDE, :].astype(BF16)


def prep_kernel(first_row, h0, h1, h2, h3, colw, roww, lastw, chunk, *, levels):
    heads = (h0, h1, h2, h3)
    part = sum([h[16:32, 0:128].astype(F32) for h in heads])
    four = (part[0:8, :] + part[8:16, :])[0:CAP, :]
    eight = jnp.concatenate([four, four], 0)
    n_rows = chunk.shape[0]
    chunk[...] = jnp.broadcast_to(eight[None], (n_rows // 8, 8, 128)).reshape(n_rows, 128)
    tops = jnp.concatenate([h[0:16, :].astype(F32) for h in heads], 1)
    at = levels - (VROWS - 16)
    fr, cr = tops[at : at + 1, :], tops[at + 2 : at + 3, :]
    n = fr.shape[1]
    turned = jnp.transpose(tops)
    fc, cc = turned[:, at + 1 : at + 2], turned[:, at + 3 : at + 4].astype(jnp.int32)
    cols = iota((n, GC), 1)
    colw[...] = jnp.where(cols == cc, 1.0 - fc, jnp.where(cols == cc + 1, fc, 0.0)).astype(BF16)
    row = cr.astype(jnp.int32)
    rel = iota((BLOCK, n), 0) + first_row[0]
    roww[...] = jnp.where(rel == row, 1.0 - fr, 0.0) + jnp.where(rel == row + 1, fr, 0.0)
    lastw[...] = jnp.broadcast_to(jnp.where(row == GR - 1, fr, 0.0), lastw.shape)


def spill_kernel(a0, a1, a2, a3, colw, lastw, spill):
    part = a0.shape[1]
    out = jnp.zeros((VROWS, GC), F32)
    for j, ref in enumerate((a0, a1, a2, a3)):
        cols = slice(j * part, (j + 1) * part)
        lhs = (ref[...].astype(F32) * lastw[0:1, cols]).astype(BF16)
        out = out + dot(lhs, colw[cols, :], NN)
    spill[...] = out.astype(BF16)


def grid_kernel(a0, a1, a2, a3, colw, roww, out):
    part = a0.shape[1]
    total = jnp.zeros((VCHUNK * BLOCK, GC), F32)
    for j, ref in enumerate((a0, a1, a2, a3)):
        cols = slice(j * part, (j + 1) * part)
        lhs = ref[...].astype(F32)[:, None, :] * roww[:, cols][None, :, :]
        lhs = lhs.reshape(VCHUNK * BLOCK, part).astype(BF16)
        total = total + dot(lhs, colw[cols, :], NN)
    out[...] = total.reshape(VCHUNK, BLOCK, GC)


def join_kernel(grid, spill, out):
    first = iota((VCHUNK, BLOCK, GC), 1) == 0
    out[...] = grid[...] + jnp.where(first, spill[...].astype(F32)[:, None, :], 0.0)


def bias_kernel(got, out, *, half, scale):
    t = jnp.transpose(got[...]) * scale
    n = got.shape[0] // 2
    out[0:half, :] = t[0:half, 0:n]
    out[half : 2 * half, :] = t[0:half, n : 2 * n]


def whole(shape):
    return pl.BlockSpec(shape, lambda *_: (0,) * len(shape))


VM = pl.BlockSpec(memory_space=pltpu.VMEM)
HBM = pl.BlockSpec(memory_space=pltpu.HBM)


def per_device(
    departure, inv_var, k_matrix, frac_row, frac_col, dest_tile, cell_row, cell_col, predictors, scan_pos
):
    n_tile = lax.axis_size("tile")
    n_slot = lax.axis_size("slot")
    obs, chans, levels = k_matrix.shape
    slots = n_tile * CAP
    params = pltpu.CompilerParams(vmem_limit_bytes=VMEM)
    tight = pltpu.CompilerParams(vmem_limit_bytes=56 * 1024 * 1024)
    steps = 10
    flat = lambda x: x.reshape(1, obs)
    small = (
        departure,
        inv_var.reshape(1, chans),
        flat(dest_tile),
        flat(frac_row),
        flat(frac_col),
        flat(cell_row),
        flat(cell_col),
        predictors.T,
        flat(scan_pos),
    )
    send = pl.pallas_call(
        functools.partial(send_kernel, steps=steps),
        out_shape=jax.ShapeDtypeStruct((2 * slots, WIDE), BF16),
        in_specs=[HBM] * (1 + len(small)),
        out_specs=VM,
        scratch_shapes=[pltpu.VMEM(x.shape, x.dtype) for x in small]
        + [
            pltpu.VMEM((chans, obs, levels), BF16),
            pltpu.VMEM((obs, LANES), F32),
            pltpu.SemaphoreType.DMA((steps,)),
            pltpu.SemaphoreType.DMA((len(small),)),
        ],
        compiler_params=tight,
        name="send",
    )(jnp.transpose(k_matrix, (1, 0, 2)), *small)
    got = lax.all_to_all(send.reshape(n_tile, 2 * CAP, WIDE), "tile", 0, 0, tiled=True).reshape(2 * slots, WIDE)
    head = pl.pallas_call(
        functools.partial(head_kernel, levels=levels, half=chans // 2),
        out_shape=jax.ShapeDtypeStruct((32, slots), BF16),
        in_specs=[VM],
        out_specs=VM,
        compiler_params=params,
        name="head",
    )(got)
    turned = pl.pallas_call(
        turn_kernel,
        out_shape=jax.ShapeDtypeStruct((VROWS, slots), BF16),
        in_specs=[VM],
        out_specs=VM,
        compiler_params=params,
        name="turn",
    )(got)

    def around(x):
        return [x] + [lax.ppermute(x, "slot", [(i, (i + d) % n_slot) for i in range(n_slot)]) for d in (1, 3, 2)]

    turned, *heads = lax.optimization_barrier((turned, *around(head)))
    blocks = around(turned)
    total = n_slot * slots
    first_row = (lax.axis_index("slot") * BLOCK).astype(jnp.int32).reshape(1)
    colw, roww, lastw, chunk = pl.pallas_call(
        functools.partial(prep_kernel, levels=levels),
        out_shape=(
            jax.ShapeDtypeStruct((total, GC), BF16),
            jax.ShapeDtypeStruct((BLOCK, total), F32),
            jax.ShapeDtypeStruct((8, total), F32),
            jax.ShapeDtypeStruct((slots, 128), F32),
        ),
        in_specs=[pl.BlockSpec(memory_space=pltpu.SMEM)] + [VM] * 4,
        out_specs=(VM,) * 4,
        compiler_params=params,
        name="prep",
    )(first_row, *heads)
    chunks = lax.all_to_all(chunk.reshape(n_tile, CAP, 128), "tile", 0, 0, tiled=True).reshape(slots, 128)
    spill = pl.pallas_call(
        spill_kernel,
        out_shape=jax.ShapeDtypeStruct((VROWS, GC), BF16),
        in_specs=[VM] * 6,
        out_specs=VM,
        compiler_params=params,
        name="spill",
    )(*blocks, colw, lastw)
    pairs = [(t * n_slot, ((t + 1) % n_tile) * n_slot) for t in range(n_tile)]
    arrived = lax.ppermute(spill, ("tile", "slot"), pairs)
    level_block = pl.BlockSpec((VCHUNK, BLOCK, GC), lambda i: (i, 0, 0))
    own = pl.pallas_call(
        grid_kernel,
        grid=(VROWS // VCHUNK,),
        out_shape=jax.ShapeDtypeStruct((VROWS, BLOCK, GC), F32),
        in_specs=[pl.BlockSpec((VCHUNK, slots), lambda i: (i, 0))] * 4 + [whole((total, GC)), whole((BLOCK, total))],
        out_specs=level_block,
        compiler_params=params,
        name="grid",
    )(*blocks, colw, roww)
    grid = pl.pallas_call(
        join_kernel,
        grid=(VROWS // VCHUNK,),
        out_shape=jax.ShapeDtypeStruct((levels, BLOCK, GC), F32),
        in_specs=[level_block, pl.BlockSpec((VCHUNK, GC), lambda i: (i, 0))],
        out_specs=level_block,
        compiler_params=params,
        name="join",
    )(own, arrived)
    chunks, grid = lax.optimization_barrier((chunks, grid))
    bias = pl.pallas_call(
        functools.partial(bias_kernel, half=chans // 2, scale=1.0 / math.sqrt(obs * n_tile * n_slot)),
        out_shape=jax.ShapeDtypeStruct((chans, 128), F32),
        in_specs=[VM],
        out_specs=VM,
        compiler_params=params,
        name="bias",
    )(chunks)
    return jnp.transpose(grid, (1, 2, 0)), bias


def solution(mesh):
    both = ("tile", "slot")
    placed = (
        P(both, None),
        P(),
        P(both, None, None),
        P(both),
        P(both),
        P(both, None),
        P(both),
        P(both),
        P(both, None),
        P(both),
    )
    return jax.shard_map(
        per_device,
        mesh=mesh,
        in_specs=placed,
        out_specs=(P(both, None, None), P()),
        check_vma=False,
    )
```

time: 65.4 us -> 65.9 us (level)
  the two profiles are of different devices: /device:TPU:1 before, /device:TPU:0 now
where the time goes in v3:
time: 65.9 us; the launch traced here: 65.7 us
  blocking collectives  23.3 us (35%)
  Pallas kernels  14.5 us (22%)
  starting transfers between devices  14.3 us (22%)
  waiting for transfers between devices  12.9 us (20%)
  between operations  0.7 us (1%)
    all_to_all x1, blocking collectives, per_device(): lax.all_to_all(send.reshape(n_tile, 2 * CAP, WIDE), 'tile', 0, 0, tiled=T...  23.3 us
    ppermute x6, starting transfers between devices, around(): lax.ppermute(x, 'slot', [(i, (i + d) % n_slot) for i in range(n_slot)])  7.49 us
    ppermute x6, waiting for transfers between devices, around(): lax.ppermute(x, 'slot', [(i, (i + d) % n_slot) for i in range(n_slot)])  6.81 us
    pallas_call x1, Pallas kernels, per_device(): pl.pallas_call(functools.partial(send_kernel, steps=steps), out_shape=jax...  6.54 us
    ppermute x1, waiting for transfers between devices, per_device(): arrived = lax.ppermute(spill, ('tile', 'slot'), pairs)  6.04 us
    all_to_all x1, starting transfers between devices, per_device(): lax.all_to_all(chunk.reshape(n_tile, CAP, 128), 'tile', 0, 0, tiled=True)  4.91 us
    pallas_call x1, Pallas kernels, per_device(): pl.pallas_call(grid_kernel, grid=(VROWS // VCHUNK,), out_shape=jax.ShapeD...  2.51 us
    pallas_call x1, Pallas kernels, per_device(): pl.pallas_call(join_kernel, grid=(VROWS // VCHUNK,), out_shape=jax.ShapeD...  2.3 us
  transfers between devices with their start and end apart: 8, of which 5 were waited for; matrix products, arithmetic and copies ran while one was open for 0% of the time, Pallas kernels for 11%

profile of v3, /device:TPU:0, one launch (start us, length us, event | category | flops | bytes accessed | tf_op | source)
XLA Modules:
  0.0 65.7 jit_solution(2909724848026837048)
XLA Ops:
  0.6 6.5 %send.1 = bf16[512,256]{1,0:T(8,128)(2,1)} custom-call(bf16[100,96,411]{2,1,0:T(8,128)(2,1)} %bitcast.18, bf16[96,100]{1,0:T(8,128)(2,1)} %refs_1_.1, f32[1,100]{1,0:T(1,128)} %bitcast.22, s32[1,96]{1,0:T(1,128)} %bitcast.23, bf16[1,96]{1,0:T(2,128)(2,1)} %bitcast.24, bf16[1,96]{1,0:T(2,128)(2,1)} %bitcast.25, s32[1,96]{1,0:T(1,128)} %bitcast.26, ...), custom_call_target="tpu_custom_call" | custom-call | tf_op jit(solution)/shard_map/send/pallas_call | solution.py:231
  7.2 23.3 %all_to_all.10 = bf16[64,8,256]{2,1,0:T(8,128)(2,1)S(1)} all-to-all(bf16[64,8,256]{2,1,0:T(8,128)(2,1)} %bitcast.20), channel_id=1, replica_groups=mesh['tile'=64,'slot'=4] {'tile'}, dimensions={0} | all-to-all | bytes 524288 | tf_op jit(solution)/shard_map/all_to_all | solution.py:246
  30.5 0.3 head.1.h0
  30.8 3.1 %collective-permute-start.2 = (bf16[32,256]{1,0:T(8,128)(2,1)S(1)}, bf16[32,256]{1,0:T(8,128)(2,1)S(1)}, u32[]{:S(2)}, u32[]{:S(2)}) collective-permute-start(bf16[32,256]{1,0:T(8,128)(2,1)S(1)} %head.1.h0), channel_id=1, source_target_pairs={{0,2},{1,3},{2,0},{3,1},{4,6},{5,7},{6,4},{7,5},{8,10},{9,11},{10,... | collective-permute-start | bytes 49160 | tf_op jit(solution)/shard_map/ppermute | solution.py:265
  33.9 1.1 %collective-permute-start.1 = (bf16[32,256]{1,0:T(8,128)(2,1)S(1)}, bf16[32,256]{1,0:T(8,128)(2,1)S(1)}, u32[]{:S(2)}, u32[]{:S(2)}) collective-permute-start(bf16[32,256]{1,0:T(8,128)(2,1)S(1)} %head.1.h0), channel_id=1, source_target_pairs={{0,3},{1,0},{2,1},{3,2},{4,7},{5,4},{6,5},{7,6},{8,11},{9,8},{10,9... | collective-permute-start | bytes 49160 | tf_op jit(solution)/shard_map/ppermute | solution.py:265
  35.1 0.9 %collective-permute-start = (bf16[32,256]{1,0:T(8,128)(2,1)S(1)}, bf16[32,256]{1,0:T(8,128)(2,1)S(1)}, u32[]{:S(2)}, u32[]{:S(2)}) collective-permute-start(bf16[32,256]{1,0:T(8,128)(2,1)S(1)} %head.1.h0), channel_id=1, source_target_pairs={{0,1},{1,2},{2,3},{3,0},{4,5},{5,6},{6,7},{7,4},{8,9},{9,10},{10,1... | collective-permute-start | bytes 49160 | tf_op jit(solution)/shard_map/ppermute | solution.py:265
  35.9 0.4 turn.1.a0
  36.3 0.0 collective-permute-done.2.h3
  36.4 1.3 %collective-permute-done.1.h2 = bf16[32,256]{1,0:T(8,128)(2,1)S(1)} collective-permute-done((bf16[32,256]{1,0:T(8,128)(2,1)S(1)}, bf16[32,256]{1,0:T(8,128)(2,1)S(1)}, u32[]{:S(2)}, u32[]{:S(2)}) %collective-permute-start.1) | collective-permute-done | bytes 16416 | tf_op jit(solution)/shard_map/ppermute | solution.py:265
  37.7 2.4 %collective-permute-done.h1 = bf16[32,256]{1,0:T(8,128)(2,1)S(1)} collective-permute-done((bf16[32,256]{1,0:T(8,128)(2,1)S(1)}, bf16[32,256]{1,0:T(8,128)(2,1)S(1)}, u32[]{:S(2)}, u32[]{:S(2)}) %collective-permute-start) | collective-permute-done | bytes 16416 | tf_op jit(solution)/shard_map/ppermute | solution.py:265
  40.0 0.3 collective-permute-start.5
  40.3 2.0 %collective-permute-start.4 = (bf16[416,256]{1,0:T(8,128)(2,1)S(1)}, bf16[416,256]{1,0:T(8,128)(2,1)S(1)}, u32[]{:S(2)}, u32[]{:S(2)}) collective-permute-start(bf16[416,256]{1,0:T(8,128)(2,1)S(1)} %turn.1.a0), channel_id=1, source_target_pairs={{0,3},{1,0},{2,1},{3,2},{4,7},{5,4},{6,5},{7,6},{8,11},{9,8},{10,9... | collective-permute-start | bytes 638984 | tf_op jit(solution)/shard_map/ppermute | solution.py:265
  42.4 0.0 collective-permute-start.3
  42.4 1.3 %prep.1 = (bf16[1024,256]{1,0:T(8,128)(2,1)S(1)}, f32[8,1024]{1,0:T(8,128)S(1)}, f32[8,1024]{1,0:T(8,128)S(1)}, f32[256,128]{1,0:T(8,128)}) custom-call(s32[1]{0:T(128)} %bitcast.first_row, bf16[32,256]{1,0:T(8,128)(2,1)S(1)} %head.1.h0, bf16[32,256]{1,0:T(8,128)(2,1)S(1)} %collective-permute-done.h1, bf16[32,256]{1,0:T(8,128)(2,1)S(1)} %collective-permute-done.1.h2, ...), custom_call_target="tpu_custom_call" | custom-call | tf_op jit(solution)/shard_map/prep/pallas_call | solution.py:271
  43.7 4.9 %all-to-all-start.1 = ((f32[64,4,128]{2,1,0:T(4,128)}), f32[64,4,128]{2,1,0:T(4,128)S(1)}, u32[]{:S(2)}, u32[]{:S(2)}) async-start(f32[64,4,128]{2,1,0:T(4,128)} %bitcast.12), calls=%async_computation.1 | async-start | bytes 262144 | tf_op jit(solution)/shard_map/all_to_all | solution.py:284
  48.6 0.9 %collective-permute-done.5.a3 = bf16[416,256]{1,0:T(8,128)(2,1)S(1)} collective-permute-done((bf16[416,256]{1,0:T(8,128)(2,1)S(1)}, bf16[416,256]{1,0:T(8,128)(2,1)S(1)}, u32[]{:S(2)}, u32[]{:S(2)}) %collective-permute-start.5) | collective-permute-done | bytes 213024 | tf_op jit(solution)/shard_map/ppermute | solution.py:265
  49.5 0.0 collective-permute-done.4.a2
  49.6 2.2 %collective-permute-done.3.a1 = bf16[416,256]{1,0:T(8,128)(2,1)S(1)} collective-permute-done((bf16[416,256]{1,0:T(8,128)(2,1)S(1)}, bf16[416,256]{1,0:T(8,128)(2,1)S(1)}, u32[]{:S(2)}, u32[]{:S(2)}) %collective-permute-start.3) | collective-permute-done | bytes 213024 | tf_op jit(solution)/shard_map/ppermute | solution.py:265
  51.8 0.4 spill.1
  52.2 1.9 %collective-permute-start.6 = (bf16[416,256]{1,0:T(8,128)(2,1)S(1)}, bf16[416,256]{1,0:T(8,128)(2,1)S(1)}, u32[]{:S(2)}, u32[]{:S(2)}) collective-permute-start(bf16[416,256]{1,0:T(8,128)(2,1)S(1)} %spill.1), channel_id=1, source_target_pairs={{0,4},{4,8},{8,12},{12,16},{16,20},{20,24},{24,28},{28,32},{32,36}... | collective-permute-start | bytes 638984 | tf_op jit(solution)/shard_map/ppermute | solution.py:294
  54.1 2.5 %grid.1 = f32[416,8,256]{2,1,0:T(8,128)S(1)} custom-call(bf16[416,256]{1,0:T(8,128)(2,1)S(1)} %turn.1.a0, bf16[416,256]{1,0:T(8,128)(2,1)S(1)} %collective-permute-done.3.a1, bf16[416,256]{1,0:T(8,128)(2,1)S(1)} %collective-permute-done.4.a2, bf16[416,256]{1,0:T(8,128)(2,1)S(1)} %collective-permute-done.5.a3, bf16[1024,256]{1,0:T(8,128)(2,1)S(1)} %get-tuple-element.19.colw, ...), custom_call_target="tpu_custom_call" | custom-call | tf_op jit(solution)/shard_map/grid/pallas_call | solution.py:296
  56.6 6.0 %collective-permute-done.6.spill = bf16[416,256]{1,0:T(8,128)(2,1)S(1)} collective-permute-done((bf16[416,256]{1,0:T(8,128)(2,1)S(1)}, bf16[416,256]{1,0:T(8,128)(2,1)S(1)}, u32[]{:S(2)}, u32[]{:S(2)}) %collective-permute-start.6) | collective-permute-done | bytes 213024 | tf_op jit(solution)/shard_map/ppermute | solution.py:294
  62.7 2.3 %join.1 = f32[411,8,256]{2,1,0:T(8,128)} custom-call(f32[416,8,256]{2,1,0:T(8,128)S(1)} %grid.1, bf16[416,256]{1,0:T(8,128)(2,1)S(1)} %collective-permute-done.6.spill), custom_call_target="tpu_custom_call" | custom-call | tf_op jit(solution)/shard_map/join/pallas_call | solution.py:305
  65.0 0.0 all-to-all-done.1
  65.0 0.7 %bias.1 = f32[100,128]{1,0:T(8,128)} custom-call(f32[256,128]{1,0:T(8,128)S(1)} %bitcast.17), custom_call_target="tpu_custom_call" | custom-call | tf_op jit(solution)/shard_map/bias/pallas_call | solution.py:315
Async XLA Ops:
  30.8 5.5 %collective-permute-start.2 = (bf16[32,256]{1,0:T(8,128)(2,1)S(1)}, bf16[32,256]{1,0:T(8,128)(2,1)S(1)}, u32[]{:S(2)}, u32[]{:S(2)}) collective-permute-start(bf16[32,256]{1,0:T(8,128)(2,1)S(1)} %head.1.h0), channel_id=1, source_target_pairs={{0,2},{1,3},{2,0},{3,1},{4,6},{5,7},{6,4},{7,5},{8,10},{9,11},{10,... | collective-permute-start | bytes 49160 | tf_op jit(solution)/shard_map/ppermute | solution.py:265
  33.9 3.7 %collective-permute-start.1 = (bf16[32,256]{1,0:T(8,128)(2,1)S(1)}, bf16[32,256]{1,0:T(8,128)(2,1)S(1)}, u32[]{:S(2)}, u32[]{:S(2)}) collective-permute-start(bf16[32,256]{1,0:T(8,128)(2,1)S(1)} %head.1.h0), channel_id=1, source_target_pairs={{0,3},{1,0},{2,1},{3,2},{4,7},{5,4},{6,5},{7,6},{8,11},{9,8},{10,9... | collective-permute-start | bytes 49160 | tf_op jit(solution)/shard_map/ppermute | solution.py:265
  35.1 4.9 %collective-permute-start = (bf16[32,256]{1,0:T(8,128)(2,1)S(1)}, bf16[32,256]{1,0:T(8,128)(2,1)S(1)}, u32[]{:S(2)}, u32[]{:S(2)}) collective-permute-start(bf16[32,256]{1,0:T(8,128)(2,1)S(1)} %head.1.h0), channel_id=1, source_target_pairs={{0,1},{1,2},{2,3},{3,0},{4,5},{5,6},{6,7},{7,4},{8,9},{9,10},{10,1... | collective-permute-start | bytes 49160 | tf_op jit(solution)/shard_map/ppermute | solution.py:265
  40.0 9.5 %collective-permute-start.5 = (bf16[416,256]{1,0:T(8,128)(2,1)S(1)}, bf16[416,256]{1,0:T(8,128)(2,1)S(1)}, u32[]{:S(2)}, u32[]{:S(2)}) collective-permute-start(bf16[416,256]{1,0:T(8,128)(2,1)S(1)} %turn.1.a0), channel_id=1, source_target_pairs={{0,2},{1,3},{2,0},{3,1},{4,6},{5,7},{6,4},{7,5},{8,10},{9,11},{10,... | collective-permute-start | bytes 638984 | tf_op jit(solution)/shard_map/ppermute | solution.py:265
  40.3 9.3 %collective-permute-start.4 = (bf16[416,256]{1,0:T(8,128)(2,1)S(1)}, bf16[416,256]{1,0:T(8,128)(2,1)S(1)}, u32[]{:S(2)}, u32[]{:S(2)}) collective-permute-start(bf16[416,256]{1,0:T(8,128)(2,1)S(1)} %turn.1.a0), channel_id=1, source_target_pairs={{0,3},{1,0},{2,1},{3,2},{4,7},{5,4},{6,5},{7,6},{8,11},{9,8},{10,9... | collective-permute-start | bytes 638984 | tf_op jit(solution)/shard_map/ppermute | solution.py:265
  42.4 9.4 %collective-permute-start.3 = (bf16[416,256]{1,0:T(8,128)(2,1)S(1)}, bf16[416,256]{1,0:T(8,128)(2,1)S(1)}, u32[]{:S(2)}, u32[]{:S(2)}) collective-permute-start(bf16[416,256]{1,0:T(8,128)(2,1)S(1)} %turn.1.a0), channel_id=1, source_target_pairs={{0,1},{1,2},{2,3},{3,0},{4,5},{5,6},{6,7},{7,4},{8,9},{9,10},{10,1... | collective-permute-start | bytes 638984 | tf_op jit(solution)/shard_map/ppermute | solution.py:265
  43.7 21.3 %all-to-all-start.1 = ((f32[64,4,128]{2,1,0:T(4,128)}), f32[64,4,128]{2,1,0:T(4,128)S(1)}, u32[]{:S(2)}, u32[]{:S(2)}) async-start(f32[64,4,128]{2,1,0:T(4,128)} %bitcast.12), calls=%async_computation.1 | async-start | bytes 262144 | tf_op jit(solution)/shard_map/all_to_all | solution.py:284
  52.2 10.5 %collective-permute-start.6 = (bf16[416,256]{1,0:T(8,128)(2,1)S(1)}, bf16[416,256]{1,0:T(8,128)(2,1)S(1)}, u32[]{:S(2)}, u32[]{:S(2)}) collective-permute-start(bf16[416,256]{1,0:T(8,128)(2,1)S(1)} %spill.1), channel_id=1, source_target_pairs={{0,4},{4,8},{8,12},{12,16},{16,20},{20,24},{24,28},{28,32},{32,36}... | collective-permute-start | bytes 638984 | tf_op jit(solution)/shard_map/ppermute | solution.py:294

commit v4 on v3

--- a/solution.py
+++ b/solution.py
@@ -19,7 +19,7 @@
 LANES = 512
 WIDE = LANES // 2
 VROWS = 416
-VCHUNK = 104
+PARTS = ((0, 112), (112, 224), (224, 320), (320, 416))
 BLOCK = 8
 VMEM = 24 * 1024 * 1024
 
@@ -51,6 +51,22 @@
         copy.start()
     dep, inv, tile, frow, fcol, crow, ccol, predt, scan = small
     rows_out = out.shape[0]
+
+    kinds = 128
+    half = chans // 2
+    base = levels - (LANES - 128)
+    first = base + 4
+    er, ec = iota((chans, 128), 0), iota((chans, 128), 1)
+    qr, qk = iota((rows_out, kinds), 0), iota((rows_out, kinds), 1)
+    spreads, places = [], []
+    for h in range(2):
+        mine = (er >= h * half) & (er < (h + 1) * half)
+        e = ones_where((ec == er - h * half + first) & mine)
+        f = ones_where((ec == er - h * half + first + half) & mine)
+        spreads.append((e, f))
+        q = qk + h * kinds
+        places.append(ones_where(qr == (q // CAP) * (2 * CAP) + CAP + q % CAP))
+    acc[...] = jnp.zeros(acc.shape, F32)
     for copy in small_copies[:2]:
         copy.wait()
     wbf = (dep[...].astype(F32) * inv[...]).astype(BF16)
@@ -64,7 +80,6 @@
                 total = total + w[r : r + 16, c : c + 1] * kbuf[c, r : r + 16, :].astype(F32)
             acc[r : r + 16, 0:levels] = total
 
-    acc[...] = jnp.zeros(acc.shape, F32)
     for i in range(steps // 2):
         sums(i)
     for copy in small_copies[2:]:
@@ -78,7 +93,6 @@
     at = iota((rows_out, obs), 0)
     first_half, second_half = ones_where(at == slot), ones_where(at == slot + CAP)
 
-    base = levels - (LANES - 128)
     rows = iota((128, obs), 0)
     place = jnp.where(rows == base, frow[...].astype(F32), 0.0)
     place = jnp.where(rows == base + 1, fcol[...].astype(F32), place)
@@ -87,23 +101,14 @@
     extra = dot(second_half, place.astype(BF16), NT)
 
     npred = predt.shape[0]
-    kinds = 128
     ind = jnp.where(iota((kinds - npred, obs), 0) == scan[...], 1.0, 0.0)
     basist = jnp.concatenate([predt[...].astype(F32), ind], 0).astype(BF16)
     biast = dot(basist, wbf, NN)
     hi = biast.astype(BF16)
     lo = (biast - hi.astype(F32)).astype(BF16)
-    half = chans // 2
-    first = base + 4
-    er, ec = iota((chans, 128), 0), iota((chans, 128), 1)
-    qr, qk = iota((rows_out, kinds), 0), iota((rows_out, kinds), 1)
-    for h in range(2):
-        mine = (er >= h * half) & (er < (h + 1) * half)
-        e = ones_where((ec == er - h * half + first) & mine)
-        f = ones_where((ec == er - h * half + first + half) & mine)
+    for (e, f), place in zip(spreads, places):
         part = (dot(hi, e, NN) + dot(lo, f, NN)).astype(BF16)
-        q = qk + h * kinds
-        extra = extra + dot(ones_where(qr == (q // CAP) * (2 * CAP) + CAP + q % CAP), part, NN)
+        extra = extra + dot(place, part, NN)
 
     for i in range(steps // 2, steps):
         sums(i)
@@ -137,11 +142,12 @@
     head[16:32, 128:slots] = jnp.zeros((16, slots - 128), BF16)
 
 
-def turn_kernel(got, out):
+def turn_kernel(got, head, out):
     slots = got.shape[0] // 2
     out[0:WIDE, :] = jnp.transpose(dot(picks(slots, 0), got[...], NN)).astype(BF16)
     rest = jnp.transpose(dot(picks(slots, CAP), got[...], NN))
-    out[WIDE:VROWS, :] = rest[0 : VROWS - WIDE, :].astype(BF16)
+    out[WIDE : VROWS - 16, :] = rest[0 : VROWS - 16 - WIDE, :].astype(BF16)
+    out[VROWS - 16 : VROWS, :] = head[0:16, :]
 
 
 def prep_kernel(first_row, h0, h1, h2, h3, colw, roww, lastw, chunk, *, levels):
@@ -165,30 +171,41 @@
     lastw[...] = jnp.broadcast_to(jnp.where(row == GR - 1, fr, 0.0), lastw.shape)
 
 
-def spill_kernel(a0, a1, a2, a3, colw, lastw, spill):
+def spill_kernel(a0, a1, a2, a3, colw, lastw, *spills):
     part = a0.shape[1]
     out = jnp.zeros((VROWS, GC), F32)
     for j, ref in enumerate((a0, a1, a2, a3)):
         cols = slice(j * part, (j + 1) * part)
         lhs = (ref[...].astype(F32) * lastw[0:1, cols]).astype(BF16)
         out = out + dot(lhs, colw[cols, :], NN)
-    spill[...] = out.astype(BF16)
+    for spill, (lo, hi) in zip(spills, PARTS):
+        spill[...] = out[lo:hi, :].astype(BF16)
 
 
 def grid_kernel(a0, a1, a2, a3, colw, roww, out):
     part = a0.shape[1]
-    total = jnp.zeros((VCHUNK * BLOCK, GC), F32)
-    for j, ref in enumerate((a0, a1, a2, a3)):
-        cols = slice(j * part, (j + 1) * part)
-        lhs = ref[...].astype(F32)[:, None, :] * roww[:, cols][None, :, :]
-        lhs = lhs.reshape(VCHUNK * BLOCK, part).astype(BF16)
-        total = total + dot(lhs, colw[cols, :], NN)
-    out[...] = total.reshape(VCHUNK, BLOCK, GC)
-
-
-def join_kernel(grid, spill, out):
-    first = iota((VCHUNK, BLOCK, GC), 1) == 0
-    out[...] = grid[...] + jnp.where(first, spill[...].astype(F32)[:, None, :], 0.0)
+    for lo, hi in PARTS:
+        total = jnp.zeros(((hi - lo) * BLOCK, GC), F32)
+        for j, ref in enumerate((a0, a1, a2, a3)):
+            cols = slice(j * part, (j + 1) * part)
+            lhs = ref[lo:hi, :].astype(F32)[:, None, :] * roww[:, cols][None, :, :]
+            lhs = lhs.reshape((hi - lo) * BLOCK, part).astype(BF16)
+            total = total + dot(lhs, colw[cols, :], NN)
+        out[lo:hi] = total.reshape(hi - lo, BLOCK, GC)
+
+
+def join_kernel(grid, *refs):
+    spills, out, joined, sems = refs[0 : len(PARTS)], *refs[len(PARTS) :]
+    levels = out.shape[0]
+    copies = []
+    for i, (lo, hi) in enumerate(PARTS):
+        first = iota((hi - lo, BLOCK, GC), 1) == 0
+        joined[lo:hi] = grid[lo:hi] + jnp.where(first, spills[i][...].astype(F32)[:, None, :], 0.0)
+        size = min(hi, levels) - lo
+        copies.append(pltpu.make_async_copy(joined.at[pl.ds(lo, size)], out.at[pl.ds(lo, size)], sems.at[i]))
+        copies[i].start()
+    for copy in copies:
+        copy.wait()
 
 
 def bias_kernel(got, out, *, half, scale):
@@ -196,10 +213,6 @@
     n = got.shape[0] // 2
     out[0:half, :] = t[0:half, 0:n]
     out[half : 2 * half, :] = t[0:half, n : 2 * n]
-
-
-def whole(shape):
-    return pl.BlockSpec(shape, lambda *_: (0,) * len(shape))
 
 
 VM = pl.BlockSpec(memory_space=pltpu.VMEM)
@@ -255,16 +268,17 @@
     turned = pl.pallas_call(
         turn_kernel,
         out_shape=jax.ShapeDtypeStruct((VROWS, slots), BF16),
-        in_specs=[VM],
-        out_specs=VM,
-        compiler_params=params,
+        in_specs=[VM, VM],
+        out_specs=VM,
+        compiler_params=params,
+        cost_estimate=pl.CostEstimate(flops=2**30, bytes_accessed=2**22, transcendentals=0),
         name="turn",
-    )(got)
+    )(got, head)
 
     def around(x):
         return [x] + [lax.ppermute(x, "slot", [(i, (i + d) % n_slot) for i in range(n_slot)]) for d in (1, 3, 2)]
 
-    turned, *heads = lax.optimization_barrier((turned, *around(head)))
+    heads = around(head)
     blocks = around(turned)
     total = n_slot * slots
     first_row = (lax.axis_index("slot") * BLOCK).astype(jnp.int32).reshape(1)
@@ -279,38 +293,41 @@
         in_specs=[pl.BlockSpec(memory_space=pltpu.SMEM)] + [VM] * 4,
         out_specs=(VM,) * 4,
         compiler_params=params,
+        cost_estimate=pl.CostEstimate(flops=10**11, bytes_accessed=10**8, transcendentals=0),
         name="prep",
     )(first_row, *heads)
     chunks = lax.all_to_all(chunk.reshape(n_tile, CAP, 128), "tile", 0, 0, tiled=True).reshape(slots, 128)
-    spill = pl.pallas_call(
+    spills = pl.pallas_call(
         spill_kernel,
-        out_shape=jax.ShapeDtypeStruct((VROWS, GC), BF16),
+        out_shape=tuple(jax.ShapeDtypeStruct((hi - lo, GC), BF16) for lo, hi in PARTS),
         in_specs=[VM] * 6,
-        out_specs=VM,
+        out_specs=(VM,) * len(PARTS),
         compiler_params=params,
         name="spill",
     )(*blocks, colw, lastw)
-    pairs = [(t * n_slot, ((t + 1) % n_tile) * n_slot) for t in range(n_tile)]
-    arrived = lax.ppermute(spill, ("tile", "slot"), pairs)
-    level_block = pl.BlockSpec((VCHUNK, BLOCK, GC), lambda i: (i, 0, 0))
+    arrived = [
+        lax.ppermute(
+            x, ("tile", "slot"), [(t * n_slot + q % n_slot, ((t + 1) % n_tile) * n_slot) for t in range(n_tile)]
+        )
+        for q, x in enumerate(spills)
+    ]
     own = pl.pallas_call(
         grid_kernel,
-        grid=(VROWS // VCHUNK,),
         out_shape=jax.ShapeDtypeStruct((VROWS, BLOCK, GC), F32),
-        in_specs=[pl.BlockSpec((VCHUNK, slots), lambda i: (i, 0))] * 4 + [whole((total, GC)), whole((BLOCK, total))],
-        out_specs=level_block,
+        in_specs=[VM] * 6,
+        out_specs=VM,
         compiler_params=params,
         name="grid",
     )(*blocks, colw, roww)
     grid = pl.pallas_call(
         join_kernel,
-        grid=(VROWS // VCHUNK,),
         out_shape=jax.ShapeDtypeStruct((levels, BLOCK, GC), F32),
-        in_specs=[level_block, pl.BlockSpec((VCHUNK, GC), lambda i: (i, 0))],
-        out_specs=level_block,
+        in_specs=[VM] * (1 + len(PARTS)),
+        out_specs=HBM,
+        scratch_shapes=[pltpu.VMEM((VROWS, BLOCK, GC), F32), pltpu.SemaphoreType.DMA((len(PARTS),))],
         compiler_params=params,
         name="join",
-    )(own, arrived)
+    )(own, *arrived)
     chunks, grid = lax.optimization_barrier((chunks, grid))
     bias = pl.pallas_call(
         functools.partial(bias_kernel, half=chans // 2, scale=1.0 / math.sqrt(obs * n_tile * n_slot)),

time: 65.9 us -> 68.5 us (1.039)
  the two profiles are of different devices: /device:TPU:0 before, /device:TPU:1 now
where the time goes in v4:
time: 68.5 us; the launch traced here: 68.2 us
  starting transfers between devices  37.2 us (54%)
  waiting for transfers between devices  16.7 us (24%)
  Pallas kernels  13.5 us (20%)
  between operations  0.78 us (1%)
    all_to_all x1, starting transfers between devices, per_device(): lax.all_to_all(send.reshape(n_tile, 2 * CAP, WIDE), 'tile', 0, 0, tiled=T...  13.2 us
    all_to_all x1, waiting for transfers between devices, per_device(): lax.all_to_all(send.reshape(n_tile, 2 * CAP, WIDE), 'tile', 0, 0, tiled=T...  13.2 us
    all_to_all x1, starting transfers between devices, per_device(): lax.all_to_all(chunk.reshape(n_tile, CAP, 128), 'tile', 0, 0, tiled=True)  9.33 us
    ppermute x4, starting transfers between devices, per_device(): lax.ppermute(x, ('tile', 'slot'), [(t * n_slot + q % n_slot, (t + 1) % n_...  7.59 us
    ppermute x6, starting transfers between devices, around(): lax.ppermute(x, 'slot', [(i, (i + d) % n_slot) for i in range(n_slot)])  7.09 us
    pallas_call x1, Pallas kernels, per_device(): pl.pallas_call(functools.partial(send_kernel, steps=steps), out_shape=jax...  6.53 us
    ppermute x4, waiting for transfers between devices, per_device(): lax.ppermute(x, ('tile', 'slot'), [(t * n_slot + q % n_slot, (t + 1) % n_...  3.54 us
    pallas_call x1, Pallas kernels, per_device(): pl.pallas_call(grid_kernel, out_shape=jax.ShapeDtypeStruct((VROWS, BLOCK,...  1.94 us
  transfers between devices with their start and end apart: 12, of which 3 were waited for; matrix products, arithmetic and copies ran while one was open for 0% of the time, Pallas kernels for 9%

profile of v4, /device:TPU:1, one launch (start us, length us, event | category | flops | bytes accessed | tf_op | source)
XLA Modules:
  0.0 68.2 jit_solution(17818921135718865388)
XLA Ops:
  0.6 6.5 %send.1 = bf16[512,256]{1,0:T(8,128)(2,1)} custom-call(bf16[100,96,411]{2,1,0:T(8,128)(2,1)} %bitcast.18, bf16[96,100]{1,0:T(8,128)(2,1)} %refs_1_.1, f32[1,100]{1,0:T(1,128)} %bitcast.22, s32[1,96]{1,0:T(1,128)} %bitcast.23, bf16[1,96]{1,0:T(2,128)(2,1)} %bitcast.24, bf16[1,96]{1,0:T(2,128)(2,1)} %bitcast.25, s32[1,96]{1,0:T(1,128)} %bitcast.26, ...), custom_call_target="tpu_custom_call" | custom-call | tf_op jit(solution)/shard_map/send/pallas_call | solution.py:244
  7.2 13.2 %all-to-all-start = ((bf16[64,8,256]{2,1,0:T(8,128)(2,1)}), bf16[64,8,256]{2,1,0:T(8,128)(2,1)S(1)}, u32[]{:S(2)}, u32[]{:S(2)}) async-start(bf16[64,8,256]{2,1,0:T(8,128)(2,1)} %bitcast.20), calls=%async_computation | async-start | bytes 524288 | tf_op jit(solution)/shard_map/all_to_all | solution.py:259
  20.4 13.2 %all-to-all-done = bf16[64,8,256]{2,1,0:T(8,128)(2,1)S(1)} async-done(((bf16[64,8,256]{2,1,0:T(8,128)(2,1)}), bf16[64,8,256]{2,1,0:T(8,128)(2,1)S(1)}, u32[]{:S(2)}, u32[]{:S(2)}) %all-to-all-start) | async-done | bytes 262176 | tf_op jit(solution)/shard_map/all_to_all | solution.py:259
  33.5 0.3 head.1.h0
  33.8 2.8 %collective-permute-start.2 = (bf16[32,256]{1,0:T(8,128)(2,1)S(1)}, bf16[32,256]{1,0:T(8,128)(2,1)S(1)}, u32[]{:S(2)}, u32[]{:S(2)}) collective-permute-start(bf16[32,256]{1,0:T(8,128)(2,1)S(1)} %head.1.h0), channel_id=1, source_target_pairs={{0,2},{1,3},{2,0},{3,1},{4,6},{5,7},{6,4},{7,5},{8,10},{9,11},{10,... | collective-permute-start | bytes 49160 | tf_op jit(solution)/shard_map/ppermute | solution.py:279
  36.6 0.9 %collective-permute-start.1 = (bf16[32,256]{1,0:T(8,128)(2,1)S(1)}, bf16[32,256]{1,0:T(8,128)(2,1)S(1)}, u32[]{:S(2)}, u32[]{:S(2)}) collective-permute-start(bf16[32,256]{1,0:T(8,128)(2,1)S(1)} %head.1.h0), channel_id=1, source_target_pairs={{0,3},{1,0},{2,1},{3,2},{4,7},{5,4},{6,5},{7,6},{8,11},{9,8},{10,9... | collective-permute-start | bytes 49160 | tf_op jit(solution)/shard_map/ppermute | solution.py:279
  37.5 0.6 collective-permute-start
  38.1 0.4 turn.1.a0
  38.5 0.7 %collective-permute-start.5 = (bf16[416,256]{1,0:T(8,128)(2,1)S(1)}, bf16[416,256]{1,0:T(8,128)(2,1)S(1)}, u32[]{:S(2)}, u32[]{:S(2)}) collective-permute-start(bf16[416,256]{1,0:T(8,128)(2,1)S(1)} %turn.1.a0), channel_id=1, source_target_pairs={{0,2},{1,3},{2,0},{3,1},{4,6},{5,7},{6,4},{7,5},{8,10},{9,11},{10,... | collective-permute-start | bytes 638984 | tf_op jit(solution)/shard_map/ppermute | solution.py:279
  39.2 2.1 %collective-permute-start.4 = (bf16[416,256]{1,0:T(8,128)(2,1)S(1)}, bf16[416,256]{1,0:T(8,128)(2,1)S(1)}, u32[]{:S(2)}, u32[]{:S(2)}) collective-permute-start(bf16[416,256]{1,0:T(8,128)(2,1)S(1)} %turn.1.a0), channel_id=1, source_target_pairs={{0,3},{1,0},{2,1},{3,2},{4,7},{5,4},{6,5},{7,6},{8,11},{9,8},{10,9... | collective-permute-start | bytes 638984 | tf_op jit(solution)/shard_map/ppermute | solution.py:279
  41.3 0.0 collective-permute-done.2.h3
  41.3 0.0 collective-permute-start.3
  41.3 0.0 collective-permute-done.1.h2
  41.3 0.0 collective-permute-done.h1
  41.3 1.4 %prep.1 = (bf16[1024,256]{1,0:T(8,128)(2,1)S(1)}, f32[8,1024]{1,0:T(8,128)S(1)}, f32[8,1024]{1,0:T(8,128)S(1)}, f32[256,128]{1,0:T(8,128)}) custom-call(s32[1]{0:T(128)} %bitcast.first_row, bf16[32,256]{1,0:T(8,128)(2,1)S(1)} %head.1.h0, bf16[32,256]{1,0:T(8,128)(2,1)S(1)} %collective-permute-done.h1, bf16[32,256]{1,0:T(8,128)(2,1)S(1)} %collective-permute-done.1.h2, ...), custom_call_target="tpu_custom_call" | custom-call | flops 99999997952 | bytes 100000000 | tf_op jit(solution)/shard_map/prep/pallas_call | solution.py:285
  42.7 9.3 %all-to-all-start.1 = ((f32[64,4,128]{2,1,0:T(4,128)}), f32[64,4,128]{2,1,0:T(4,128)S(1)}, u32[]{:S(2)}, u32[]{:S(2)}) async-start(f32[64,4,128]{2,1,0:T(4,128)} %bitcast.12), calls=%async_computation.1 | async-start | bytes 262144 | tf_op jit(solution)/shard_map/all_to_all | solution.py:299
  52.0 0.0 collective-permute-done.5.a3
  52.0 0.0 collective-permute-done.4.a2
  52.0 0.0 collective-permute-done.3.a1
  52.0 0.4 spill.1
  52.4 3.5 %collective-permute-start.6 = (bf16[112,256]{1,0:T(8,128)(2,1)S(1)}, bf16[112,256]{1,0:T(8,128)(2,1)S(1)}, u32[]{:S(2)}, u32[]{:S(2)}) collective-permute-start(bf16[112,256]{1,0:T(8,128)(2,1)S(1)} %get-tuple-element.16), channel_id=1, source_target_pairs={{0,4},{4,8},{8,12},{12,16},{16,20},{20,24},{24,28},{28,32},{32,36}... | collective-permute-start | bytes 172040 | tf_op jit(solution)/shard_map/ppermute | solution.py:309
  56.0 1.3 %collective-permute-start.7 = (bf16[112,256]{1,0:T(8,128)(2,1)S(1)}, bf16[112,256]{1,0:T(8,128)(2,1)S(1)}, u32[]{:S(2)}, u32[]{:S(2)}) collective-permute-start(bf16[112,256]{1,0:T(8,128)(2,1)S(1)} %get-tuple-element.17), channel_id=1, source_target_pairs={{1,4},{5,8},{9,12},{13,16},{17,20},{21,24},{25,28},{29,32},{33,36}... | collective-permute-start | bytes 172040 | tf_op jit(solution)/shard_map/ppermute | solution.py:309
  57.3 1.3 %collective-permute-start.8 = (bf16[96,256]{1,0:T(8,128)(2,1)S(1)}, bf16[96,256]{1,0:T(8,128)(2,1)S(1)}, u32[]{:S(2)}, u32[]{:S(2)}) collective-permute-start(bf16[96,256]{1,0:T(8,128)(2,1)S(1)} %get-tuple-element.18), channel_id=1, source_target_pairs={{2,4},{6,8},{10,12},{14,16},{18,20},{22,24},{26,28},{30,32},{34,36... | collective-permute-start | bytes 147464 | tf_op jit(solution)/shard_map/ppermute | solution.py:309
  58.6 1.5 %collective-permute-start.9 = (bf16[96,256]{1,0:T(8,128)(2,1)S(1)}, bf16[96,256]{1,0:T(8,128)(2,1)S(1)}, u32[]{:S(2)}, u32[]{:S(2)}) collective-permute-start(bf16[96,256]{1,0:T(8,128)(2,1)S(1)} %get-tuple-element.19), channel_id=1, source_target_pairs={{3,4},{7,8},{11,12},{15,16},{19,20},{23,24},{27,28},{31,32},{35,36... | collective-permute-start | bytes 147464 | tf_op jit(solution)/shard_map/ppermute | solution.py:309
  60.1 1.9 %grid.1 = f32[416,8,256]{2,1,0:T(8,128)S(1)} custom-call(bf16[416,256]{1,0:T(8,128)(2,1)S(1)} %turn.1.a0, bf16[416,256]{1,0:T(8,128)(2,1)S(1)} %collective-permute-done.3.a1, bf16[416,256]{1,0:T(8,128)(2,1)S(1)} %collective-permute-done.4.a2, bf16[416,256]{1,0:T(8,128)(2,1)S(1)} %collective-permute-done.5.a3, bf16[1024,256]{1,0:T(8,128)(2,1)S(1)} %get-tuple-element.13.colw, ...), custom_call_target="tpu_custom_call" | custom-call | tf_op jit(solution)/shard_map/grid/pallas_call | solution.py:314
  62.0 2.2 %collective-permute-done.8.refs_2_ = bf16[96,256]{1,0:T(8,128)(2,1)S(1)} collective-permute-done((bf16[96,256]{1,0:T(8,128)(2,1)S(1)}, bf16[96,256]{1,0:T(8,128)(2,1)S(1)}, u32[]{:S(2)}, u32[]{:S(2)}) %collective-permute-start.8) | collective-permute-done | bytes 49184 | tf_op jit(solution)/shard_map/ppermute | solution.py:309
  64.2 1.3 %collective-permute-done.9.refs_3_ = bf16[96,256]{1,0:T(8,128)(2,1)S(1)} collective-permute-done((bf16[96,256]{1,0:T(8,128)(2,1)S(1)}, bf16[96,256]{1,0:T(8,128)(2,1)S(1)}, u32[]{:S(2)}, u32[]{:S(2)}) %collective-permute-start.9) | collective-permute-done | bytes 49184 | tf_op jit(solution)/shard_map/ppermute | solution.py:309
  65.5 0.0 collective-permute-done.6.refs_0_
  65.5 0.0 collective-permute-done.7.refs_1_
  65.6 1.9 %join.1 = f32[411,8,256]{2,1,0:T(8,128)} custom-call(f32[416,8,256]{2,1,0:T(8,128)S(1)} %grid.1, bf16[112,256]{1,0:T(8,128)(2,1)S(1)} %collective-permute-done.6.refs_0_, bf16[112,256]{1,0:T(8,128)(2,1)S(1)} %collective-permute-done.7.refs_1_, bf16[96,256]{1,0:T(8,128)(2,1)S(1)} %collective-permute-done.8.refs_2_, ...), custom_call_target="tpu_custom_call" | custom-call | tf_op jit(solution)/shard_map/join/pallas_call | solution.py:322
  67.5 0.0 all-to-all-done.1
  67.5 0.7 %bias.1 = f32[100,128]{1,0:T(8,128)} custom-call(f32[256,128]{1,0:T(8,128)S(1)} %bitcast.17), custom_call_target="tpu_custom_call" | custom-call | tf_op jit(solution)/shard_map/bias/pallas_call | solution.py:332
Async XLA Ops:
  7.2 26.3 %all-to-all-start = ((bf16[64,8,256]{2,1,0:T(8,128)(2,1)}), bf16[64,8,256]{2,1,0:T(8,128)(2,1)S(1)}, u32[]{:S(2)}, u32[]{:S(2)}) async-start(bf16[64,8,256]{2,1,0:T(8,128)(2,1)} %bitcast.20), calls=%async_computation | async-start | bytes 524288 | tf_op jit(solution)/shard_map/all_to_all | solution.py:259
  33.8 7.5 %collective-permute-start.2 = (bf16[32,256]{1,0:T(8,128)(2,1)S(1)}, bf16[32,256]{1,0:T(8,128)(2,1)S(1)}, u32[]{:S(2)}, u32[]{:S(2)}) collective-permute-start(bf16[32,256]{1,0:T(8,128)(2,1)S(1)} %head.1.h0), channel_id=1, source_target_pairs={{0,2},{1,3},{2,0},{3,1},{4,6},{5,7},{6,4},{7,5},{8,10},{9,11},{10,... | collective-permute-start | bytes 49160 | tf_op jit(solution)/shard_map/ppermute | solution.py:279
  36.6 4.7 %collective-permute-start.1 = (bf16[32,256]{1,0:T(8,128)(2,1)S(1)}, bf16[32,256]{1,0:T(8,128)(2,1)S(1)}, u32[]{:S(2)}, u32[]{:S(2)}) collective-permute-start(bf16[32,256]{1,0:T(8,128)(2,1)S(1)} %head.1.h0), channel_id=1, source_target_pairs={{0,3},{1,0},{2,1},{3,2},{4,7},{5,4},{6,5},{7,6},{8,11},{9,8},{10,9... | collective-permute-start | bytes 49160 | tf_op jit(solution)/shard_map/ppermute | solution.py:279
  37.5 3.8 %collective-permute-start = (bf16[32,256]{1,0:T(8,128)(2,1)S(1)}, bf16[32,256]{1,0:T(8,128)(2,1)S(1)}, u32[]{:S(2)}, u32[]{:S(2)}) collective-permute-start(bf16[32,256]{1,0:T(8,128)(2,1)S(1)} %head.1.h0), channel_id=1, source_target_pairs={{0,1},{1,2},{2,3},{3,0},{4,5},{5,6},{6,7},{7,4},{8,9},{9,10},{10,1... | collective-permute-start | bytes 49160 | tf_op jit(solution)/shard_map/ppermute | solution.py:279
  38.5 13.5 %collective-permute-start.5 = (bf16[416,256]{1,0:T(8,128)(2,1)S(1)}, bf16[416,256]{1,0:T(8,128)(2,1)S(1)}, u32[]{:S(2)}, u32[]{:S(2)}) collective-permute-start(bf16[416,256]{1,0:T(8,128)(2,1)S(1)} %turn.1.a0), channel_id=1, source_target_pairs={{0,2},{1,3},{2,0},{3,1},{4,6},{5,7},{6,4},{7,5},{8,10},{9,11},{10,... | collective-permute-start | bytes 638984 | tf_op jit(solution)/shard_map/ppermute | solution.py:279
  39.2 12.8 %collective-permute-start.4 = (bf16[416,256]{1,0:T(8,128)(2,1)S(1)}, bf16[416,256]{1,0:T(8,128)(2,1)S(1)}, u32[]{:S(2)}, u32[]{:S(2)}) collective-permute-start(bf16[416,256]{1,0:T(8,128)(2,1)S(1)} %turn.1.a0), channel_id=1, source_target_pairs={{0,3},{1,0},{2,1},{3,2},{4,7},{5,4},{6,5},{7,6},{8,11},{9,8},{10,9... | collective-permute-start | bytes 638984 | tf_op jit(solution)/shard_map/ppermute | solution.py:279
  41.3 10.8 %collective-permute-start.3 = (bf16[416,256]{1,0:T(8,128)(2,1)S(1)}, bf16[416,256]{1,0:T(8,128)(2,1)S(1)}, u32[]{:S(2)}, u32[]{:S(2)}) collective-permute-start(bf16[416,256]{1,0:T(8,128)(2,1)S(1)} %turn.1.a0), channel_id=1, source_target_pairs={{0,1},{1,2},{2,3},{3,0},{4,5},{5,6},{6,7},{7,4},{8,9},{9,10},{10,1... | collective-permute-start | bytes 638984 | tf_op jit(solution)/shard_map/ppermute | solution.py:279
  42.7 24.8 %all-to-all-start.1 = ((f32[64,4,128]{2,1,0:T(4,128)}), f32[64,4,128]{2,1,0:T(4,128)S(1)}, u32[]{:S(2)}, u32[]{:S(2)}) async-start(f32[64,4,128]{2,1,0:T(4,128)} %bitcast.12), calls=%async_computation.1 | async-start | bytes 262144 | tf_op jit(solution)/shard_map/all_to_all | solution.py:299
  52.4 13.1 %collective-permute-start.6 = (bf16[112,256]{1,0:T(8,128)(2,1)S(1)}, bf16[112,256]{1,0:T(8,128)(2,1)S(1)}, u32[]{:S(2)}, u32[]{:S(2)}) collective-permute-start(bf16[112,256]{1,0:T(8,128)(2,1)S(1)} %get-tuple-element.16), channel_id=1, source_target_pairs={{0,4},{4,8},{8,12},{12,16},{16,20},{20,24},{24,28},{28,32},{32,36}... | collective-permute-start | bytes 172040 | tf_op jit(solution)/shard_map/ppermute | solution.py:309
  56.0 9.6 %collective-permute-start.7 = (bf16[112,256]{1,0:T(8,128)(2,1)S(1)}, bf16[112,256]{1,0:T(8,128)(2,1)S(1)}, u32[]{:S(2)}, u32[]{:S(2)}) collective-permute-start(bf16[112,256]{1,0:T(8,128)(2,1)S(1)} %get-tuple-element.17), channel_id=1, source_target_pairs={{1,4},{5,8},{9,12},{13,16},{17,20},{21,24},{25,28},{29,32},{33,36}... | collective-permute-start | bytes 172040 | tf_op jit(solution)/shard_map/ppermute | solution.py:309
  57.3 6.9 %collective-permute-start.8 = (bf16[96,256]{1,0:T(8,128)(2,1)S(1)}, bf16[96,256]{1,0:T(8,128)(2,1)S(1)}, u32[]{:S(2)}, u32[]{:S(2)}) collective-permute-start(bf16[96,256]{1,0:T(8,128)(2,1)S(1)} %get-tuple-element.18), channel_id=1, source_target_pairs={{2,4},{6,8},{10,12},{14,16},{18,20},{22,24},{26,28},{30,32},{34,36... | collective-permute-start | bytes 147464 | tf_op jit(solution)/shard_map/ppermute | solution.py:309
  58.6 7.0 %collective-permute-start.9 = (bf16[96,256]{1,0:T(8,128)(2,1)S(1)}, bf16[96,256]{1,0:T(8,128)(2,1)S(1)}, u32[]{:S(2)}, u32[]{:S(2)}) collective-permute-start(bf16[96,256]{1,0:T(8,128)(2,1)S(1)} %get-tuple-element.19), channel_id=1, source_target_pairs={{3,4},{7,8},{11,12},{15,16},{19,20},{23,24},{27,28},{31,32},{35,36... | collective-permute-start | bytes 147464 | tf_op jit(solution)/shard_map/ppermute | solution.py:309

commit v5 on v4

--- a/solution.py
+++ b/solution.py
@@ -123,63 +123,45 @@
     return ones_where(r == (q // CAP) * (2 * CAP) + q % CAP + offset)
 
 
-def head_kernel(got, head, *, levels, half):
+def chunk_kernel(got, chunk, *, levels, half):
     slots = got.shape[0] // 2
-    lanes = got[:, WIDE - 128 : WIDE]
-    rest = jnp.transpose(dot(picks(slots, CAP), lanes, NN))
-    at = VROWS - 16 - (LANES - 128)
-    head[0:16, :] = rest[at : at + 16, :].astype(BF16)
-    q, r = iota((8, 2 * slots), 0), iota((8, 2 * slots), 1)
-    pick = ones_where(r % (2 * CAP) == q + CAP)
-    total = dot(pick, lanes, NN)
+    q, r = iota((slots, 2 * slots), 0), iota((slots, 2 * slots), 1)
+    pick = ones_where(r % (2 * CAP) == q % CAP + CAP)
+    total = dot(pick, got[:, WIDE - 128 : WIDE], NN)
     first = levels - (LANES - 128) + 4
-    lane = iota((8, 128), 1)
+    lane = iota((slots, 128), 1)
     kept = 128 - first - half
-    chunk = jnp.where(lane < half, pltpu.roll(total, 128 - first, 1), 0.0)
-    chunk = chunk + jnp.where(lane < kept, pltpu.roll(total, 128 - first - half, 1), 0.0)
-    high = chunk.astype(BF16).astype(F32)
-    head[16:32, 0:128] = jnp.concatenate([high, chunk - high], 0).astype(BF16)
-    head[16:32, 128:slots] = jnp.zeros((16, slots - 128), BF16)
-
-
-def turn_kernel(got, head, out):
+    sums = jnp.where(lane < half, pltpu.roll(total, 128 - first, 1), 0.0)
+    chunk[...] = sums + jnp.where(lane < kept, pltpu.roll(total, 128 - first - half, 1), 0.0)
+
+
+def turn_kernel(got, out):
     slots = got.shape[0] // 2
     out[0:WIDE, :] = jnp.transpose(dot(picks(slots, 0), got[...], NN)).astype(BF16)
     rest = jnp.transpose(dot(picks(slots, CAP), got[...], NN))
-    out[WIDE : VROWS - 16, :] = rest[0 : VROWS - 16 - WIDE, :].astype(BF16)
-    out[VROWS - 16 : VROWS, :] = head[0:16, :]
-
-
-def prep_kernel(first_row, h0, h1, h2, h3, colw, roww, lastw, chunk, *, levels):
-    heads = (h0, h1, h2, h3)
-    part = sum([h[16:32, 0:128].astype(F32) for h in heads])
-    four = (part[0:8, :] + part[8:16, :])[0:CAP, :]
-    eight = jnp.concatenate([four, four], 0)
-    n_rows = chunk.shape[0]
-    chunk[...] = jnp.broadcast_to(eight[None], (n_rows // 8, 8, 128)).reshape(n_rows, 128)
-    tops = jnp.concatenate([h[0:16, :].astype(F32) for h in heads], 1)
+    out[WIDE:VROWS, :] = rest[0 : VROWS - WIDE, :].astype(BF16)
+
+
+def prep_kernel(first_row, a0, a1, a2, a3, spill, colw, roww, *, levels):
+    refs = (a0, a1, a2, a3)
+    tops = jnp.concatenate([ref[VROWS - 16 : VROWS, :].astype(F32) for ref in refs], 1)
     at = levels - (VROWS - 16)
-    fr, cr = tops[at : at + 1, :], tops[at + 2 : at + 3, :]
+    fr, fc = tops[at : at + 1, :], tops[at + 1 : at + 2, :]
+    row, col = tops[at + 2 : at + 3, :].astype(jnp.int32), tops[at + 3 : at + 4, :].astype(jnp.int32)
     n = fr.shape[1]
-    turned = jnp.transpose(tops)
-    fc, cc = turned[:, at + 1 : at + 2], turned[:, at + 3 : at + 4].astype(jnp.int32)
-    cols = iota((n, GC), 1)
-    colw[...] = jnp.where(cols == cc, 1.0 - fc, jnp.where(cols == cc + 1, fc, 0.0)).astype(BF16)
-    row = cr.astype(jnp.int32)
+    cols = iota((GC, n), 0)
+    cw = jnp.where(cols == col, 1.0 - fc, jnp.where(cols == col + 1, fc, 0.0)).astype(BF16)
+    colw[...] = cw
     rel = iota((BLOCK, n), 0) + first_row[0]
     roww[...] = jnp.where(rel == row, 1.0 - fr, 0.0) + jnp.where(rel == row + 1, fr, 0.0)
-    lastw[...] = jnp.broadcast_to(jnp.where(row == GR - 1, fr, 0.0), lastw.shape)
-
-
-def spill_kernel(a0, a1, a2, a3, colw, lastw, *spills):
+    last = jnp.where(row == GR - 1, fr, 0.0)
     part = a0.shape[1]
     out = jnp.zeros((VROWS, GC), F32)
-    for j, ref in enumerate((a0, a1, a2, a3)):
+    for j, ref in enumerate(refs):
         cols = slice(j * part, (j + 1) * part)
-        lhs = (ref[...].astype(F32) * lastw[0:1, cols]).astype(BF16)
-        out = out + dot(lhs, colw[cols, :], NN)
-    for spill, (lo, hi) in zip(spills, PARTS):
-        spill[...] = out[lo:hi, :].astype(BF16)
+        lhs = (ref[...].astype(F32) * last[:, cols]).astype(BF16)
+        out = out + dot(lhs, cw[:, cols], NT)
+    spill[...] = out.astype(BF16)
 
 
 def grid_kernel(a0, a1, a2, a3, colw, roww, out):
@@ -190,17 +172,16 @@
             cols = slice(j * part, (j + 1) * part)
             lhs = ref[lo:hi, :].astype(F32)[:, None, :] * roww[:, cols][None, :, :]
             lhs = lhs.reshape((hi - lo) * BLOCK, part).astype(BF16)
-            total = total + dot(lhs, colw[cols, :], NN)
+            total = total + dot(lhs, colw[:, cols], NT)
         out[lo:hi] = total.reshape(hi - lo, BLOCK, GC)
 
 
-def join_kernel(grid, *refs):
-    spills, out, joined, sems = refs[0 : len(PARTS)], *refs[len(PARTS) :]
+def join_kernel(grid, spill, out, joined, sems):
     levels = out.shape[0]
     copies = []
     for i, (lo, hi) in enumerate(PARTS):
         first = iota((hi - lo, BLOCK, GC), 1) == 0
-        joined[lo:hi] = grid[lo:hi] + jnp.where(first, spills[i][...].astype(F32)[:, None, :], 0.0)
+        joined[lo:hi] = grid[lo:hi] + jnp.where(first, spill[lo:hi, :].astype(F32)[:, None, :], 0.0)
         size = min(hi, levels) - lo
         copies.append(pltpu.make_async_copy(joined.at[pl.ds(lo, size)], out.at[pl.ds(lo, size)], sems.at[i]))
         copies[i].start()
@@ -208,11 +189,15 @@
         copy.wait()
 
 
-def bias_kernel(got, out, *, half, scale):
-    t = jnp.transpose(got[...]) * scale
+def slot_bias_kernel(got, out, *, half):
+    t = jnp.transpose(got[...])
     n = got.shape[0] // 2
     out[0:half, :] = t[0:half, 0:n]
     out[half : 2 * half, :] = t[0:half, n : 2 * n]
+
+
+def bias_kernel(b0, b1, b2, b3, out, *, scale):
+    out[...] = ((b0[...] + b1[...]) + (b2[...] + b3[...])) * scale
 
 
 VM = pl.BlockSpec(memory_space=pltpu.VMEM)
@@ -257,60 +242,44 @@
         name="send",
     )(jnp.transpose(k_matrix, (1, 0, 2)), *small)
     got = lax.all_to_all(send.reshape(n_tile, 2 * CAP, WIDE), "tile", 0, 0, tiled=True).reshape(2 * slots, WIDE)
-    head = pl.pallas_call(
-        functools.partial(head_kernel, levels=levels, half=chans // 2),
-        out_shape=jax.ShapeDtypeStruct((32, slots), BF16),
-        in_specs=[VM],
-        out_specs=VM,
-        compiler_params=params,
-        name="head",
-    )(got)
     turned = pl.pallas_call(
         turn_kernel,
         out_shape=jax.ShapeDtypeStruct((VROWS, slots), BF16),
-        in_specs=[VM, VM],
-        out_specs=VM,
-        compiler_params=params,
-        cost_estimate=pl.CostEstimate(flops=2**30, bytes_accessed=2**22, transcendentals=0),
+        in_specs=[VM],
+        out_specs=VM,
+        compiler_params=params,
         name="turn",
-    )(got, head)
+    )(got)
 
     def around(x):
         return [x] + [lax.ppermute(x, "slot", [(i, (i + d) % n_slot) for i in range(n_slot)]) for d in (1, 3, 2)]
 
-    heads = around(head)
     blocks = around(turned)
+    chunk = pl.pallas_call(
+        functools.partial(chunk_kernel, levels=levels, half=chans // 2),
+        out_shape=jax.ShapeDtypeStruct((slots, 128), F32),
+        in_specs=[VM],
+        out_specs=VM,
+        compiler_params=params,
+        name="chunk",
+    )(got)
+    chunks = lax.all_to_all(chunk.reshape(n_tile, CAP, 128), "tile", 0, 0, tiled=True).reshape(slots, 128)
     total = n_slot * slots
     first_row = (lax.axis_index("slot") * BLOCK).astype(jnp.int32).reshape(1)
-    colw, roww, lastw, chunk = pl.pallas_call(
+    spill, colw, roww = pl.pallas_call(
         functools.partial(prep_kernel, levels=levels),
         out_shape=(
-            jax.ShapeDtypeStruct((total, GC), BF16),
+            jax.ShapeDtypeStruct((VROWS, GC), BF16),
+            jax.ShapeDtypeStruct((GC, total), BF16),
             jax.ShapeDtypeStruct((BLOCK, total), F32),
-            jax.ShapeDtypeStruct((8, total), F32),
-            jax.ShapeDtypeStruct((slots, 128), F32),
         ),
         in_specs=[pl.BlockSpec(memory_space=pltpu.SMEM)] + [VM] * 4,
-        out_specs=(VM,) * 4,
-        compiler_params=params,
-        cost_estimate=pl.CostEstimate(flops=10**11, bytes_accessed=10**8, transcendentals=0),
+        out_specs=(VM,) * 3,
+        compiler_params=params,
         name="prep",
-    )(first_row, *heads)
-    chunks = lax.all_to_all(chunk.reshape(n_tile, CAP, 128), "tile", 0, 0, tiled=True).reshape(slots, 128)
-    spills = pl.pallas_call(
-        spill_kernel,
-        out_shape=tuple(jax.ShapeDtypeStruct((hi - lo, GC), BF16) for lo, hi in PARTS),
-        in_specs=[VM] * 6,
-        out_specs=(VM,) * len(PARTS),
-        compiler_params=params,
-        name="spill",
-    )(*blocks, colw, lastw)
-    arrived = [
-        lax.ppermute(
-            x, ("tile", "slot"), [(t * n_slot + q % n_slot, ((t + 1) % n_tile) * n_slot) for t in range(n_tile)]
-        )
-        for q, x in enumerate(spills)
-    ]
+    )(first_row, *blocks)
+    pairs = [(t * n_slot, ((t + 1) % n_tile) * n_slot) for t in range(n_tile)]
+    arrived = lax.ppermute(spill, ("tile", "slot"), pairs)
     own = pl.pallas_call(
         grid_kernel,
         out_shape=jax.ShapeDtypeStruct((VROWS, BLOCK, GC), F32),
@@ -319,24 +288,33 @@
         compiler_params=params,
         name="grid",
     )(*blocks, colw, roww)
+    slot_bias = pl.pallas_call(
+        functools.partial(slot_bias_kernel, half=chans // 2),
+        out_shape=jax.ShapeDtypeStruct((chans, 128), F32),
+        in_specs=[VM],
+        out_specs=VM,
+        compiler_params=params,
+        name="slot_bias",
+    )(chunks)
+    biases = around(slot_bias)
     grid = pl.pallas_call(
         join_kernel,
         out_shape=jax.ShapeDtypeStruct((levels, BLOCK, GC), F32),
-        in_specs=[VM] * (1 + len(PARTS)),
+        in_specs=[VM] * 2,
         out_specs=HBM,
         scratch_shapes=[pltpu.VMEM((VROWS, BLOCK, GC), F32), pltpu.SemaphoreType.DMA((len(PARTS),))],
         compiler_params=params,
         name="join",
-    )(own, *arrived)
-    chunks, grid = lax.optimization_barrier((chunks, grid))
+    )(own, arrived)
+    *biases, grid = lax.optimization_barrier((*biases, grid))
     bias = pl.pallas_call(
-        functools.partial(bias_kernel, half=chans // 2, scale=1.0 / math.sqrt(obs * n_tile * n_slot)),
+        functools.partial(bias_kernel, scale=1.0 / math.sqrt(obs * n_tile * n_slot)),
         out_shape=jax.ShapeDtypeStruct((chans, 128), F32),
-        in_specs=[VM],
+        in_specs=[VM] * 4,
         out_specs=VM,
         compiler_params=params,
         name="bias",
-    )(chunks)
+    )(*biases)
     return jnp.transpose(grid, (1, 2, 0)), bias
 
 

time: 68.5 us -> 63.8 us (0.931)
  blocking collectives: 0 us -> 26.3 us
  starting transfers between devices: 37.2 us -> 15.7 us
  waiting for transfers between devices: 16.7 us -> 7.74 us
    all_to_all x0 -> x1, blocking collectives: none -> 26.3 us  [per_device(): lax.all_to_all(send.reshape(n_tile, 2 * CAP, WIDE), 'tile', 0, 0, tiled=T...]
    all_to_all x1 -> x0, starting transfers between devices: 13.2 us -> none  [per_device(): lax.all_to_all(send.reshape(n_tile, 2 * CAP, WIDE), 'tile', 0, 0, tiled=T...]
    all_to_all x1 -> x0, waiting for transfers between devices: 13.2 us -> none  [per_device(): lax.all_to_all(send.reshape(n_tile, 2 * CAP, WIDE), 'tile', 0, 0, tiled=T...]
    all_to_all x1, waiting for transfers between devices: 0.01 us -> 5.21 us  [per_device(): lax.all_to_all(chunk.reshape(n_tile, CAP, 128), 'tile', 0, 0, tiled=True)]
    ppermute x4 -> x1, starting transfers between devices: 7.59 us -> 3.1 us  [per_device(): arrived = lax.ppermute(spill, ('tile', 'slot'), pairs)]
    all_to_all x1, starting transfers between devices: 9.33 us -> 5.55 us  [per_device(): lax.all_to_all(chunk.reshape(n_tile, CAP, 128), 'tile', 0, 0, tiled=True)]
    ppermute x4 -> x1, waiting for transfers between devices: 3.54 us -> 0.01 us  [per_device(): arrived = lax.ppermute(spill, ('tile', 'slot'), pairs)]
    ppermute x6, waiting for transfers between devices: 0.02 us -> 2.53 us  [around(): lax.ppermute(x, 'slot', [(i, (i + d) % n_slot) for i in range(n_slot)])]
  transfers between devices with their start and end apart: 12 -> 8, of which waited for: 3 -> 4; matrix products, arithmetic and copies ran while one was open for 0% -> 0% of each run, Pallas kernels for 9% -> 9%
where the time goes in v5:
time: 63.8 us; the launch traced here: 63.6 us
  blocking collectives  26.3 us (41%)
  starting transfers between devices  15.7 us (25%)
  Pallas kernels  13 us (20%)
  waiting for transfers between devices  7.74 us (12%)
  between operations  0.73 us (1%)
    all_to_all x1, blocking collectives, per_device(): lax.all_to_all(send.reshape(n_tile, 2 * CAP, WIDE), 'tile', 0, 0, tiled=T...  26.3 us
    ppermute x6, starting transfers between devices, around(): lax.ppermute(x, 'slot', [(i, (i + d) % n_slot) for i in range(n_slot)])  7.1 us
    pallas_call x1, Pallas kernels, per_device(): pl.pallas_call(functools.partial(send_kernel, steps=steps), out_shape=jax...  6.54 us
    all_to_all x1, starting transfers between devices, per_device(): lax.all_to_all(chunk.reshape(n_tile, CAP, 128), 'tile', 0, 0, tiled=True)  5.55 us
    all_to_all x1, waiting for transfers between devices, per_device(): lax.all_to_all(chunk.reshape(n_tile, CAP, 128), 'tile', 0, 0, tiled=True)  5.21 us
    ppermute x1, starting transfers between devices, per_device(): arrived = lax.ppermute(spill, ('tile', 'slot'), pairs)  3.1 us
    ppermute x6, waiting for transfers between devices, around(): lax.ppermute(x, 'slot', [(i, (i + d) % n_slot) for i in range(n_slot)])  2.53 us
    pallas_call x1, Pallas kernels, per_device(): pl.pallas_call(grid_kernel, out_shape=jax.ShapeDtypeStruct((VROWS, BLOCK,...  1.97 us
  transfers between devices with their start and end apart: 8, of which 4 were waited for; matrix products, arithmetic and copies ran while one was open for 0% of the time, Pallas kernels for 9%

profile of v5, /device:TPU:1, one launch (start us, length us, event | category | flops | bytes accessed | tf_op | source)
XLA Modules:
  0.0 63.6 jit_solution(2187715854945125861)
XLA Ops:
  0.6 6.5 %send.1 = bf16[512,256]{1,0:T(8,128)(2,1)} custom-call(bf16[100,96,411]{2,1,0:T(8,128)(2,1)} %bitcast.18, bf16[96,100]{1,0:T(8,128)(2,1)} %refs_1_.1, f32[1,100]{1,0:T(1,128)} %bitcast.22, s32[1,96]{1,0:T(1,128)} %bitcast.23, bf16[1,96]{1,0:T(2,128)(2,1)} %bitcast.24, bf16[1,96]{1,0:T(2,128)(2,1)} %bitcast.25, s32[1,96]{1,0:T(1,128)} %bitcast.26, ...), custom_call_target="tpu_custom_call" | custom-call | tf_op jit(solution)/shard_map/send/pallas_call | solution.py:229
  7.2 26.3 %all_to_all.10 = bf16[64,8,256]{2,1,0:T(8,128)(2,1)S(1)} all-to-all(bf16[64,8,256]{2,1,0:T(8,128)(2,1)} %bitcast.20), channel_id=1, replica_groups=mesh['tile'=64,'slot'=4] {'tile'}, dimensions={0} | all-to-all | bytes 524288 | tf_op jit(solution)/shard_map/all_to_all | solution.py:244
  33.5 0.4 turn.1.a0
  33.9 2.8 %collective-permute-start.5 = (bf16[416,256]{1,0:T(8,128)(2,1)S(1)}, bf16[416,256]{1,0:T(8,128)(2,1)S(1)}, u32[]{:S(2)}, u32[]{:S(2)}) collective-permute-start(bf16[416,256]{1,0:T(8,128)(2,1)S(1)} %turn.1.a0), channel_id=1, source_target_pairs={{0,2},{1,3},{2,0},{3,1},{4,6},{5,7},{6,4},{7,5},{8,10},{9,11},{10,... | collective-permute-start | bytes 638984 | tf_op jit(solution)/shard_map/ppermute | solution.py:255
  36.7 0.9 %collective-permute-start.4 = (bf16[416,256]{1,0:T(8,128)(2,1)S(1)}, bf16[416,256]{1,0:T(8,128)(2,1)S(1)}, u32[]{:S(2)}, u32[]{:S(2)}) collective-permute-start(bf16[416,256]{1,0:T(8,128)(2,1)S(1)} %turn.1.a0), channel_id=1, source_target_pairs={{0,3},{1,0},{2,1},{3,2},{4,7},{5,4},{6,5},{7,6},{8,11},{9,8},{10,9... | collective-permute-start | bytes 638984 | tf_op jit(solution)/shard_map/ppermute | solution.py:255
  37.6 0.6 collective-permute-start.3
  38.2 1.0 %chunk.1 = f32[256,128]{1,0:T(8,128)} custom-call(bf16[512,256]{1,0:T(8,128)(2,1)S(1)} %bitcast.16), custom_call_target="tpu_custom_call" | custom-call | tf_op jit(solution)/shard_map/chunk/pallas_call | solution.py:258
  39.2 5.5 %all-to-all-start.1 = ((f32[64,4,128]{2,1,0:T(4,128)}), f32[64,4,128]{2,1,0:T(4,128)S(1)}, u32[]{:S(2)}, u32[]{:S(2)}) async-start(f32[64,4,128]{2,1,0:T(4,128)} %bitcast.11), calls=%async_computation.1 | async-start | bytes 262144 | tf_op jit(solution)/shard_map/all_to_all | solution.py:266
  44.7 0.0 collective-permute-done.5.a3
  44.7 2.0 %collective-permute-done.4.a2 = bf16[416,256]{1,0:T(8,128)(2,1)S(1)} collective-permute-done((bf16[416,256]{1,0:T(8,128)(2,1)S(1)}, bf16[416,256]{1,0:T(8,128)(2,1)S(1)}, u32[]{:S(2)}, u32[]{:S(2)}) %collective-permute-start.4) | collective-permute-done | bytes 213024 | tf_op jit(solution)/shard_map/ppermute | solution.py:255
  46.8 0.2 collective-permute-done.3.a1
  47.0 0.5 prep.1
  47.5 3.1 %collective-permute-start.6 = (bf16[416,256]{1,0:T(8,128)(2,1)S(1)}, bf16[416,256]{1,0:T(8,128)(2,1)S(1)}, u32[]{:S(2)}, u32[]{:S(2)}) collective-permute-start(bf16[416,256]{1,0:T(8,128)(2,1)S(1)} %get-tuple-element.12), channel_id=1, source_target_pairs={{0,4},{4,8},{8,12},{12,16},{16,20},{20,24},{24,28},{28,32},{32,36}... | collective-permute-start | bytes 638984 | tf_op jit(solution)/shard_map/ppermute | solution.py:282
  50.6 5.2 %all-to-all-done.1 = f32[64,4,128]{2,1,0:T(4,128)S(1)} async-done(((f32[64,4,128]{2,1,0:T(4,128)}), f32[64,4,128]{2,1,0:T(4,128)S(1)}, u32[]{:S(2)}, u32[]{:S(2)}) %all-to-all-start.1) | async-done | bytes 131104 | tf_op jit(solution)/shard_map/all_to_all | solution.py:266
  55.8 0.1 slot_bias.1.b0
  55.9 0.4 collective-permute-start.2
  56.4 2.4 %collective-permute-start.1 = (f32[100,128]{1,0:T(8,128)S(1)}, f32[100,128]{1,0:T(8,128)S(1)}, u32[]{:S(2)}, u32[]{:S(2)}) collective-permute-start(f32[100,128]{1,0:T(8,128)S(1)} %slot_bias.1.b0), channel_id=1, source_target_pairs={{0,3},{1,0},{2,1},{3,2},{4,7},{5,4},{6,5},{7,6},{8,11},{9,8},{10,9... | collective-permute-start | bytes 153608 | tf_op jit(solution)/shard_map/ppermute | solution.py:255
  58.7 0.0 collective-permute-start
  58.7 2.0 %grid.1 = f32[416,8,256]{2,1,0:T(8,128)S(1)} custom-call(bf16[416,256]{1,0:T(8,128)(2,1)S(1)} %turn.1.a0, bf16[416,256]{1,0:T(8,128)(2,1)S(1)} %collective-permute-done.3.a1, bf16[416,256]{1,0:T(8,128)(2,1)S(1)} %collective-permute-done.4.a2, bf16[416,256]{1,0:T(8,128)(2,1)S(1)} %collective-permute-done.5.a3, bf16[256,1024]{1,0:T(8,128)(2,1)S(1)} %get-tuple-element.10.colw, ...), custom_call_target="tpu_custom_call" | custom-call | tf_op jit(solution)/shard_map/grid/pallas_call | solution.py:283
  60.7 0.0 collective-permute-done.6.spill
  60.7 1.9 %join.1 = f32[411,8,256]{2,1,0:T(8,128)} custom-call(f32[416,8,256]{2,1,0:T(8,128)S(1)} %grid.1, bf16[416,256]{1,0:T(8,128)(2,1)S(1)} %collective-permute-done.6.spill), custom_call_target="tpu_custom_call" | custom-call | tf_op jit(solution)/shard_map/join/pallas_call | solution.py:300
  62.6 0.0 collective-permute-done.2.b3
  62.6 0.0 collective-permute-done.1.b2
  62.6 0.3 collective-permute-done.b1
  62.9 0.6 %bias.1 = f32[100,128]{1,0:T(8,128)} custom-call(f32[100,128]{1,0:T(8,128)S(1)} %slot_bias.1.b0, f32[100,128]{1,0:T(8,128)S(1)} %collective-permute-done.b1, f32[100,128]{1,0:T(8,128)S(1)} %collective-permute-done.1.b2, f32[100,128]{1,0:T(8,128)S(1)} %collective-permute-done.2.b3), custom_call_target="tpu_custom_call" | custom-call | tf_op jit(solution)/shard_map/bias/pallas_call | solution.py:310
Async XLA Ops:
  33.9 10.8 %collective-permute-start.5 = (bf16[416,256]{1,0:T(8,128)(2,1)S(1)}, bf16[416,256]{1,0:T(8,128)(2,1)S(1)}, u32[]{:S(2)}, u32[]{:S(2)}) collective-permute-start(bf16[416,256]{1,0:T(8,128)(2,1)S(1)} %turn.1.a0), channel_id=1, source_target_pairs={{0,2},{1,3},{2,0},{3,1},{4,6},{5,7},{6,4},{7,5},{8,10},{9,11},{10,... | collective-permute-start | bytes 638984 | tf_op jit(solution)/shard_map/ppermute | solution.py:255
  36.7 10.0 %collective-permute-start.4 = (bf16[416,256]{1,0:T(8,128)(2,1)S(1)}, bf16[416,256]{1,0:T(8,128)(2,1)S(1)}, u32[]{:S(2)}, u32[]{:S(2)}) collective-permute-start(bf16[416,256]{1,0:T(8,128)(2,1)S(1)} %turn.1.a0), channel_id=1, source_target_pairs={{0,3},{1,0},{2,1},{3,2},{4,7},{5,4},{6,5},{7,6},{8,11},{9,8},{10,9... | collective-permute-start | bytes 638984 | tf_op jit(solution)/shard_map/ppermute | solution.py:255
  37.6 9.4 %collective-permute-start.3 = (bf16[416,256]{1,0:T(8,128)(2,1)S(1)}, bf16[416,256]{1,0:T(8,128)(2,1)S(1)}, u32[]{:S(2)}, u32[]{:S(2)}) collective-permute-start(bf16[416,256]{1,0:T(8,128)(2,1)S(1)} %turn.1.a0), channel_id=1, source_target_pairs={{0,1},{1,2},{2,3},{3,0},{4,5},{5,6},{6,7},{7,4},{8,9},{9,10},{10,1... | collective-permute-start | bytes 638984 | tf_op jit(solution)/shard_map/ppermute | solution.py:255
  39.2 16.7 %all-to-all-start.1 = ((f32[64,4,128]{2,1,0:T(4,128)}), f32[64,4,128]{2,1,0:T(4,128)S(1)}, u32[]{:S(2)}, u32[]{:S(2)}) async-start(f32[64,4,128]{2,1,0:T(4,128)} %bitcast.11), calls=%async_computation.1 | async-start | bytes 262144 | tf_op jit(solution)/shard_map/all_to_all | solution.py:266
  47.5 13.2 %collective-permute-start.6 = (bf16[416,256]{1,0:T(8,128)(2,1)S(1)}, bf16[416,256]{1,0:T(8,128)(2,1)S(1)}, u32[]{:S(2)}, u32[]{:S(2)}) collective-permute-start(bf16[416,256]{1,0:T(8,128)(2,1)S(1)} %get-tuple-element.12), channel_id=1, source_target_pairs={{0,4},{4,8},{8,12},{12,16},{16,20},{20,24},{24,28},{28,32},{32,36}... | collective-permute-start | bytes 638984 | tf_op jit(solution)/shard_map/ppermute | solution.py:282
  55.9 6.7 %collective-permute-start.2 = (f32[100,128]{1,0:T(8,128)S(1)}, f32[100,128]{1,0:T(8,128)S(1)}, u32[]{:S(2)}, u32[]{:S(2)}) collective-permute-start(f32[100,128]{1,0:T(8,128)S(1)} %slot_bias.1.b0), channel_id=1, source_target_pairs={{0,2},{1,3},{2,0},{3,1},{4,6},{5,7},{6,4},{7,5},{8,10},{9,11},{10,... | collective-permute-start | bytes 153608 | tf_op jit(solution)/shard_map/ppermute | solution.py:255
  56.4 6.3 %collective-permute-start.1 = (f32[100,128]{1,0:T(8,128)S(1)}, f32[100,128]{1,0:T(8,128)S(1)}, u32[]{:S(2)}, u32[]{:S(2)}) collective-permute-start(f32[100,128]{1,0:T(8,128)S(1)} %slot_bias.1.b0), channel_id=1, source_target_pairs={{0,3},{1,0},{2,1},{3,2},{4,7},{5,4},{6,5},{7,6},{8,11},{9,8},{10,9... | collective-permute-start | bytes 153608 | tf_op jit(solution)/shard_map/ppermute | solution.py:255
  58.7 4.2 %collective-permute-start = (f32[100,128]{1,0:T(8,128)S(1)}, f32[100,128]{1,0:T(8,128)S(1)}, u32[]{:S(2)}, u32[]{:S(2)}) collective-permute-start(f32[100,128]{1,0:T(8,128)S(1)} %slot_bias.1.b0), channel_id=1, source_target_pairs={{0,1},{1,2},{2,3},{3,0},{4,5},{5,6},{6,7},{7,4},{8,9},{9,10},{10,1... | collective-permute-start | bytes 153608 | tf_op jit(solution)/shard_map/ppermute | solution.py:255

commit v6 on v5

--- a/solution.py
+++ b/solution.py
@@ -288,6 +288,7 @@
         compiler_params=params,
         name="grid",
     )(*blocks, colw, roww)
+    own, chunks = lax.optimization_barrier((own, chunks))
     slot_bias = pl.pallas_call(
         functools.partial(slot_bias_kernel, half=chans // 2),
         out_shape=jax.ShapeDtypeStruct((chans, 128), F32),

time: 63.8 us -> 66 us (1.034)
  local copies, waits for them, and re-layouts: 0 us -> 3.74 us
  waiting for transfers between devices: 7.74 us -> 4.2 us
  Pallas kernels: 13 us -> 14.7 us
    all_to_all x1, waiting for transfers between devices: 5.21 us -> 0.01 us  [per_device(): lax.all_to_all(chunk.reshape(n_tile, CAP, 128), 'tile', 0, 0, tiled=True)]
    unnamed x0 -> x16, local copies, waits for them, and re-layouts: none -> 3.74 us
    ppermute x6, waiting for transfers between devices: 2.53 us -> 4.19 us  [around(): lax.ppermute(x, 'slot', [(i, (i + d) % n_slot) for i in range(n_slot)])]
    pallas_call x1, Pallas kernels: 1.89 us -> 2.82 us  [per_device(): pl.pallas_call(join_kernel, out_shape=jax.ShapeDtypeStruct((levels, BLOCK...]
    pallas_call x1, Pallas kernels: 0.55 us -> 1.24 us  [per_device(): pl.pallas_call(functools.partial(prep_kernel, levels=levels), out_shape=(...]
  transfers between devices with their start and end apart: 8 -> 8, of which waited for: 4 -> 2; matrix products, arithmetic and copies ran while one was open for 0% -> 0% of each run, Pallas kernels for 9% -> 11%
where the time goes in v6:
time: 66 us; the launch traced here: 65.6 us
  blocking collectives  26.3 us (40%)
  starting transfers between devices  15.9 us (24%)
  Pallas kernels  14.7 us (22%)
  waiting for transfers between devices  4.2 us (6%)
  local copies, waits for them, and re-layouts  3.74 us (6%)
  between operations  0.81 us (1%)
    all_to_all x1, blocking collectives, per_device(): lax.all_to_all(send.reshape(n_tile, 2 * CAP, WIDE), 'tile', 0, 0, tiled=T...  26.3 us
    ppermute x6, starting transfers between devices, around(): lax.ppermute(x, 'slot', [(i, (i + d) % n_slot) for i in range(n_slot)])  7.03 us
    pallas_call x1, Pallas kernels, per_device(): pl.pallas_call(functools.partial(send_kernel, steps=steps), out_shape=jax...  6.54 us
    all_to_all x1, starting transfers between devices, per_device(): lax.all_to_all(chunk.reshape(n_tile, CAP, 128), 'tile', 0, 0, tiled=True)  5.55 us
    ppermute x6, waiting for transfers between devices, around(): lax.ppermute(x, 'slot', [(i, (i + d) % n_slot) for i in range(n_slot)])  4.19 us
    unnamed x16, local copies, waits for them, and re-layouts  3.74 us
    ppermute x1, starting transfers between devices, per_device(): arrived = lax.ppermute(spill, ('tile', 'slot'), pairs)  3.3 us
    pallas_call x1, Pallas kernels, per_device(): pl.pallas_call(join_kernel, out_shape=jax.ShapeDtypeStruct((levels, BLOCK...  2.82 us
  transfers between devices with their start and end apart: 8, of which 2 were waited for; matrix products, arithmetic and copies ran while one was open for 0% of the time, Pallas kernels for 11%

profile of v6, /device:TPU:1, one launch (start us, length us, event | category | flops | bytes accessed | tf_op | source)
XLA Modules:
  0.0 65.6 jit_solution(248706840301697474)
XLA Ops:
  0.6 6.5 %send.1 = bf16[512,256]{1,0:T(8,128)(2,1)} custom-call(bf16[100,96,411]{2,1,0:T(8,128)(2,1)} %bitcast.18, bf16[96,100]{1,0:T(8,128)(2,1)} %refs_1_.1, f32[1,100]{1,0:T(1,128)} %bitcast.22, s32[1,96]{1,0:T(1,128)} %bitcast.23, bf16[1,96]{1,0:T(2,128)(2,1)} %bitcast.24, bf16[1,96]{1,0:T(2,128)(2,1)} %bitcast.25, s32[1,96]{1,0:T(1,128)} %bitcast.26, ...), custom_call_target="tpu_custom_call" | custom-call | tf_op jit(solution)/shard_map/send/pallas_call | solution.py:229
  7.2 26.3 %all_to_all.10 = bf16[64,8,256]{2,1,0:T(8,128)(2,1)S(1)} all-to-all(bf16[64,8,256]{2,1,0:T(8,128)(2,1)} %bitcast.20), channel_id=1, replica_groups=mesh['tile'=64,'slot'=4] {'tile'}, dimensions={0} | all-to-all | bytes 524288 | tf_op jit(solution)/shard_map/all_to_all | solution.py:244
  33.5 0.4 turn.1.a0
  33.9 0.0 copy-start
  33.9 1.3 %collective-permute-start = (bf16[416,256]{1,0:T(8,128)(2,1)S(1)}, bf16[416,256]{1,0:T(8,128)(2,1)S(1)}, u32[]{:S(2)}, u32[]{:S(2)}) collective-permute-start(bf16[416,256]{1,0:T(8,128)(2,1)S(1)} %turn.1.a0), channel_id=1, source_target_pairs={{0,1},{1,2},{2,3},{3,0},{4,5},{5,6},{6,7},{7,4},{8,9},{9,10},{10,1... | collective-permute-start | bytes 638984 | tf_op jit(solution)/shard_map/ppermute | solution.py:255
  35.2 1.5 %collective-permute-start.1 = (bf16[416,256]{1,0:T(8,128)(2,1)S(1)}, bf16[416,256]{1,0:T(8,128)(2,1)S(1)}, u32[]{:S(2)}, u32[]{:S(2)}) collective-permute-start(bf16[416,256]{1,0:T(8,128)(2,1)S(1)} %turn.1.a0), channel_id=1, source_target_pairs={{0,3},{1,0},{2,1},{3,2},{4,7},{5,4},{6,5},{7,6},{8,11},{9,8},{10,9... | collective-permute-start | bytes 638984 | tf_op jit(solution)/shard_map/ppermute | solution.py:255
  36.7 1.5 %collective-permute-start.2 = (bf16[416,256]{1,0:T(8,128)(2,1)S(1)}, bf16[416,256]{1,0:T(8,128)(2,1)S(1)}, u32[]{:S(2)}, u32[]{:S(2)}) collective-permute-start(bf16[416,256]{1,0:T(8,128)(2,1)S(1)} %turn.1.a0), channel_id=1, source_target_pairs={{0,2},{1,3},{2,0},{3,1},{4,6},{5,7},{6,4},{7,5},{8,10},{9,11},{10,... | collective-permute-start | bytes 638984 | tf_op jit(solution)/shard_map/ppermute | solution.py:255
  38.2 1.0 %chunk.1 = f32[256,128]{1,0:T(8,128)} custom-call(bf16[512,256]{1,0:T(8,128)(2,1)S(1)} %bitcast.16), custom_call_target="tpu_custom_call" | custom-call | tf_op jit(solution)/shard_map/chunk/pallas_call | solution.py:258
  39.2 5.6 %all-to-all-start.1 = ((f32[64,4,128]{2,1,0:T(4,128)}), f32[64,4,128]{2,1,0:T(4,128)S(1)}, u32[]{:S(2)}, u32[]{:S(2)}) async-start(f32[64,4,128]{2,1,0:T(4,128)} %bitcast.12), calls=%async_computation.1 | async-start | bytes 262144 | tf_op jit(solution)/shard_map/all_to_all | solution.py:266
  44.7 0.0 collective-permute-done.a1
  44.8 0.0 collective-permute-done.1.a2
  44.8 0.0 copy-start.4
  44.8 2.5 %collective-permute-done.2.a3 = bf16[416,256]{1,0:T(8,128)(2,1)S(1)} collective-permute-done((bf16[416,256]{1,0:T(8,128)(2,1)S(1)}, bf16[416,256]{1,0:T(8,128)(2,1)S(1)}, u32[]{:S(2)}, u32[]{:S(2)}) %collective-permute-start.2) | collective-permute-done | bytes 213024 | tf_op jit(solution)/shard_map/ppermute | solution.py:255
  47.3 1.2 %prep.1 = (bf16[416,256]{1,0:T(8,128)(2,1)}, bf16[256,1024]{1,0:T(8,128)(2,1)S(1)}, f32[8,1024]{1,0:T(8,128)S(1)}) custom-call(s32[1]{0:T(128)} %bitcast.11.first_row, bf16[416,256]{1,0:T(8,128)(2,1)S(1)} %turn.1.a0, bf16[416,256]{1,0:T(8,128)(2,1)S(1)} %collective-permute-done.a1, bf16[416,256]{1,0:T(8,128)(2,1)S(1)} %collective-permute-done.1.a2, ...), custom_call_target="tpu_custom_call" | custom-call | tf_op jit(solution)/shard_map/prep/pallas_call | solution.py:269
  48.6 3.3 %collective-permute-start.6 = (bf16[416,256]{1,0:T(8,128)(2,1)}, bf16[416,256]{1,0:T(8,128)(2,1)}, u32[]{:S(2)}, u32[]{:S(2)}) collective-permute-start(bf16[416,256]{1,0:T(8,128)(2,1)} %get-tuple-element.16), channel_id=1, source_target_pairs={{0,4},{4,8},{8,12},{12,16},{16,20},{20,24},{24,28},{28,32},{32,36}... | collective-permute-start | bytes 638984 | tf_op jit(solution)/shard_map/ppermute | solution.py:282
  51.9 0.0 copy-start.1
  51.9 0.9 %copy-done.1 = bf16[416,256]{1,0:T(8,128)(2,1)S(1)} copy-done((bf16[416,256]{1,0:T(8,128)(2,1)S(1)}, bf16[416,256]{1,0:T(8,128)(2,1)}, u32[]{:S(2)}) %copy-start.1) | copy-done | bytes 213016
  52.9 0.9 %copy-done.3 = bf16[416,256]{1,0:T(8,128)(2,1)S(1)} copy-done((bf16[416,256]{1,0:T(8,128)(2,1)S(1)}, bf16[416,256]{1,0:T(8,128)(2,1)}, u32[]{:S(2)}) %copy-start.3) | copy-done | bytes 213016
  53.8 0.9 %copy-done.5 = bf16[416,256]{1,0:T(8,128)(2,1)S(1)} copy-done((bf16[416,256]{1,0:T(8,128)(2,1)S(1)}, bf16[416,256]{1,0:T(8,128)(2,1)}, u32[]{:S(2)}) %copy-start.5) | copy-done | bytes 213016
  54.7 0.9 %copy-done.7 = bf16[416,256]{1,0:T(8,128)(2,1)S(1)} copy-done((bf16[416,256]{1,0:T(8,128)(2,1)S(1)}, bf16[416,256]{1,0:T(8,128)(2,1)}, u32[]{:S(2)}) %copy-start.7) | copy-done | bytes 213016
  55.7 2.0 %grid.1 = f32[416,8,256]{2,1,0:T(8,128)S(1)} custom-call(bf16[416,256]{1,0:T(8,128)(2,1)S(1)} %copy-done.1, bf16[416,256]{1,0:T(8,128)(2,1)S(1)} %copy-done.3, bf16[416,256]{1,0:T(8,128)(2,1)S(1)} %copy-done.5, bf16[416,256]{1,0:T(8,128)(2,1)S(1)} %copy-done.7, bf16[256,1024]{1,0:T(8,128)(2,1)S(1)} %get-tuple-element.12.colw, ...), custom_call_target="tpu_custom_call" | custom-call | tf_op jit(solution)/shard_map/grid/pallas_call | solution.py:283
  57.6 0.0 all-to-all-done.1
  57.7 0.1 slot_bias.1.b0
  57.7 0.1 collective-permute-start.3
  57.8 2.7 %collective-permute-start.4 = (f32[100,128]{1,0:T(8,128)S(1)}, f32[100,128]{1,0:T(8,128)S(1)}, u32[]{:S(2)}, u32[]{:S(2)}) collective-permute-start(f32[100,128]{1,0:T(8,128)S(1)} %slot_bias.1.b0), channel_id=1, source_target_pairs={{0,3},{1,0},{2,1},{3,2},{4,7},{5,4},{6,5},{7,6},{8,11},{9,8},{10,9... | collective-permute-start | bytes 153608 | tf_op jit(solution)/shard_map/ppermute | solution.py:255
  60.5 0.0 collective-permute-start.5
  60.5 0.0 collective-permute-done.6.spill
  60.5 2.8 %join.1 = f32[411,8,256]{2,1,0:T(8,128)} custom-call(f32[416,8,256]{2,1,0:T(8,128)S(1)} %grid.1, bf16[416,256]{1,0:T(8,128)(2,1)} %collective-permute-done.6.spill), custom_call_target="tpu_custom_call" | custom-call | tf_op jit(solution)/shard_map/join/pallas_call | solution.py:301
  63.3 0.0 collective-permute-done.3.b1
  63.3 0.0 collective-permute-done.4.b2
  63.3 1.6 %collective-permute-done.5.b3 = f32[100,128]{1,0:T(8,128)S(1)} collective-permute-done((f32[100,128]{1,0:T(8,128)S(1)}, f32[100,128]{1,0:T(8,128)S(1)}, u32[]{:S(2)}, u32[]{:S(2)}) %collective-permute-start.5) | collective-permute-done | bytes 51232 | tf_op jit(solution)/shard_map/ppermute | solution.py:255
  65.0 0.6 bias.1
  (9 shorter events, 0.0 us)
Async XLA Ops:
  33.9 18.0 %copy-start = (bf16[416,256]{1,0:T(8,128)(2,1)}, bf16[416,256]{1,0:T(8,128)(2,1)S(1)}, u32[]{:S(2)}) copy-start(bf16[416,256]{1,0:T(8,128)(2,1)S(1)} %turn.1.a0) | copy-start | bytes 638980
  33.9 10.8 %collective-permute-start = (bf16[416,256]{1,0:T(8,128)(2,1)S(1)}, bf16[416,256]{1,0:T(8,128)(2,1)S(1)}, u32[]{:S(2)}, u32[]{:S(2)}) collective-permute-start(bf16[416,256]{1,0:T(8,128)(2,1)S(1)} %turn.1.a0), channel_id=1, source_target_pairs={{0,1},{1,2},{2,3},{3,0},{4,5},{5,6},{6,7},{7,4},{8,9},{9,10},{10,1... | collective-permute-start | bytes 638984 | tf_op jit(solution)/shard_map/ppermute | solution.py:255
  35.2 9.6 %collective-permute-start.1 = (bf16[416,256]{1,0:T(8,128)(2,1)S(1)}, bf16[416,256]{1,0:T(8,128)(2,1)S(1)}, u32[]{:S(2)}, u32[]{:S(2)}) collective-permute-start(bf16[416,256]{1,0:T(8,128)(2,1)S(1)} %turn.1.a0), channel_id=1, source_target_pairs={{0,3},{1,0},{2,1},{3,2},{4,7},{5,4},{6,5},{7,6},{8,11},{9,8},{10,9... | collective-permute-start | bytes 638984 | tf_op jit(solution)/shard_map/ppermute | solution.py:255
  36.7 10.7 %collective-permute-start.2 = (bf16[416,256]{1,0:T(8,128)(2,1)S(1)}, bf16[416,256]{1,0:T(8,128)(2,1)S(1)}, u32[]{:S(2)}, u32[]{:S(2)}) collective-permute-start(bf16[416,256]{1,0:T(8,128)(2,1)S(1)} %turn.1.a0), channel_id=1, source_target_pairs={{0,2},{1,3},{2,0},{3,1},{4,6},{5,7},{6,4},{7,5},{8,10},{9,11},{10,... | collective-permute-start | bytes 638984 | tf_op jit(solution)/shard_map/ppermute | solution.py:255
  39.2 18.5 %all-to-all-start.1 = ((f32[64,4,128]{2,1,0:T(4,128)}), f32[64,4,128]{2,1,0:T(4,128)S(1)}, u32[]{:S(2)}, u32[]{:S(2)}) async-start(f32[64,4,128]{2,1,0:T(4,128)} %bitcast.12), calls=%async_computation.1 | async-start | bytes 262144 | tf_op jit(solution)/shard_map/all_to_all | solution.py:266
  44.8 7.1 %copy-start.2 = (bf16[416,256]{1,0:T(8,128)(2,1)}, bf16[416,256]{1,0:T(8,128)(2,1)S(1)}, u32[]{:S(2)}) copy-start(bf16[416,256]{1,0:T(8,128)(2,1)S(1)} %collective-permute-done.a1) | copy-start | bytes 638980
  44.8 7.1 %copy-start.4 = (bf16[416,256]{1,0:T(8,128)(2,1)}, bf16[416,256]{1,0:T(8,128)(2,1)S(1)}, u32[]{:S(2)}) copy-start(bf16[416,256]{1,0:T(8,128)(2,1)S(1)} %collective-permute-done.1.a2) | copy-start | bytes 638980
  47.3 4.6 %copy-start.6 = (bf16[416,256]{1,0:T(8,128)(2,1)}, bf16[416,256]{1,0:T(8,128)(2,1)S(1)}, u32[]{:S(2)}) copy-start(bf16[416,256]{1,0:T(8,128)(2,1)S(1)} %collective-permute-done.2.a3) | copy-start | bytes 638980
  48.6 11.9 %collective-permute-start.6 = (bf16[416,256]{1,0:T(8,128)(2,1)}, bf16[416,256]{1,0:T(8,128)(2,1)}, u32[]{:S(2)}, u32[]{:S(2)}) collective-permute-start(bf16[416,256]{1,0:T(8,128)(2,1)} %get-tuple-element.16), channel_id=1, source_target_pairs={{0,4},{4,8},{8,12},{12,16},{16,20},{20,24},{24,28},{28,32},{32,36}... | collective-permute-start | bytes 638984 | tf_op jit(solution)/shard_map/ppermute | solution.py:282
  51.9 0.9 %copy-start.1 = (bf16[416,256]{1,0:T(8,128)(2,1)S(1)}, bf16[416,256]{1,0:T(8,128)(2,1)}, u32[]{:S(2)}) copy-start(bf16[416,256]{1,0:T(8,128)(2,1)} %copy-done) | copy-start | bytes 638980
  52.9 0.9 %copy-start.3 = (bf16[416,256]{1,0:T(8,128)(2,1)S(1)}, bf16[416,256]{1,0:T(8,128)(2,1)}, u32[]{:S(2)}) copy-start(bf16[416,256]{1,0:T(8,128)(2,1)} %copy-done.2) | copy-start | bytes 638980
  53.8 0.9 %copy-start.5 = (bf16[416,256]{1,0:T(8,128)(2,1)S(1)}, bf16[416,256]{1,0:T(8,128)(2,1)}, u32[]{:S(2)}) copy-start(bf16[416,256]{1,0:T(8,128)(2,1)} %copy-done.4) | copy-start | bytes 638980
  54.7 0.9 %copy-start.7 = (bf16[416,256]{1,0:T(8,128)(2,1)S(1)}, bf16[416,256]{1,0:T(8,128)(2,1)}, u32[]{:S(2)}) copy-start(bf16[416,256]{1,0:T(8,128)(2,1)} %copy-done.6) | copy-start | bytes 638980
  57.7 5.6 %collective-permute-start.3 = (f32[100,128]{1,0:T(8,128)S(1)}, f32[100,128]{1,0:T(8,128)S(1)}, u32[]{:S(2)}, u32[]{:S(2)}) collective-permute-start(f32[100,128]{1,0:T(8,128)S(1)} %slot_bias.1.b0), channel_id=1, source_target_pairs={{0,1},{1,2},{2,3},{3,0},{4,5},{5,6},{6,7},{7,4},{8,9},{9,10},{10,1... | collective-permute-start | bytes 153608 | tf_op jit(solution)/shard_map/ppermute | solution.py:255
  57.8 5.5 %collective-permute-start.4 = (f32[100,128]{1,0:T(8,128)S(1)}, f32[100,128]{1,0:T(8,128)S(1)}, u32[]{:S(2)}, u32[]{:S(2)}) collective-permute-start(f32[100,128]{1,0:T(8,128)S(1)} %slot_bias.1.b0), channel_id=1, source_target_pairs={{0,3},{1,0},{2,1},{3,2},{4,7},{5,4},{6,5},{7,6},{8,11},{9,8},{10,9... | collective-permute-start | bytes 153608 | tf_op jit(solution)/shard_map/ppermute | solution.py:255
  60.5 4.5 %collective-permute-start.5 = (f32[100,128]{1,0:T(8,128)S(1)}, f32[100,128]{1,0:T(8,128)S(1)}, u32[]{:S(2)}, u32[]{:S(2)}) collective-permute-start(f32[100,128]{1,0:T(8,128)S(1)} %slot_bias.1.b0), channel_id=1, source_target_pairs={{0,2},{1,3},{2,0},{3,1},{4,6},{5,7},{6,4},{7,5},{8,10},{9,11},{10,... | collective-permute-start | bytes 153608 | tf_op jit(solution)/shard_map/ppermute | solution.py:255

commit v7 on v6

--- a/solution.py
+++ b/solution.py
@@ -19,7 +19,8 @@
 LANES = 512
 WIDE = LANES // 2
 VROWS = 416
-PARTS = ((0, 112), (112, 224), (224, 320), (320, 416))
+PARTS = ((0, 128), (128, 256), (256, 336), (336, 416))
+EARLY = 2
 BLOCK = 8
 VMEM = 24 * 1024 * 1024
 
@@ -142,7 +143,7 @@
     out[WIDE:VROWS, :] = rest[0 : VROWS - WIDE, :].astype(BF16)
 
 
-def prep_kernel(first_row, a0, a1, a2, a3, spill, colw, roww, *, levels):
+def prep_kernel(first_row, a0, a1, a2, a3, spill, colw, roww, early, late, *, levels):
     refs = (a0, a1, a2, a3)
     tops = jnp.concatenate([ref[VROWS - 16 : VROWS, :].astype(F32) for ref in refs], 1)
     at = levels - (VROWS - 16)
@@ -159,29 +160,31 @@
     out = jnp.zeros((VROWS, GC), F32)
     for j, ref in enumerate(refs):
         cols = slice(j * part, (j + 1) * part)
+        early[:, cols] = ref[0 : early.shape[0], :]
+        late[:, cols] = ref[early.shape[0] : VROWS, :]
         lhs = (ref[...].astype(F32) * last[:, cols]).astype(BF16)
         out = out + dot(lhs, cw[:, cols], NT)
     spill[...] = out.astype(BF16)
 
 
-def grid_kernel(a0, a1, a2, a3, colw, roww, out):
-    part = a0.shape[1]
-    for lo, hi in PARTS:
-        total = jnp.zeros(((hi - lo) * BLOCK, GC), F32)
-        for j, ref in enumerate((a0, a1, a2, a3)):
-            cols = slice(j * part, (j + 1) * part)
-            lhs = ref[lo:hi, :].astype(F32)[:, None, :] * roww[:, cols][None, :, :]
-            lhs = lhs.reshape((hi - lo) * BLOCK, part).astype(BF16)
-            total = total + dot(lhs, colw[:, cols], NT)
-        out[lo:hi] = total.reshape(hi - lo, BLOCK, GC)
-
-
-def join_kernel(grid, spill, out, joined, sems):
+def grid_part(rows, colw, roww, lo, hi):
+    lhs = rows[lo:hi, :].astype(F32)[:, None, :] * roww[...][None, :, :]
+    lhs = lhs.reshape((hi - lo) * BLOCK, rows.shape[1]).astype(BF16)
+    return dot(lhs, colw[...], NT).reshape(hi - lo, BLOCK, GC)
+
+
+def grid_kernel(rows, colw, roww, out):
+    for lo, hi in PARTS[:EARLY]:
+        out[lo:hi] = grid_part(rows, colw, roww, lo, hi)
+
+
+def join_kernel(grid, rows, colw, roww, spill, out, joined, sems):
     levels = out.shape[0]
     copies = []
     for i, (lo, hi) in enumerate(PARTS):
         first = iota((hi - lo, BLOCK, GC), 1) == 0
-        joined[lo:hi] = grid[lo:hi] + jnp.where(first, spill[lo:hi, :].astype(F32)[:, None, :], 0.0)
+        own = grid[lo:hi] if i < EARLY else grid_part(rows, colw, roww, lo - PARTS[EARLY][0], hi - PARTS[EARLY][0])
+        joined[lo:hi] = own + jnp.where(first, spill[lo:hi, :].astype(F32)[:, None, :], 0.0)
         size = min(hi, levels) - lo
         copies.append(pltpu.make_async_copy(joined.at[pl.ds(lo, size)], out.at[pl.ds(lo, size)], sems.at[i]))
         copies[i].start()
@@ -265,16 +268,19 @@
     )(got)
     chunks = lax.all_to_all(chunk.reshape(n_tile, CAP, 128), "tile", 0, 0, tiled=True).reshape(slots, 128)
     total = n_slot * slots
+    split = PARTS[EARLY][0]
     first_row = (lax.axis_index("slot") * BLOCK).astype(jnp.int32).reshape(1)
-    spill, colw, roww = pl.pallas_call(
+    spill, colw, roww, early, late = pl.pallas_call(
         functools.partial(prep_kernel, levels=levels),
         out_shape=(
             jax.ShapeDtypeStruct((VROWS, GC), BF16),
             jax.ShapeDtypeStruct((GC, total), BF16),
             jax.ShapeDtypeStruct((BLOCK, total), F32),
+            jax.ShapeDtypeStruct((split, total), BF16),
+            jax.ShapeDtypeStruct((VROWS - split, total), BF16),
         ),
         in_specs=[pl.BlockSpec(memory_space=pltpu.SMEM)] + [VM] * 4,
-        out_specs=(VM,) * 3,
+        out_specs=(VM,) * 5,
         compiler_params=params,
         name="prep",
     )(first_row, *blocks)
@@ -282,12 +288,12 @@
     arrived = lax.ppermute(spill, ("tile", "slot"), pairs)
     own = pl.pallas_call(
         grid_kernel,
-        out_shape=jax.ShapeDtypeStruct((VROWS, BLOCK, GC), F32),
-        in_specs=[VM] * 6,
+        out_shape=jax.ShapeDtypeStruct((split, BLOCK, GC), F32),
+        in_specs=[VM] * 3,
         out_specs=VM,
         compiler_params=params,
         name="grid",
-    )(*blocks, colw, roww)
+    )(early, colw, roww)
     own, chunks = lax.optimization_barrier((own, chunks))
     slot_bias = pl.pallas_call(
         functools.partial(slot_bias_kernel, half=chans // 2),
@@ -301,12 +307,12 @@
     grid = pl.pallas_call(
         join_kernel,
         out_shape=jax.ShapeDtypeStruct((levels, BLOCK, GC), F32),
-        in_specs=[VM] * 2,
+        in_specs=[VM] * 5,
         out_specs=HBM,
         scratch_shapes=[pltpu.VMEM((VROWS, BLOCK, GC), F32), pltpu.SemaphoreType.DMA((len(PARTS),))],
         compiler_params=params,
         name="join",
-    )(own, arrived)
+    )(own, late, colw, roww, arrived)
     *biases, grid = lax.optimization_barrier((*biases, grid))
     bias = pl.pallas_call(
         functools.partial(bias_kernel, scale=1.0 / math.sqrt(obs * n_tile * n_slot)),

time: 66 us -> 64 us (0.970)
  local copies, waits for them, and re-layouts: 3.74 us -> 0 us
  waiting for transfers between devices: 4.2 us -> 7.26 us
  Pallas kernels: 14.7 us -> 13.4 us
    unnamed x16 -> x0, local copies, waits for them, and re-layouts: 3.74 us -> none
    all_to_all x1, waiting for transfers between devices: 0.01 us -> 3.17 us  [per_device(): lax.all_to_all(chunk.reshape(n_tile, CAP, 128), 'tile', 0, 0, tiled=True)]
  transfers between devices with their start and end apart: 8 -> 8, of which waited for: 2 -> 3; matrix products, arithmetic and copies ran while one was open for 0% -> 0% of each run, Pallas kernels for 11% -> 9%
where the time goes in v7:
time: 64 us; the launch traced here: 63.8 us
  blocking collectives  26.3 us (41%)
  starting transfers between devices  16.1 us (25%)
  Pallas kernels  13.4 us (21%)
  waiting for transfers between devices  7.26 us (11%)
  between operations  0.74 us (1%)
    all_to_all x1, blocking collectives, per_device(): lax.all_to_all(send.reshape(n_tile, 2 * CAP, WIDE), 'tile', 0, 0, tiled=T...  26.3 us
    ppermute x6, starting transfers between devices, around(): lax.ppermute(x, 'slot', [(i, (i + d) % n_slot) for i in range(n_slot)])  7.27 us
    pallas_call x1, Pallas kernels, per_device(): pl.pallas_call(functools.partial(send_kernel, steps=steps), out_shape=jax...  6.54 us
    all_to_all x1, starting transfers between devices, per_device(): lax.all_to_all(chunk.reshape(n_tile, CAP, 128), 'tile', 0, 0, tiled=True)  5.55 us
    ppermute x6, waiting for transfers between devices, around(): lax.ppermute(x, 'slot', [(i, (i + d) % n_slot) for i in range(n_slot)])  4.09 us
    ppermute x1, starting transfers between devices, per_device(): arrived = lax.ppermute(spill, ('tile', 'slot'), pairs)  3.31 us
    all_to_all x1, waiting for transfers between devices, per_device(): lax.all_to_all(chunk.reshape(n_tile, CAP, 128), 'tile', 0, 0, tiled=True)  3.17 us
    pallas_call x1, Pallas kernels, per_device(): pl.pallas_call(join_kernel, out_shape=jax.ShapeDtypeStruct((levels, BLOCK...  2.72 us
  transfers between devices with their start and end apart: 8, of which 3 were waited for; matrix products, arithmetic and copies ran while one was open for 0% of the time, Pallas kernels for 9%

profile of v7, /device:TPU:1, one launch (start us, length us, event | category | flops | bytes accessed | tf_op | source)
XLA Modules:
  0.0 63.8 jit_solution(418375438043066128)
XLA Ops:
  0.6 6.5 %send.1 = bf16[512,256]{1,0:T(8,128)(2,1)} custom-call(bf16[100,96,411]{2,1,0:T(8,128)(2,1)} %bitcast.18, bf16[96,100]{1,0:T(8,128)(2,1)} %refs_1_.1, f32[1,100]{1,0:T(1,128)} %bitcast.22, s32[1,96]{1,0:T(1,128)} %bitcast.23, bf16[1,96]{1,0:T(2,128)(2,1)} %bitcast.24, bf16[1,96]{1,0:T(2,128)(2,1)} %bitcast.25, s32[1,96]{1,0:T(1,128)} %bitcast.26, ...), custom_call_target="tpu_custom_call" | custom-call | tf_op jit(solution)/shard_map/send/pallas_call | solution.py:232
  7.2 26.3 %all_to_all.10 = bf16[64,8,256]{2,1,0:T(8,128)(2,1)S(1)} all-to-all(bf16[64,8,256]{2,1,0:T(8,128)(2,1)} %bitcast.20), channel_id=1, replica_groups=mesh['tile'=64,'slot'=4] {'tile'}, dimensions={0} | all-to-all | bytes 524288 | tf_op jit(solution)/shard_map/all_to_all | solution.py:247
  33.5 0.4 turn.1.a0
  33.9 1.3 %collective-permute-start = (bf16[416,256]{1,0:T(8,128)(2,1)S(1)}, bf16[416,256]{1,0:T(8,128)(2,1)S(1)}, u32[]{:S(2)}, u32[]{:S(2)}) collective-permute-start(bf16[416,256]{1,0:T(8,128)(2,1)S(1)} %turn.1.a0), channel_id=1, source_target_pairs={{0,1},{1,2},{2,3},{3,0},{4,5},{5,6},{6,7},{7,4},{8,9},{9,10},{10,1... | collective-permute-start | bytes 638984 | tf_op jit(solution)/shard_map/ppermute | solution.py:258
  35.2 1.5 %collective-permute-start.1 = (bf16[416,256]{1,0:T(8,128)(2,1)S(1)}, bf16[416,256]{1,0:T(8,128)(2,1)S(1)}, u32[]{:S(2)}, u32[]{:S(2)}) collective-permute-start(bf16[416,256]{1,0:T(8,128)(2,1)S(1)} %turn.1.a0), channel_id=1, source_target_pairs={{0,3},{1,0},{2,1},{3,2},{4,7},{5,4},{6,5},{7,6},{8,11},{9,8},{10,9... | collective-permute-start | bytes 638984 | tf_op jit(solution)/shard_map/ppermute | solution.py:258
  36.7 1.5 %collective-permute-start.2 = (bf16[416,256]{1,0:T(8,128)(2,1)S(1)}, bf16[416,256]{1,0:T(8,128)(2,1)S(1)}, u32[]{:S(2)}, u32[]{:S(2)}) collective-permute-start(bf16[416,256]{1,0:T(8,128)(2,1)S(1)} %turn.1.a0), channel_id=1, source_target_pairs={{0,2},{1,3},{2,0},{3,1},{4,6},{5,7},{6,4},{7,5},{8,10},{9,11},{10,... | collective-permute-start | bytes 638984 | tf_op jit(solution)/shard_map/ppermute | solution.py:258
  38.2 1.0 %chunk.1 = f32[256,128]{1,0:T(8,128)} custom-call(bf16[512,256]{1,0:T(8,128)(2,1)S(1)} %bitcast.16), custom_call_target="tpu_custom_call" | custom-call | tf_op jit(solution)/shard_map/chunk/pallas_call | solution.py:261
  39.2 5.6 %all-to-all-start.1 = ((f32[64,4,128]{2,1,0:T(4,128)}), f32[64,4,128]{2,1,0:T(4,128)S(1)}, u32[]{:S(2)}, u32[]{:S(2)}) async-start(f32[64,4,128]{2,1,0:T(4,128)} %bitcast.12), calls=%async_computation.1 | async-start | bytes 262144 | tf_op jit(solution)/shard_map/all_to_all | solution.py:269
  44.7 0.0 collective-permute-done.a1
  44.7 0.0 collective-permute-done.1.a2
  44.7 2.6 %collective-permute-done.2.a3 = bf16[416,256]{1,0:T(8,128)(2,1)S(1)} collective-permute-done((bf16[416,256]{1,0:T(8,128)(2,1)S(1)}, bf16[416,256]{1,0:T(8,128)(2,1)S(1)}, u32[]{:S(2)}, u32[]{:S(2)}) %collective-permute-start.2) | collective-permute-done | bytes 213024 | tf_op jit(solution)/shard_map/ppermute | solution.py:258
  47.3 0.6 prep.1
  47.9 3.3 %collective-permute-start.6 = (bf16[416,256]{1,0:T(8,128)(2,1)S(1)}, bf16[416,256]{1,0:T(8,128)(2,1)S(1)}, u32[]{:S(2)}, u32[]{:S(2)}) collective-permute-start(bf16[416,256]{1,0:T(8,128)(2,1)S(1)} %get-tuple-element.20), channel_id=1, source_target_pairs={{0,4},{4,8},{8,12},{12,16},{16,20},{20,24},{24,28},{28,32},{32,36}... | collective-permute-start | bytes 638984 | tf_op jit(solution)/shard_map/ppermute | solution.py:288
  51.3 1.4 %grid.1 = f32[256,8,256]{2,1,0:T(8,128)S(1)} custom-call(bf16[256,1024]{1,0:T(8,128)(2,1)S(1)} %get-tuple-element.14.rows, bf16[256,1024]{1,0:T(8,128)(2,1)S(1)} %get-tuple-element.15.colw, f32[8,1024]{1,0:T(8,128)S(1)} %get-tuple-element.16.roww), custom_call_target="tpu_custom_call" | custom-call | tf_op jit(solution)/shard_map/grid/pallas_call | solution.py:289
  52.7 3.2 %all-to-all-done.1 = f32[64,4,128]{2,1,0:T(4,128)S(1)} async-done(((f32[64,4,128]{2,1,0:T(4,128)}), f32[64,4,128]{2,1,0:T(4,128)S(1)}, u32[]{:S(2)}, u32[]{:S(2)}) %all-to-all-start.1) | async-done | bytes 131104 | tf_op jit(solution)/shard_map/all_to_all | solution.py:269
  55.8 0.1 slot_bias.1.b0
  55.9 0.4 collective-permute-start.3
  56.3 2.4 %collective-permute-start.4 = (f32[100,128]{1,0:T(8,128)S(1)}, f32[100,128]{1,0:T(8,128)S(1)}, u32[]{:S(2)}, u32[]{:S(2)}) collective-permute-start(f32[100,128]{1,0:T(8,128)S(1)} %slot_bias.1.b0), channel_id=1, source_target_pairs={{0,3},{1,0},{2,1},{3,2},{4,7},{5,4},{6,5},{7,6},{8,11},{9,8},{10,9... | collective-permute-start | bytes 153608 | tf_op jit(solution)/shard_map/ppermute | solution.py:258
  58.7 0.2 collective-permute-start.5
  58.9 0.0 collective-permute-done.6.spill
  58.9 2.7 %join.1 = f32[411,8,256]{2,1,0:T(8,128)} custom-call(f32[256,8,256]{2,1,0:T(8,128)S(1)} %grid.1, bf16[160,1024]{1,0:T(8,128)(2,1)S(1)} %get-tuple-element.19.rows, bf16[256,1024]{1,0:T(8,128)(2,1)S(1)} %get-tuple-element.15.colw, f32[8,1024]{1,0:T(8,128)S(1)} %get-tuple-element.16.roww, bf16[416,256]{1,0:T(8,128)(2,1)S(1)} %collective-permute-done.6.spill), custom_call_target="tpu_custom_call" | custom-call | tf_op jit(solution)/shard_map/join/pallas_call | solution.py:307
  61.6 0.0 collective-permute-done.3.b1
  61.6 0.0 collective-permute-done.4.b2
  61.7 1.5 %collective-permute-done.5.b3 = f32[100,128]{1,0:T(8,128)S(1)} collective-permute-done((f32[100,128]{1,0:T(8,128)S(1)}, f32[100,128]{1,0:T(8,128)S(1)}, u32[]{:S(2)}, u32[]{:S(2)}) %collective-permute-start.5) | collective-permute-done | bytes 51232 | tf_op jit(solution)/shard_map/ppermute | solution.py:258
  63.2 0.6 %bias.1 = f32[100,128]{1,0:T(8,128)} custom-call(f32[100,128]{1,0:T(8,128)S(1)} %slot_bias.1.b0, f32[100,128]{1,0:T(8,128)S(1)} %collective-permute-done.3.b1, f32[100,128]{1,0:T(8,128)S(1)} %collective-permute-done.4.b2, f32[100,128]{1,0:T(8,128)S(1)} %collective-permute-done.5.b3), custom_call_target="tpu_custom_call" | custom-call | tf_op jit(solution)/shard_map/bias/pallas_call | solution.py:317
Async XLA Ops:
  33.9 10.8 %collective-permute-start = (bf16[416,256]{1,0:T(8,128)(2,1)S(1)}, bf16[416,256]{1,0:T(8,128)(2,1)S(1)}, u32[]{:S(2)}, u32[]{:S(2)}) collective-permute-start(bf16[416,256]{1,0:T(8,128)(2,1)S(1)} %turn.1.a0), channel_id=1, source_target_pairs={{0,1},{1,2},{2,3},{3,0},{4,5},{5,6},{6,7},{7,4},{8,9},{9,10},{10,1... | collective-permute-start | bytes 638984 | tf_op jit(solution)/shard_map/ppermute | solution.py:258
  35.2 9.5 %collective-permute-start.1 = (bf16[416,256]{1,0:T(8,128)(2,1)S(1)}, bf16[416,256]{1,0:T(8,128)(2,1)S(1)}, u32[]{:S(2)}, u32[]{:S(2)}) collective-permute-start(bf16[416,256]{1,0:T(8,128)(2,1)S(1)} %turn.1.a0), channel_id=1, source_target_pairs={{0,3},{1,0},{2,1},{3,2},{4,7},{5,4},{6,5},{7,6},{8,11},{9,8},{10,9... | collective-permute-start | bytes 638984 | tf_op jit(solution)/shard_map/ppermute | solution.py:258
  36.7 10.7 %collective-permute-start.2 = (bf16[416,256]{1,0:T(8,128)(2,1)S(1)}, bf16[416,256]{1,0:T(8,128)(2,1)S(1)}, u32[]{:S(2)}, u32[]{:S(2)}) collective-permute-start(bf16[416,256]{1,0:T(8,128)(2,1)S(1)} %turn.1.a0), channel_id=1, source_target_pairs={{0,2},{1,3},{2,0},{3,1},{4,6},{5,7},{6,4},{7,5},{8,10},{9,11},{10,... | collective-permute-start | bytes 638984 | tf_op jit(solution)/shard_map/ppermute | solution.py:258
  39.2 16.7 %all-to-all-start.1 = ((f32[64,4,128]{2,1,0:T(4,128)}), f32[64,4,128]{2,1,0:T(4,128)S(1)}, u32[]{:S(2)}, u32[]{:S(2)}) async-start(f32[64,4,128]{2,1,0:T(4,128)} %bitcast.12), calls=%async_computation.1 | async-start | bytes 262144 | tf_op jit(solution)/shard_map/all_to_all | solution.py:269
  47.9 11.0 %collective-permute-start.6 = (bf16[416,256]{1,0:T(8,128)(2,1)S(1)}, bf16[416,256]{1,0:T(8,128)(2,1)S(1)}, u32[]{:S(2)}, u32[]{:S(2)}) collective-permute-start(bf16[416,256]{1,0:T(8,128)(2,1)S(1)} %get-tuple-element.20), channel_id=1, source_target_pairs={{0,4},{4,8},{8,12},{12,16},{16,20},{20,24},{24,28},{28,32},{32,36}... | collective-permute-start | bytes 638984 | tf_op jit(solution)/shard_map/ppermute | solution.py:288
  55.9 5.7 %collective-permute-start.3 = (f32[100,128]{1,0:T(8,128)S(1)}, f32[100,128]{1,0:T(8,128)S(1)}, u32[]{:S(2)}, u32[]{:S(2)}) collective-permute-start(f32[100,128]{1,0:T(8,128)S(1)} %slot_bias.1.b0), channel_id=1, source_target_pairs={{0,1},{1,2},{2,3},{3,0},{4,5},{5,6},{6,7},{7,4},{8,9},{9,10},{10,1... | collective-permute-start | bytes 153608 | tf_op jit(solution)/shard_map/ppermute | solution.py:258
  56.3 5.3 %collective-permute-start.4 = (f32[100,128]{1,0:T(8,128)S(1)}, f32[100,128]{1,0:T(8,128)S(1)}, u32[]{:S(2)}, u32[]{:S(2)}) collective-permute-start(f32[100,128]{1,0:T(8,128)S(1)} %slot_bias.1.b0), channel_id=1, source_target_pairs={{0,3},{1,0},{2,1},{3,2},{4,7},{5,4},{6,5},{7,6},{8,11},{9,8},{10,9... | collective-permute-start | bytes 153608 | tf_op jit(solution)/shard_map/ppermute | solution.py:258
  58.7 4.5 %collective-permute-start.5 = (f32[100,128]{1,0:T(8,128)S(1)}, f32[100,128]{1,0:T(8,128)S(1)}, u32[]{:S(2)}, u32[]{:S(2)}) collective-permute-start(f32[100,128]{1,0:T(8,128)S(1)} %slot_bias.1.b0), channel_id=1, source_target_pairs={{0,2},{1,3},{2,0},{3,1},{4,6},{5,7},{6,4},{7,5},{8,10},{9,11},{10,... | collective-permute-start | bytes 153608 | tf_op jit(solution)/shard_map/ppermute | solution.py:258

commit v8 on v7

--- a/solution.py
+++ b/solution.py
@@ -19,8 +19,9 @@
 LANES = 512
 WIDE = LANES // 2
 VROWS = 416
-PARTS = ((0, 128), (128, 256), (256, 336), (336, 416))
+PARTS = ((0, 128), (128, 256), (256, 368), (368, 416))
 EARLY = 2
+OUT_BLOCKS = 4
 BLOCK = 8
 VMEM = 24 * 1024 * 1024
 
@@ -38,7 +39,8 @@
 
 
 def send_kernel(*refs, steps):
-    k_hbm, small_hbm, out, small, kbuf, acc, sems, small_sems = refs[0], refs[1:10], *refs[10:11], refs[11:20], *refs[20:]
+    k_hbm, small_hbm, out, small = refs[0], refs[1:10], refs[10], refs[11:20]
+    kbuf, acc, placed, sems, small_sems, out_sems = refs[20:]
     chans, obs, levels = k_hbm.shape
     per = chans // steps
     small_copies = [
@@ -114,9 +116,18 @@
     for i in range(steps // 2, steps):
         sums(i)
     rows = acc[...].astype(BF16)
-    placed = dot(first_half, rows[:, 0:WIDE], NN) + dot(second_half, rows[:, WIDE:LANES], NN)
-    out[:, 0 : WIDE - 128] = placed[:, 0 : WIDE - 128].astype(BF16)
-    out[:, WIDE - 128 : WIDE] = (placed[:, WIDE - 128 : WIDE] + extra).astype(BF16)
+    size = rows_out // OUT_BLOCKS
+    out_copies = []
+    for i in range(OUT_BLOCKS):
+        at = slice(i * size, (i + 1) * size)
+        block = dot(first_half[at, :], rows[:, 0:WIDE], NN) + dot(second_half[at, :], rows[:, WIDE:LANES], NN)
+        placed[at, 0 : WIDE - 128] = block[:, 0 : WIDE - 128].astype(BF16)
+        placed[at, WIDE - 128 : WIDE] = (block[:, WIDE - 128 : WIDE] + extra[at, :]).astype(BF16)
+        here = pl.ds(i * size, size)
+        out_copies.append(pltpu.make_async_copy(placed.at[here], out.at[here], out_sems.at[i]))
+        out_copies[i].start()
+    for copy in out_copies:
+        copy.wait()
 
 
 def picks(slots, offset):
@@ -233,13 +244,15 @@
         functools.partial(send_kernel, steps=steps),
         out_shape=jax.ShapeDtypeStruct((2 * slots, WIDE), BF16),
         in_specs=[HBM] * (1 + len(small)),
-        out_specs=VM,
+        out_specs=HBM,
         scratch_shapes=[pltpu.VMEM(x.shape, x.dtype) for x in small]
         + [
             pltpu.VMEM((chans, obs, levels), BF16),
             pltpu.VMEM((obs, LANES), F32),
+            pltpu.VMEM((2 * slots, WIDE), BF16),
             pltpu.SemaphoreType.DMA((steps,)),
             pltpu.SemaphoreType.DMA((len(small),)),
+            pltpu.SemaphoreType.DMA((OUT_BLOCKS,)),
         ],
         compiler_params=tight,
         name="send",
@@ -254,10 +267,10 @@
         name="turn",
     )(got)
 
-    def around(x):
-        return [x] + [lax.ppermute(x, "slot", [(i, (i + d) % n_slot) for i in range(n_slot)]) for d in (1, 3, 2)]
-
-    blocks = around(turned)
+    def around(x, distances):
+        return [x] + [lax.ppermute(x, "slot", [(i, (i + d) % n_slot) for i in range(n_slot)]) for d in distances]
+
+    blocks = around(turned, (1, 3, 2))
     chunk = pl.pallas_call(
         functools.partial(chunk_kernel, levels=levels, half=chans // 2),
         out_shape=jax.ShapeDtypeStruct((slots, 128), F32),
@@ -303,7 +316,7 @@
         compiler_params=params,
         name="slot_bias",
     )(chunks)
-    biases = around(slot_bias)
+    biases = around(slot_bias, (2, 1, 3))
     grid = pl.pallas_call(
         join_kernel,
         out_shape=jax.ShapeDtypeStruct((levels, BLOCK, GC), F32),

time: 64 us -> 63.7 us (level)
  waiting for transfers between devices: 7.26 us -> 5.78 us
  starting transfers between devices: 16.1 us -> 17.3 us
    ppermute x6, waiting for transfers between devices: 4.09 us -> 2.61 us  [around(): lax.ppermute(x, 'slot', [(i, (i + d) % n_slot) for i in range(n_slot)])]
    ppermute x6, starting transfers between devices: 7.27 us -> 8.49 us  [around(): lax.ppermute(x, 'slot', [(i, (i + d) % n_slot) for i in range(n_slot)])]
  transfers between devices with their start and end apart: 8 -> 8, of which waited for: 3 -> 2; matrix products, arithmetic and copies ran while one was open for 0% -> 0% of each run, Pallas kernels for 9% -> 9%
where the time goes in v8:
time: 63.7 us; the launch traced here: 63.4 us
  blocking collectives  26.3 us (41%)
  starting transfers between devices  17.3 us (27%)
  Pallas kernels  13.3 us (21%)
  waiting for transfers between devices  5.78 us (9%)
  between operations  0.74 us (1%)
    all_to_all x1, blocking collectives, per_device(): lax.all_to_all(send.reshape(n_tile, 2 * CAP, WIDE), 'tile', 0, 0, tiled=T...  26.3 us
    ppermute x6, starting transfers between devices, around(): lax.ppermute(x, 'slot', [(i, (i + d) % n_slot) for i in range(n_slot)])  8.49 us
    pallas_call x1, Pallas kernels, per_device(): pl.pallas_call(functools.partial(send_kernel, steps=steps), out_shape=jax...  6.51 us
    all_to_all x1, starting transfers between devices, per_device(): lax.all_to_all(chunk.reshape(n_tile, CAP, 128), 'tile', 0, 0, tiled=True)  5.56 us
    ppermute x1, starting transfers between devices, per_device(): arrived = lax.ppermute(spill, ('tile', 'slot'), pairs)  3.29 us
    all_to_all x1, waiting for transfers between devices, per_device(): lax.all_to_all(chunk.reshape(n_tile, CAP, 128), 'tile', 0, 0, tiled=True)  3.18 us
    pallas_call x1, Pallas kernels, per_device(): pl.pallas_call(join_kernel, out_shape=jax.ShapeDtypeStruct((levels, BLOCK...  2.66 us
    ppermute x6, waiting for transfers between devices, around(): lax.ppermute(x, 'slot', [(i, (i + d) % n_slot) for i in range(n_slot)])  2.61 us
  transfers between devices with their start and end apart: 8, of which 2 were waited for; matrix products, arithmetic and copies ran while one was open for 0% of the time, Pallas kernels for 9%

profile of v8, /device:TPU:1, one launch (start us, length us, event | category | flops | bytes accessed | tf_op | source)
XLA Modules:
  0.0 63.4 jit_solution(14111879030666539633)
XLA Ops:
  0.6 6.5 %send.1 = bf16[512,256]{1,0:T(8,128)(2,1)} custom-call(bf16[100,96,411]{2,1,0:T(8,128)(2,1)} %bitcast.18, bf16[96,100]{1,0:T(8,128)(2,1)} %refs_1_.1, f32[1,100]{1,0:T(1,128)} %bitcast.22, s32[1,96]{1,0:T(1,128)} %bitcast.23, bf16[1,96]{1,0:T(2,128)(2,1)} %bitcast.24, bf16[1,96]{1,0:T(2,128)(2,1)} %bitcast.25, s32[1,96]{1,0:T(1,128)} %bitcast.26, ...), custom_call_target="tpu_custom_call" | custom-call | tf_op jit(solution)/shard_map/send/pallas_call | solution.py:243
  7.2 26.3 %all_to_all.10 = bf16[64,8,256]{2,1,0:T(8,128)(2,1)S(1)} all-to-all(bf16[64,8,256]{2,1,0:T(8,128)(2,1)} %bitcast.20), channel_id=1, replica_groups=mesh['tile'=64,'slot'=4] {'tile'}, dimensions={0} | all-to-all | bytes 524288 | tf_op jit(solution)/shard_map/all_to_all | solution.py:260
  33.5 0.4 turn.1.a0
  33.9 1.3 %collective-permute-start = (bf16[416,256]{1,0:T(8,128)(2,1)S(1)}, bf16[416,256]{1,0:T(8,128)(2,1)S(1)}, u32[]{:S(2)}, u32[]{:S(2)}) collective-permute-start(bf16[416,256]{1,0:T(8,128)(2,1)S(1)} %turn.1.a0), channel_id=1, source_target_pairs={{0,1},{1,2},{2,3},{3,0},{4,5},{5,6},{6,7},{7,4},{8,9},{9,10},{10,1... | collective-permute-start | bytes 638984 | tf_op jit(solution)/shard_map/ppermute | solution.py:271
  35.2 1.5 %collective-permute-start.1 = (bf16[416,256]{1,0:T(8,128)(2,1)S(1)}, bf16[416,256]{1,0:T(8,128)(2,1)S(1)}, u32[]{:S(2)}, u32[]{:S(2)}) collective-permute-start(bf16[416,256]{1,0:T(8,128)(2,1)S(1)} %turn.1.a0), channel_id=1, source_target_pairs={{0,3},{1,0},{2,1},{3,2},{4,7},{5,4},{6,5},{7,6},{8,11},{9,8},{10,9... | collective-permute-start | bytes 638984 | tf_op jit(solution)/shard_map/ppermute | solution.py:271
  36.6 1.5 %collective-permute-start.2 = (bf16[416,256]{1,0:T(8,128)(2,1)S(1)}, bf16[416,256]{1,0:T(8,128)(2,1)S(1)}, u32[]{:S(2)}, u32[]{:S(2)}) collective-permute-start(bf16[416,256]{1,0:T(8,128)(2,1)S(1)} %turn.1.a0), channel_id=1, source_target_pairs={{0,2},{1,3},{2,0},{3,1},{4,6},{5,7},{6,4},{7,5},{8,10},{9,11},{10,... | collective-permute-start | bytes 638984 | tf_op jit(solution)/shard_map/ppermute | solution.py:271
  38.2 1.0 %chunk.1 = f32[256,128]{1,0:T(8,128)} custom-call(bf16[512,256]{1,0:T(8,128)(2,1)S(1)} %bitcast.16), custom_call_target="tpu_custom_call" | custom-call | tf_op jit(solution)/shard_map/chunk/pallas_call | solution.py:274
  39.1 5.6 %all-to-all-start.1 = ((f32[64,4,128]{2,1,0:T(4,128)}), f32[64,4,128]{2,1,0:T(4,128)S(1)}, u32[]{:S(2)}, u32[]{:S(2)}) async-start(f32[64,4,128]{2,1,0:T(4,128)} %bitcast.12), calls=%async_computation.1 | async-start | bytes 262144 | tf_op jit(solution)/shard_map/all_to_all | solution.py:282
  44.7 0.0 collective-permute-done.a1
  44.7 0.0 collective-permute-done.1.a2
  44.7 2.6 %collective-permute-done.2.a3 = bf16[416,256]{1,0:T(8,128)(2,1)S(1)} collective-permute-done((bf16[416,256]{1,0:T(8,128)(2,1)S(1)}, bf16[416,256]{1,0:T(8,128)(2,1)S(1)}, u32[]{:S(2)}, u32[]{:S(2)}) %collective-permute-start.2) | collective-permute-done | bytes 213024 | tf_op jit(solution)/shard_map/ppermute | solution.py:271
  47.3 0.6 prep.1
  47.9 3.3 %collective-permute-start.6 = (bf16[416,256]{1,0:T(8,128)(2,1)S(1)}, bf16[416,256]{1,0:T(8,128)(2,1)S(1)}, u32[]{:S(2)}, u32[]{:S(2)}) collective-permute-start(bf16[416,256]{1,0:T(8,128)(2,1)S(1)} %get-tuple-element.20), channel_id=1, source_target_pairs={{0,4},{4,8},{8,12},{12,16},{16,20},{20,24},{24,28},{28,32},{32,36}... | collective-permute-start | bytes 638984 | tf_op jit(solution)/shard_map/ppermute | solution.py:301
  51.2 1.4 %grid.1 = f32[256,8,256]{2,1,0:T(8,128)S(1)} custom-call(bf16[256,1024]{1,0:T(8,128)(2,1)S(1)} %get-tuple-element.14.rows, bf16[256,1024]{1,0:T(8,128)(2,1)S(1)} %get-tuple-element.15.colw, f32[8,1024]{1,0:T(8,128)S(1)} %get-tuple-element.16.roww), custom_call_target="tpu_custom_call" | custom-call | tf_op jit(solution)/shard_map/grid/pallas_call | solution.py:302
  52.6 3.2 %all-to-all-done.1 = f32[64,4,128]{2,1,0:T(4,128)S(1)} async-done(((f32[64,4,128]{2,1,0:T(4,128)}), f32[64,4,128]{2,1,0:T(4,128)S(1)}, u32[]{:S(2)}, u32[]{:S(2)}) %all-to-all-start.1) | async-done | bytes 131104 | tf_op jit(solution)/shard_map/all_to_all | solution.py:282
  55.8 0.1 slot_bias.1.b0
  55.9 1.5 %collective-permute-start.3 = (f32[100,128]{1,0:T(8,128)S(1)}, f32[100,128]{1,0:T(8,128)S(1)}, u32[]{:S(2)}, u32[]{:S(2)}) collective-permute-start(f32[100,128]{1,0:T(8,128)S(1)} %slot_bias.1.b0), channel_id=1, source_target_pairs={{0,2},{1,3},{2,0},{3,1},{4,6},{5,7},{6,4},{7,5},{8,10},{9,11},{10,... | collective-permute-start | bytes 153608 | tf_op jit(solution)/shard_map/ppermute | solution.py:271
  57.4 0.0 collective-permute-start.4
  57.4 2.7 %collective-permute-start.5 = (f32[100,128]{1,0:T(8,128)S(1)}, f32[100,128]{1,0:T(8,128)S(1)}, u32[]{:S(2)}, u32[]{:S(2)}) collective-permute-start(f32[100,128]{1,0:T(8,128)S(1)} %slot_bias.1.b0), channel_id=1, source_target_pairs={{0,3},{1,0},{2,1},{3,2},{4,7},{5,4},{6,5},{7,6},{8,11},{9,8},{10,9... | collective-permute-start | bytes 153608 | tf_op jit(solution)/shard_map/ppermute | solution.py:271
  60.1 0.0 collective-permute-done.6.spill
  60.1 2.7 %join.1 = f32[411,8,256]{2,1,0:T(8,128)} custom-call(f32[256,8,256]{2,1,0:T(8,128)S(1)} %grid.1, bf16[160,1024]{1,0:T(8,128)(2,1)S(1)} %get-tuple-element.19.rows, bf16[256,1024]{1,0:T(8,128)(2,1)S(1)} %get-tuple-element.15.colw, f32[8,1024]{1,0:T(8,128)S(1)} %get-tuple-element.16.roww, bf16[416,256]{1,0:T(8,128)(2,1)S(1)} %collective-permute-done.6.spill), custom_call_target="tpu_custom_call" | custom-call | tf_op jit(solution)/shard_map/join/pallas_call | solution.py:320
  62.8 0.0 collective-permute-done.3.b1
  62.8 0.0 collective-permute-done.4.b2
  62.8 0.0 collective-permute-done.5.b3
  62.8 0.6 %bias.1 = f32[100,128]{1,0:T(8,128)} custom-call(f32[100,128]{1,0:T(8,128)S(1)} %slot_bias.1.b0, f32[100,128]{1,0:T(8,128)S(1)} %collective-permute-done.3.b1, f32[100,128]{1,0:T(8,128)S(1)} %collective-permute-done.4.b2, f32[100,128]{1,0:T(8,128)S(1)} %collective-permute-done.5.b3), custom_call_target="tpu_custom_call" | custom-call | tf_op jit(solution)/shard_map/bias/pallas_call | solution.py:330
Async XLA Ops:
  33.9 10.8 %collective-permute-start = (bf16[416,256]{1,0:T(8,128)(2,1)S(1)}, bf16[416,256]{1,0:T(8,128)(2,1)S(1)}, u32[]{:S(2)}, u32[]{:S(2)}) collective-permute-start(bf16[416,256]{1,0:T(8,128)(2,1)S(1)} %turn.1.a0), channel_id=1, source_target_pairs={{0,1},{1,2},{2,3},{3,0},{4,5},{5,6},{6,7},{7,4},{8,9},{9,10},{10,1... | collective-permute-start | bytes 638984 | tf_op jit(solution)/shard_map/ppermute | solution.py:271
  35.2 9.6 %collective-permute-start.1 = (bf16[416,256]{1,0:T(8,128)(2,1)S(1)}, bf16[416,256]{1,0:T(8,128)(2,1)S(1)}, u32[]{:S(2)}, u32[]{:S(2)}) collective-permute-start(bf16[416,256]{1,0:T(8,128)(2,1)S(1)} %turn.1.a0), channel_id=1, source_target_pairs={{0,3},{1,0},{2,1},{3,2},{4,7},{5,4},{6,5},{7,6},{8,11},{9,8},{10,9... | collective-permute-start | bytes 638984 | tf_op jit(solution)/shard_map/ppermute | solution.py:271
  36.6 10.7 %collective-permute-start.2 = (bf16[416,256]{1,0:T(8,128)(2,1)S(1)}, bf16[416,256]{1,0:T(8,128)(2,1)S(1)}, u32[]{:S(2)}, u32[]{:S(2)}) collective-permute-start(bf16[416,256]{1,0:T(8,128)(2,1)S(1)} %turn.1.a0), channel_id=1, source_target_pairs={{0,2},{1,3},{2,0},{3,1},{4,6},{5,7},{6,4},{7,5},{8,10},{9,11},{10,... | collective-permute-start | bytes 638984 | tf_op jit(solution)/shard_map/ppermute | solution.py:271
  39.1 16.7 %all-to-all-start.1 = ((f32[64,4,128]{2,1,0:T(4,128)}), f32[64,4,128]{2,1,0:T(4,128)S(1)}, u32[]{:S(2)}, u32[]{:S(2)}) async-start(f32[64,4,128]{2,1,0:T(4,128)} %bitcast.12), calls=%async_computation.1 | async-start | bytes 262144 | tf_op jit(solution)/shard_map/all_to_all | solution.py:282
  47.9 12.2 %collective-permute-start.6 = (bf16[416,256]{1,0:T(8,128)(2,1)S(1)}, bf16[416,256]{1,0:T(8,128)(2,1)S(1)}, u32[]{:S(2)}, u32[]{:S(2)}) collective-permute-start(bf16[416,256]{1,0:T(8,128)(2,1)S(1)} %get-tuple-element.20), channel_id=1, source_target_pairs={{0,4},{4,8},{8,12},{12,16},{16,20},{20,24},{24,28},{28,32},{32,36}... | collective-permute-start | bytes 638984 | tf_op jit(solution)/shard_map/ppermute | solution.py:301
  55.9 6.9 %collective-permute-start.3 = (f32[100,128]{1,0:T(8,128)S(1)}, f32[100,128]{1,0:T(8,128)S(1)}, u32[]{:S(2)}, u32[]{:S(2)}) collective-permute-start(f32[100,128]{1,0:T(8,128)S(1)} %slot_bias.1.b0), channel_id=1, source_target_pairs={{0,2},{1,3},{2,0},{3,1},{4,6},{5,7},{6,4},{7,5},{8,10},{9,11},{10,... | collective-permute-start | bytes 153608 | tf_op jit(solution)/shard_map/ppermute | solution.py:271
  57.4 5.4 %collective-permute-start.4 = (f32[100,128]{1,0:T(8,128)S(1)}, f32[100,128]{1,0:T(8,128)S(1)}, u32[]{:S(2)}, u32[]{:S(2)}) collective-permute-start(f32[100,128]{1,0:T(8,128)S(1)} %slot_bias.1.b0), channel_id=1, source_target_pairs={{0,1},{1,2},{2,3},{3,0},{4,5},{5,6},{6,7},{7,4},{8,9},{9,10},{10,1... | collective-permute-start | bytes 153608 | tf_op jit(solution)/shard_map/ppermute | solution.py:271
  57.4 5.4 %collective-permute-start.5 = (f32[100,128]{1,0:T(8,128)S(1)}, f32[100,128]{1,0:T(8,128)S(1)}, u32[]{:S(2)}, u32[]{:S(2)}) collective-permute-start(f32[100,128]{1,0:T(8,128)S(1)} %slot_bias.1.b0), channel_id=1, source_target_pairs={{0,3},{1,0},{2,1},{3,2},{4,7},{5,4},{6,5},{7,6},{8,11},{9,8},{10,9... | collective-permute-start | bytes 153608 | tf_op jit(solution)/shard_map/ppermute | solution.py:271

commit v9 on v8

--- a/solution.py
+++ b/solution.py
@@ -19,7 +19,7 @@
 LANES = 512
 WIDE = LANES // 2
 VROWS = 416
-PARTS = ((0, 128), (128, 256), (256, 368), (368, 416))
+PARTS = ((0, 128), (128, 256), (256, 336), (336, 416))
 EARLY = 2
 OUT_BLOCKS = 4
 BLOCK = 8
@@ -135,8 +135,11 @@
     return ones_where(r == (q // CAP) * (2 * CAP) + q % CAP + offset)
 
 
-def chunk_kernel(got, chunk, *, levels, half):
+def turn_kernel(got, out, chunk, *, levels, half):
     slots = got.shape[0] // 2
+    out[0:WIDE, :] = jnp.transpose(dot(picks(slots, 0), got[...], NN)).astype(BF16)
+    rest = jnp.transpose(dot(picks(slots, CAP), got[...], NN))
+    out[WIDE:VROWS, :] = rest[0 : VROWS - WIDE, :].astype(BF16)
     q, r = iota((slots, 2 * slots), 0), iota((slots, 2 * slots), 1)
     pick = ones_where(r % (2 * CAP) == q % CAP + CAP)
     total = dot(pick, got[:, WIDE - 128 : WIDE], NN)
@@ -145,13 +148,6 @@
     kept = 128 - first - half
     sums = jnp.where(lane < half, pltpu.roll(total, 128 - first, 1), 0.0)
     chunk[...] = sums + jnp.where(lane < kept, pltpu.roll(total, 128 - first - half, 1), 0.0)
-
-
-def turn_kernel(got, out):
-    slots = got.shape[0] // 2
-    out[0:WIDE, :] = jnp.transpose(dot(picks(slots, 0), got[...], NN)).astype(BF16)
-    rest = jnp.transpose(dot(picks(slots, CAP), got[...], NN))
-    out[WIDE:VROWS, :] = rest[0 : VROWS - WIDE, :].astype(BF16)
 
 
 def prep_kernel(first_row, a0, a1, a2, a3, spill, colw, roww, early, late, *, levels):
@@ -191,16 +187,36 @@
 
 def join_kernel(grid, rows, colw, roww, spill, out, joined, sems):
     levels = out.shape[0]
-    copies = []
-    for i, (lo, hi) in enumerate(PARTS):
-        first = iota((hi - lo, BLOCK, GC), 1) == 0
-        own = grid[lo:hi] if i < EARLY else grid_part(rows, colw, roww, lo - PARTS[EARLY][0], hi - PARTS[EARLY][0])
-        joined[lo:hi] = own + jnp.where(first, spill[lo:hi, :].astype(F32)[:, None, :], 0.0)
-        size = min(hi, levels) - lo
-        copies.append(pltpu.make_async_copy(joined.at[pl.ds(lo, size)], out.at[pl.ds(lo, size)], sems.at[i]))
-        copies[i].start()
-    for copy in copies:
-        copy.wait()
+    split, size = PARTS[EARLY][0], PARTS[EARLY][1] - PARTS[EARLY][0]
+
+    def copy_of(i):
+        lo, hi = PARTS[i][0], min(PARTS[i][1], levels)
+        return pltpu.make_async_copy(joined.at[pl.ds(lo, hi - lo)], out.at[pl.ds(lo, hi - lo)], sems.at[i])
+
+    def add(own, at, n):
+        first = iota((n, BLOCK, GC), 1) == 0
+        joined[pl.ds(at, n)] = own + jnp.where(first, spill[pl.ds(at, n), :].astype(F32)[:, None, :], 0.0)
+
+    for i, (lo, hi) in enumerate(PARTS[:EARLY]):
+        add(grid[lo:hi], lo, hi - lo)
+        copy_of(i).start()
+
+    def later(i, carry):
+        lo = pl.multiple_of(i * size, 16)
+        lhs = rows[pl.ds(lo, size), :].astype(F32)[:, None, :] * roww[...][None, :, :]
+        lhs = lhs.reshape(size * BLOCK, rows.shape[1]).astype(BF16)
+        add(dot(lhs, colw[...], NT).reshape(size, BLOCK, GC), pl.multiple_of(split + lo, 16), size)
+        for part in range(EARLY, len(PARTS)):
+
+            @pl.when(i == part - EARLY)
+            def _():
+                copy_of(part).start()
+
+        return carry
+
+    lax.fori_loop(0, len(PARTS) - EARLY, later, 0)
+    for i in range(len(PARTS)):
+        copy_of(i).wait()
 
 
 def slot_bias_kernel(got, out, *, half):
@@ -258,11 +274,11 @@
         name="send",
     )(jnp.transpose(k_matrix, (1, 0, 2)), *small)
     got = lax.all_to_all(send.reshape(n_tile, 2 * CAP, WIDE), "tile", 0, 0, tiled=True).reshape(2 * slots, WIDE)
-    turned = pl.pallas_call(
-        turn_kernel,
-        out_shape=jax.ShapeDtypeStruct((VROWS, slots), BF16),
+    turned, chunk = pl.pallas_call(
+        functools.partial(turn_kernel, levels=levels, half=chans // 2),
+        out_shape=(jax.ShapeDtypeStruct((VROWS, slots), BF16), jax.ShapeDtypeStruct((slots, 128), F32)),
         in_specs=[VM],
-        out_specs=VM,
+        out_specs=(VM, VM),
         compiler_params=params,
         name="turn",
     )(got)
@@ -271,14 +287,6 @@
         return [x] + [lax.ppermute(x, "slot", [(i, (i + d) % n_slot) for i in range(n_slot)]) for d in distances]
 
     blocks = around(turned, (1, 3, 2))
-    chunk = pl.pallas_call(
-        functools.partial(chunk_kernel, levels=levels, half=chans // 2),
-        out_shape=jax.ShapeDtypeStruct((slots, 128), F32),
-        in_specs=[VM],
-        out_specs=VM,
-        compiler_params=params,
-        name="chunk",
-    )(got)
     chunks = lax.all_to_all(chunk.reshape(n_tile, CAP, 128), "tile", 0, 0, tiled=True).reshape(slots, 128)
     total = n_slot * slots
     split = PARTS[EARLY][0]

time: 63.7 us -> 63 us (0.989)
    all_to_all x1, waiting for transfers between devices: 3.18 us -> 2.2 us  [per_device(): lax.all_to_all(chunk.reshape(n_tile, CAP, 128), 'tile', 0, 0, tiled=True)]
    ppermute x6, waiting for transfers between devices: 2.61 us -> 3.57 us  [around(): lax.ppermute(x, 'slot', [(i, (i + d) % n_slot) for i in range(n_slot)])]
    pallas_call x2 -> x1, Pallas kernels: 1.36 us -> 1.15 us  [per_device(): pl.pallas_call(functools.partial(turn_kernel, levels=levels, half=chans /...]
  transfers between devices with their start and end apart: 8 -> 8, of which waited for: 2 -> 2; matrix products, arithmetic and copies ran while one was open for 0% -> 0% of each run, Pallas kernels for 9% -> 7%
where the time goes in v9:
time: 63 us; the launch traced here: 62.8 us
  blocking collectives  26.3 us (42%)
  starting transfers between devices  17.3 us (27%)
  Pallas kernels  12.7 us (20%)
  waiting for transfers between devices  5.77 us (9%)
  between operations  0.74 us (1%)
    all_to_all x1, blocking collectives, per_device(): lax.all_to_all(send.reshape(n_tile, 2 * CAP, WIDE), 'tile', 0, 0, tiled=T...  26.3 us
    ppermute x6, starting transfers between devices, around(): lax.ppermute(x, 'slot', [(i, (i + d) % n_slot) for i in range(n_slot)])  8.41 us
    pallas_call x1, Pallas kernels, per_device(): pl.pallas_call(functools.partial(send_kernel, steps=steps), out_shape=jax...  6.51 us
    all_to_all x1, starting transfers between devices, per_device(): lax.all_to_all(chunk.reshape(n_tile, CAP, 128), 'tile', 0, 0, tiled=True)  5.55 us
    ppermute x6, waiting for transfers between devices, around(): lax.ppermute(x, 'slot', [(i, (i + d) % n_slot) for i in range(n_slot)])  3.57 us
    ppermute x1, starting transfers between devices, per_device(): arrived = lax.ppermute(spill, ('tile', 'slot'), pairs)  3.29 us
    pallas_call x1, Pallas kernels, per_device(): pl.pallas_call(join_kernel, out_shape=jax.ShapeDtypeStruct((levels, BLOCK...  2.27 us
    all_to_all x1, waiting for transfers between devices, per_device(): lax.all_to_all(chunk.reshape(n_tile, CAP, 128), 'tile', 0, 0, tiled=True)  2.2 us
  transfers between devices with their start and end apart: 8, of which 2 were waited for; matrix products, arithmetic and copies ran while one was open for 0% of the time, Pallas kernels for 7%

profile of v9, /device:TPU:1, one launch (start us, length us, event | category | flops | bytes accessed | tf_op | source)
XLA Modules:
  0.0 62.8 jit_solution(7120146506427367870)
XLA Ops:
  0.6 6.5 %send.1 = bf16[512,256]{1,0:T(8,128)(2,1)} custom-call(bf16[100,96,411]{2,1,0:T(8,128)(2,1)} %bitcast.17, bf16[96,100]{1,0:T(8,128)(2,1)} %refs_1_.1, f32[1,100]{1,0:T(1,128)} %bitcast.21, s32[1,96]{1,0:T(1,128)} %bitcast.22, bf16[1,96]{1,0:T(2,128)(2,1)} %bitcast.23, bf16[1,96]{1,0:T(2,128)(2,1)} %bitcast.24, s32[1,96]{1,0:T(1,128)} %bitcast.25, ...), custom_call_target="tpu_custom_call" | custom-call | tf_op jit(solution)/shard_map/send/pallas_call | solution.py:259
  7.2 26.3 %all_to_all.10 = bf16[64,8,256]{2,1,0:T(8,128)(2,1)S(1)} all-to-all(bf16[64,8,256]{2,1,0:T(8,128)(2,1)} %bitcast.19), channel_id=1, replica_groups=mesh['tile'=64,'slot'=4] {'tile'}, dimensions={0} | all-to-all | bytes 524288 | tf_op jit(solution)/shard_map/all_to_all | solution.py:276
  33.5 1.1 %turn.1 = (bf16[416,256]{1,0:T(8,128)(2,1)S(1)}, f32[256,128]{1,0:T(8,128)}) custom-call(bf16[512,256]{1,0:T(8,128)(2,1)S(1)} %bitcast.15), custom_call_target="tpu_custom_call" | custom-call | tf_op jit(solution)/shard_map/turn/pallas_call | solution.py:277
  34.6 1.2 %collective-permute-start = (bf16[416,256]{1,0:T(8,128)(2,1)S(1)}, bf16[416,256]{1,0:T(8,128)(2,1)S(1)}, u32[]{:S(2)}, u32[]{:S(2)}) collective-permute-start(bf16[416,256]{1,0:T(8,128)(2,1)S(1)} %get-tuple-element.16.a0), channel_id=1, source_target_pairs={{0,1},{1,2},{2,3},{3,0},{4,5},{5,6},{6,7},{7,4},{8,9},{9,10},{10,1... | collective-permute-start | bytes 638984 | tf_op jit(solution)/shard_map/ppermute | solution.py:287
  35.8 1.5 %collective-permute-start.1 = (bf16[416,256]{1,0:T(8,128)(2,1)S(1)}, bf16[416,256]{1,0:T(8,128)(2,1)S(1)}, u32[]{:S(2)}, u32[]{:S(2)}) collective-permute-start(bf16[416,256]{1,0:T(8,128)(2,1)S(1)} %get-tuple-element.16.a0), channel_id=1, source_target_pairs={{0,3},{1,0},{2,1},{3,2},{4,7},{5,4},{6,5},{7,6},{8,11},{9,8},{10,9... | collective-permute-start | bytes 638984 | tf_op jit(solution)/shard_map/ppermute | solution.py:287
  37.3 1.5 %collective-permute-start.2 = (bf16[416,256]{1,0:T(8,128)(2,1)S(1)}, bf16[416,256]{1,0:T(8,128)(2,1)S(1)}, u32[]{:S(2)}, u32[]{:S(2)}) collective-permute-start(bf16[416,256]{1,0:T(8,128)(2,1)S(1)} %get-tuple-element.16.a0), channel_id=1, source_target_pairs={{0,2},{1,3},{2,0},{3,1},{4,6},{5,7},{6,4},{7,5},{8,10},{9,11},{10,... | collective-permute-start | bytes 638984 | tf_op jit(solution)/shard_map/ppermute | solution.py:287
  38.8 5.6 %all-to-all-start.1 = ((f32[64,4,128]{2,1,0:T(4,128)}), f32[64,4,128]{2,1,0:T(4,128)S(1)}, u32[]{:S(2)}, u32[]{:S(2)}) async-start(f32[64,4,128]{2,1,0:T(4,128)} %bitcast.12), calls=%async_computation.1 | async-start | bytes 262144 | tf_op jit(solution)/shard_map/all_to_all | solution.py:290
  44.4 0.0 collective-permute-done.a1
  44.4 0.0 collective-permute-done.1.a2
  44.4 3.6 %collective-permute-done.2.a3 = bf16[416,256]{1,0:T(8,128)(2,1)S(1)} collective-permute-done((bf16[416,256]{1,0:T(8,128)(2,1)S(1)}, bf16[416,256]{1,0:T(8,128)(2,1)S(1)}, u32[]{:S(2)}, u32[]{:S(2)}) %collective-permute-start.2) | collective-permute-done | bytes 213024 | tf_op jit(solution)/shard_map/ppermute | solution.py:287
  48.0 0.6 prep.1
  48.6 3.3 %collective-permute-start.6 = (bf16[416,256]{1,0:T(8,128)(2,1)S(1)}, bf16[416,256]{1,0:T(8,128)(2,1)S(1)}, u32[]{:S(2)}, u32[]{:S(2)}) collective-permute-start(bf16[416,256]{1,0:T(8,128)(2,1)S(1)} %get-tuple-element.24), channel_id=1, source_target_pairs={{0,4},{4,8},{8,12},{12,16},{16,20},{20,24},{24,28},{28,32},{32,36}... | collective-permute-start | bytes 638984 | tf_op jit(solution)/shard_map/ppermute | solution.py:309
  51.9 1.4 %grid.1 = f32[256,8,256]{2,1,0:T(8,128)S(1)} custom-call(bf16[256,1024]{1,0:T(8,128)(2,1)S(1)} %get-tuple-element.17.rows, bf16[256,1024]{1,0:T(8,128)(2,1)S(1)} %get-tuple-element.18.colw, f32[8,1024]{1,0:T(8,128)S(1)} %get-tuple-element.19.roww), custom_call_target="tpu_custom_call" | custom-call | tf_op jit(solution)/shard_map/grid/pallas_call | solution.py:310
  53.3 2.2 %all-to-all-done.1 = f32[64,4,128]{2,1,0:T(4,128)S(1)} async-done(((f32[64,4,128]{2,1,0:T(4,128)}), f32[64,4,128]{2,1,0:T(4,128)S(1)}, u32[]{:S(2)}, u32[]{:S(2)}) %all-to-all-start.1) | async-done | bytes 131104 | tf_op jit(solution)/shard_map/all_to_all | solution.py:290
  55.5 0.1 slot_bias.1.b0
  55.6 1.5 %collective-permute-start.3 = (f32[100,128]{1,0:T(8,128)S(1)}, f32[100,128]{1,0:T(8,128)S(1)}, u32[]{:S(2)}, u32[]{:S(2)}) collective-permute-start(f32[100,128]{1,0:T(8,128)S(1)} %slot_bias.1.b0), channel_id=1, source_target_pairs={{0,2},{1,3},{2,0},{3,1},{4,6},{5,7},{6,4},{7,5},{8,10},{9,11},{10,... | collective-permute-start | bytes 153608 | tf_op jit(solution)/shard_map/ppermute | solution.py:287
  57.1 0.0 collective-permute-start.4
  57.1 2.7 %collective-permute-start.5 = (f32[100,128]{1,0:T(8,128)S(1)}, f32[100,128]{1,0:T(8,128)S(1)}, u32[]{:S(2)}, u32[]{:S(2)}) collective-permute-start(f32[100,128]{1,0:T(8,128)S(1)} %slot_bias.1.b0), channel_id=1, source_target_pairs={{0,3},{1,0},{2,1},{3,2},{4,7},{5,4},{6,5},{7,6},{8,11},{9,8},{10,9... | collective-permute-start | bytes 153608 | tf_op jit(solution)/shard_map/ppermute | solution.py:287
  59.8 0.0 collective-permute-done.6.spill
  59.8 2.3 %join.1 = f32[411,8,256]{2,1,0:T(8,128)} custom-call(f32[256,8,256]{2,1,0:T(8,128)S(1)} %grid.1, bf16[160,1024]{1,0:T(8,128)(2,1)S(1)} %get-tuple-element.23.rows, bf16[256,1024]{1,0:T(8,128)(2,1)S(1)} %get-tuple-element.18.colw, f32[8,1024]{1,0:T(8,128)S(1)} %get-tuple-element.19.roww, bf16[416,256]{1,0:T(8,128)(2,1)S(1)} %collective-permute-done.6.spill), custom_call_target="tpu_custom_call" | custom-call | tf_op jit(solution)/shard_map/join/pallas_call | solution.py:328
  62.1 0.0 collective-permute-done.3.b1
  62.1 0.0 collective-permute-done.4.b2
  62.1 0.0 collective-permute-done.5.b3
  62.1 0.6 %bias.1 = f32[100,128]{1,0:T(8,128)} custom-call(f32[100,128]{1,0:T(8,128)S(1)} %slot_bias.1.b0, f32[100,128]{1,0:T(8,128)S(1)} %collective-permute-done.3.b1, f32[100,128]{1,0:T(8,128)S(1)} %collective-permute-done.4.b2, f32[100,128]{1,0:T(8,128)S(1)} %collective-permute-done.5.b3), custom_call_target="tpu_custom_call" | custom-call | tf_op jit(solution)/shard_map/bias/pallas_call | solution.py:338
Async XLA Ops:
  34.6 9.8 %collective-permute-start = (bf16[416,256]{1,0:T(8,128)(2,1)S(1)}, bf16[416,256]{1,0:T(8,128)(2,1)S(1)}, u32[]{:S(2)}, u32[]{:S(2)}) collective-permute-start(bf16[416,256]{1,0:T(8,128)(2,1)S(1)} %get-tuple-element.16.a0), channel_id=1, source_target_pairs={{0,1},{1,2},{2,3},{3,0},{4,5},{5,6},{6,7},{7,4},{8,9},{9,10},{10,1... | collective-permute-start | bytes 638984 | tf_op jit(solution)/shard_map/ppermute | solution.py:287
  35.8 8.6 %collective-permute-start.1 = (bf16[416,256]{1,0:T(8,128)(2,1)S(1)}, bf16[416,256]{1,0:T(8,128)(2,1)S(1)}, u32[]{:S(2)}, u32[]{:S(2)}) collective-permute-start(bf16[416,256]{1,0:T(8,128)(2,1)S(1)} %get-tuple-element.16.a0), channel_id=1, source_target_pairs={{0,3},{1,0},{2,1},{3,2},{4,7},{5,4},{6,5},{7,6},{8,11},{9,8},{10,9... | collective-permute-start | bytes 638984 | tf_op jit(solution)/shard_map/ppermute | solution.py:287
  37.3 10.7 %collective-permute-start.2 = (bf16[416,256]{1,0:T(8,128)(2,1)S(1)}, bf16[416,256]{1,0:T(8,128)(2,1)S(1)}, u32[]{:S(2)}, u32[]{:S(2)}) collective-permute-start(bf16[416,256]{1,0:T(8,128)(2,1)S(1)} %get-tuple-element.16.a0), channel_id=1, source_target_pairs={{0,2},{1,3},{2,0},{3,1},{4,6},{5,7},{6,4},{7,5},{8,10},{9,11},{10,... | collective-permute-start | bytes 638984 | tf_op jit(solution)/shard_map/ppermute | solution.py:287
  38.8 16.7 %all-to-all-start.1 = ((f32[64,4,128]{2,1,0:T(4,128)}), f32[64,4,128]{2,1,0:T(4,128)S(1)}, u32[]{:S(2)}, u32[]{:S(2)}) async-start(f32[64,4,128]{2,1,0:T(4,128)} %bitcast.12), calls=%async_computation.1 | async-start | bytes 262144 | tf_op jit(solution)/shard_map/all_to_all | solution.py:290
  48.6 11.2 %collective-permute-start.6 = (bf16[416,256]{1,0:T(8,128)(2,1)S(1)}, bf16[416,256]{1,0:T(8,128)(2,1)S(1)}, u32[]{:S(2)}, u32[]{:S(2)}) collective-permute-start(bf16[416,256]{1,0:T(8,128)(2,1)S(1)} %get-tuple-element.24), channel_id=1, source_target_pairs={{0,4},{4,8},{8,12},{12,16},{16,20},{20,24},{24,28},{28,32},{32,36}... | collective-permute-start | bytes 638984 | tf_op jit(solution)/shard_map/ppermute | solution.py:309
  55.6 6.5 %collective-permute-start.3 = (f32[100,128]{1,0:T(8,128)S(1)}, f32[100,128]{1,0:T(8,128)S(1)}, u32[]{:S(2)}, u32[]{:S(2)}) collective-permute-start(f32[100,128]{1,0:T(8,128)S(1)} %slot_bias.1.b0), channel_id=1, source_target_pairs={{0,2},{1,3},{2,0},{3,1},{4,6},{5,7},{6,4},{7,5},{8,10},{9,11},{10,... | collective-permute-start | bytes 153608 | tf_op jit(solution)/shard_map/ppermute | solution.py:287
  57.1 5.0 %collective-permute-start.4 = (f32[100,128]{1,0:T(8,128)S(1)}, f32[100,128]{1,0:T(8,128)S(1)}, u32[]{:S(2)}, u32[]{:S(2)}) collective-permute-start(f32[100,128]{1,0:T(8,128)S(1)} %slot_bias.1.b0), channel_id=1, source_target_pairs={{0,1},{1,2},{2,3},{3,0},{4,5},{5,6},{6,7},{7,4},{8,9},{9,10},{10,1... | collective-permute-start | bytes 153608 | tf_op jit(solution)/shard_map/ppermute | solution.py:287
  57.1 5.0 %collective-permute-start.5 = (f32[100,128]{1,0:T(8,128)S(1)}, f32[100,128]{1,0:T(8,128)S(1)}, u32[]{:S(2)}, u32[]{:S(2)}) collective-permute-start(f32[100,128]{1,0:T(8,128)S(1)} %slot_bias.1.b0), channel_id=1, source_target_pairs={{0,3},{1,0},{2,1},{3,2},{4,7},{5,4},{6,5},{7,6},{8,11},{9,8},{10,9... | collective-permute-start | bytes 153608 | tf_op jit(solution)/shard_map/ppermute | solution.py:287

commit v10 on v9

--- a/solution.py
+++ b/solution.py
@@ -83,7 +83,7 @@
                 total = total + w[r : r + 16, c : c + 1] * kbuf[c, r : r + 16, :].astype(F32)
             acc[r : r + 16, 0:levels] = total
 
-    for i in range(steps // 2):
+    for i in range(steps - 1):
         sums(i)
     for copy in small_copies[2:]:
         copy.wait()
@@ -113,7 +113,7 @@
         part = (dot(hi, e, NN) + dot(lo, f, NN)).astype(BF16)
         extra = extra + dot(place, part, NN)
 
-    for i in range(steps // 2, steps):
+    for i in range(steps - 1, steps):
         sums(i)
     rows = acc[...].astype(BF16)
     size = rows_out // OUT_BLOCKS

time: 63 us -> 62.5 us (level)
  no operation moved by 1% of the time
where the time goes in v10:
time: 62.5 us; the launch traced here: 62.2 us
  blocking collectives  26.3 us (42%)
  starting transfers between devices  17.3 us (28%)
  Pallas kernels  12.1 us (19%)
  waiting for transfers between devices  5.78 us (9%)
  between operations  0.74 us (1%)
    all_to_all x1, blocking collectives, per_device(): lax.all_to_all(send.reshape(n_tile, 2 * CAP, WIDE), 'tile', 0, 0, tiled=T...  26.3 us
    ppermute x6, starting transfers between devices, around(): lax.ppermute(x, 'slot', [(i, (i + d) % n_slot) for i in range(n_slot)])  8.41 us
    pallas_call x1, Pallas kernels, per_device(): pl.pallas_call(functools.partial(send_kernel, steps=steps), out_shape=jax...  5.99 us
    all_to_all x1, starting transfers between devices, per_device(): lax.all_to_all(chunk.reshape(n_tile, CAP, 128), 'tile', 0, 0, tiled=True)  5.55 us
    ppermute x6, waiting for transfers between devices, around(): lax.ppermute(x, 'slot', [(i, (i + d) % n_slot) for i in range(n_slot)])  3.58 us
    ppermute x1, starting transfers between devices, per_device(): arrived = lax.ppermute(spill, ('tile', 'slot'), pairs)  3.29 us
    pallas_call x1, Pallas kernels, per_device(): pl.pallas_call(join_kernel, out_shape=jax.ShapeDtypeStruct((levels, BLOCK...  2.27 us
    all_to_all x1, waiting for transfers between devices, per_device(): lax.all_to_all(chunk.reshape(n_tile, CAP, 128), 'tile', 0, 0, tiled=True)  2.2 us
  transfers between devices with their start and end apart: 8, of which 2 were waited for; matrix products, arithmetic and copies ran while one was open for 0% of the time, Pallas kernels for 7%

profile of v10, /device:TPU:1, one launch (start us, length us, event | category | flops | bytes accessed | tf_op | source)
XLA Modules:
  0.0 62.2 jit_solution(15442310154982319013)
XLA Ops:
  0.6 6.0 %send.1 = bf16[512,256]{1,0:T(8,128)(2,1)} custom-call(bf16[100,96,411]{2,1,0:T(8,128)(2,1)} %bitcast.17, bf16[96,100]{1,0:T(8,128)(2,1)} %refs_1_.1, f32[1,100]{1,0:T(1,128)} %bitcast.21, s32[1,96]{1,0:T(1,128)} %bitcast.22, bf16[1,96]{1,0:T(2,128)(2,1)} %bitcast.23, bf16[1,96]{1,0:T(2,128)(2,1)} %bitcast.24, s32[1,96]{1,0:T(1,128)} %bitcast.25, ...), custom_call_target="tpu_custom_call" | custom-call | tf_op jit(solution)/shard_map/send/pallas_call | solution.py:259
  6.6 26.3 %all_to_all.10 = bf16[64,8,256]{2,1,0:T(8,128)(2,1)S(1)} all-to-all(bf16[64,8,256]{2,1,0:T(8,128)(2,1)} %bitcast.19), channel_id=1, replica_groups=mesh['tile'=64,'slot'=4] {'tile'}, dimensions={0} | all-to-all | bytes 524288 | tf_op jit(solution)/shard_map/all_to_all | solution.py:276
  33.0 1.1 %turn.1 = (bf16[416,256]{1,0:T(8,128)(2,1)S(1)}, f32[256,128]{1,0:T(8,128)}) custom-call(bf16[512,256]{1,0:T(8,128)(2,1)S(1)} %bitcast.15), custom_call_target="tpu_custom_call" | custom-call | tf_op jit(solution)/shard_map/turn/pallas_call | solution.py:277
  34.1 1.2 %collective-permute-start = (bf16[416,256]{1,0:T(8,128)(2,1)S(1)}, bf16[416,256]{1,0:T(8,128)(2,1)S(1)}, u32[]{:S(2)}, u32[]{:S(2)}) collective-permute-start(bf16[416,256]{1,0:T(8,128)(2,1)S(1)} %get-tuple-element.16.a0), channel_id=1, source_target_pairs={{0,1},{1,2},{2,3},{3,0},{4,5},{5,6},{6,7},{7,4},{8,9},{9,10},{10,1... | collective-permute-start | bytes 638984 | tf_op jit(solution)/shard_map/ppermute | solution.py:287
  35.3 1.5 %collective-permute-start.1 = (bf16[416,256]{1,0:T(8,128)(2,1)S(1)}, bf16[416,256]{1,0:T(8,128)(2,1)S(1)}, u32[]{:S(2)}, u32[]{:S(2)}) collective-permute-start(bf16[416,256]{1,0:T(8,128)(2,1)S(1)} %get-tuple-element.16.a0), channel_id=1, source_target_pairs={{0,3},{1,0},{2,1},{3,2},{4,7},{5,4},{6,5},{7,6},{8,11},{9,8},{10,9... | collective-permute-start | bytes 638984 | tf_op jit(solution)/shard_map/ppermute | solution.py:287
  36.8 1.5 %collective-permute-start.2 = (bf16[416,256]{1,0:T(8,128)(2,1)S(1)}, bf16[416,256]{1,0:T(8,128)(2,1)S(1)}, u32[]{:S(2)}, u32[]{:S(2)}) collective-permute-start(bf16[416,256]{1,0:T(8,128)(2,1)S(1)} %get-tuple-element.16.a0), channel_id=1, source_target_pairs={{0,2},{1,3},{2,0},{3,1},{4,6},{5,7},{6,4},{7,5},{8,10},{9,11},{10,... | collective-permute-start | bytes 638984 | tf_op jit(solution)/shard_map/ppermute | solution.py:287
  38.3 5.6 %all-to-all-start.1 = ((f32[64,4,128]{2,1,0:T(4,128)}), f32[64,4,128]{2,1,0:T(4,128)S(1)}, u32[]{:S(2)}, u32[]{:S(2)}) async-start(f32[64,4,128]{2,1,0:T(4,128)} %bitcast.12), calls=%async_computation.1 | async-start | bytes 262144 | tf_op jit(solution)/shard_map/all_to_all | solution.py:290
  43.9 0.0 collective-permute-done.a1
  43.9 0.0 collective-permute-done.1.a2
  43.9 3.6 %collective-permute-done.2.a3 = bf16[416,256]{1,0:T(8,128)(2,1)S(1)} collective-permute-done((bf16[416,256]{1,0:T(8,128)(2,1)S(1)}, bf16[416,256]{1,0:T(8,128)(2,1)S(1)}, u32[]{:S(2)}, u32[]{:S(2)}) %collective-permute-start.2) | collective-permute-done | bytes 213024 | tf_op jit(solution)/shard_map/ppermute | solution.py:287
  47.5 0.6 prep.1
  48.1 3.3 %collective-permute-start.6 = (bf16[416,256]{1,0:T(8,128)(2,1)S(1)}, bf16[416,256]{1,0:T(8,128)(2,1)S(1)}, u32[]{:S(2)}, u32[]{:S(2)}) collective-permute-start(bf16[416,256]{1,0:T(8,128)(2,1)S(1)} %get-tuple-element.24), channel_id=1, source_target_pairs={{0,4},{4,8},{8,12},{12,16},{16,20},{20,24},{24,28},{28,32},{32,36}... | collective-permute-start | bytes 638984 | tf_op jit(solution)/shard_map/ppermute | solution.py:309
  51.4 1.4 %grid.1 = f32[256,8,256]{2,1,0:T(8,128)S(1)} custom-call(bf16[256,1024]{1,0:T(8,128)(2,1)S(1)} %get-tuple-element.17.rows, bf16[256,1024]{1,0:T(8,128)(2,1)S(1)} %get-tuple-element.18.colw, f32[8,1024]{1,0:T(8,128)S(1)} %get-tuple-element.19.roww), custom_call_target="tpu_custom_call" | custom-call | tf_op jit(solution)/shard_map/grid/pallas_call | solution.py:310
  52.8 2.2 %all-to-all-done.1 = f32[64,4,128]{2,1,0:T(4,128)S(1)} async-done(((f32[64,4,128]{2,1,0:T(4,128)}), f32[64,4,128]{2,1,0:T(4,128)S(1)}, u32[]{:S(2)}, u32[]{:S(2)}) %all-to-all-start.1) | async-done | bytes 131104 | tf_op jit(solution)/shard_map/all_to_all | solution.py:290
  55.0 0.1 slot_bias.1.b0
  55.1 1.5 %collective-permute-start.3 = (f32[100,128]{1,0:T(8,128)S(1)}, f32[100,128]{1,0:T(8,128)S(1)}, u32[]{:S(2)}, u32[]{:S(2)}) collective-permute-start(f32[100,128]{1,0:T(8,128)S(1)} %slot_bias.1.b0), channel_id=1, source_target_pairs={{0,2},{1,3},{2,0},{3,1},{4,6},{5,7},{6,4},{7,5},{8,10},{9,11},{10,... | collective-permute-start | bytes 153608 | tf_op jit(solution)/shard_map/ppermute | solution.py:287
  56.6 0.0 collective-permute-start.4
  56.6 2.7 %collective-permute-start.5 = (f32[100,128]{1,0:T(8,128)S(1)}, f32[100,128]{1,0:T(8,128)S(1)}, u32[]{:S(2)}, u32[]{:S(2)}) collective-permute-start(f32[100,128]{1,0:T(8,128)S(1)} %slot_bias.1.b0), channel_id=1, source_target_pairs={{0,3},{1,0},{2,1},{3,2},{4,7},{5,4},{6,5},{7,6},{8,11},{9,8},{10,9... | collective-permute-start | bytes 153608 | tf_op jit(solution)/shard_map/ppermute | solution.py:287
  59.3 0.0 collective-permute-done.6.spill
  59.3 2.3 %join.1 = f32[411,8,256]{2,1,0:T(8,128)} custom-call(f32[256,8,256]{2,1,0:T(8,128)S(1)} %grid.1, bf16[160,1024]{1,0:T(8,128)(2,1)S(1)} %get-tuple-element.23.rows, bf16[256,1024]{1,0:T(8,128)(2,1)S(1)} %get-tuple-element.18.colw, f32[8,1024]{1,0:T(8,128)S(1)} %get-tuple-element.19.roww, bf16[416,256]{1,0:T(8,128)(2,1)S(1)} %collective-permute-done.6.spill), custom_call_target="tpu_custom_call" | custom-call | tf_op jit(solution)/shard_map/join/pallas_call | solution.py:328
  61.6 0.0 collective-permute-done.3.b1
  61.6 0.0 collective-permute-done.4.b2
  61.6 0.0 collective-permute-done.5.b3
  61.6 0.6 %bias.1 = f32[100,128]{1,0:T(8,128)} custom-call(f32[100,128]{1,0:T(8,128)S(1)} %slot_bias.1.b0, f32[100,128]{1,0:T(8,128)S(1)} %collective-permute-done.3.b1, f32[100,128]{1,0:T(8,128)S(1)} %collective-permute-done.4.b2, f32[100,128]{1,0:T(8,128)S(1)} %collective-permute-done.5.b3), custom_call_target="tpu_custom_call" | custom-call | tf_op jit(solution)/shard_map/bias/pallas_call | solution.py:338
Async XLA Ops:
  34.1 9.8 %collective-permute-start = (bf16[416,256]{1,0:T(8,128)(2,1)S(1)}, bf16[416,256]{1,0:T(8,128)(2,1)S(1)}, u32[]{:S(2)}, u32[]{:S(2)}) collective-permute-start(bf16[416,256]{1,0:T(8,128)(2,1)S(1)} %get-tuple-element.16.a0), channel_id=1, source_target_pairs={{0,1},{1,2},{2,3},{3,0},{4,5},{5,6},{6,7},{7,4},{8,9},{9,10},{10,1... | collective-permute-start | bytes 638984 | tf_op jit(solution)/shard_map/ppermute | solution.py:287
  35.3 8.6 %collective-permute-start.1 = (bf16[416,256]{1,0:T(8,128)(2,1)S(1)}, bf16[416,256]{1,0:T(8,128)(2,1)S(1)}, u32[]{:S(2)}, u32[]{:S(2)}) collective-permute-start(bf16[416,256]{1,0:T(8,128)(2,1)S(1)} %get-tuple-element.16.a0), channel_id=1, source_target_pairs={{0,3},{1,0},{2,1},{3,2},{4,7},{5,4},{6,5},{7,6},{8,11},{9,8},{10,9... | collective-permute-start | bytes 638984 | tf_op jit(solution)/shard_map/ppermute | solution.py:287
  36.8 10.7 %collective-permute-start.2 = (bf16[416,256]{1,0:T(8,128)(2,1)S(1)}, bf16[416,256]{1,0:T(8,128)(2,1)S(1)}, u32[]{:S(2)}, u32[]{:S(2)}) collective-permute-start(bf16[416,256]{1,0:T(8,128)(2,1)S(1)} %get-tuple-element.16.a0), channel_id=1, source_target_pairs={{0,2},{1,3},{2,0},{3,1},{4,6},{5,7},{6,4},{7,5},{8,10},{9,11},{10,... | collective-permute-start | bytes 638984 | tf_op jit(solution)/shard_map/ppermute | solution.py:287
  38.3 16.7 %all-to-all-start.1 = ((f32[64,4,128]{2,1,0:T(4,128)}), f32[64,4,128]{2,1,0:T(4,128)S(1)}, u32[]{:S(2)}, u32[]{:S(2)}) async-start(f32[64,4,128]{2,1,0:T(4,128)} %bitcast.12), calls=%async_computation.1 | async-start | bytes 262144 | tf_op jit(solution)/shard_map/all_to_all | solution.py:290
  48.1 11.2 %collective-permute-start.6 = (bf16[416,256]{1,0:T(8,128)(2,1)S(1)}, bf16[416,256]{1,0:T(8,128)(2,1)S(1)}, u32[]{:S(2)}, u32[]{:S(2)}) collective-permute-start(bf16[416,256]{1,0:T(8,128)(2,1)S(1)} %get-tuple-element.24), channel_id=1, source_target_pairs={{0,4},{4,8},{8,12},{12,16},{16,20},{20,24},{24,28},{28,32},{32,36}... | collective-permute-start | bytes 638984 | tf_op jit(solution)/shard_map/ppermute | solution.py:309
  55.1 6.5 %collective-permute-start.3 = (f32[100,128]{1,0:T(8,128)S(1)}, f32[100,128]{1,0:T(8,128)S(1)}, u32[]{:S(2)}, u32[]{:S(2)}) collective-permute-start(f32[100,128]{1,0:T(8,128)S(1)} %slot_bias.1.b0), channel_id=1, source_target_pairs={{0,2},{1,3},{2,0},{3,1},{4,6},{5,7},{6,4},{7,5},{8,10},{9,11},{10,... | collective-permute-start | bytes 153608 | tf_op jit(solution)/shard_map/ppermute | solution.py:287
  56.6 5.0 %collective-permute-start.4 = (f32[100,128]{1,0:T(8,128)S(1)}, f32[100,128]{1,0:T(8,128)S(1)}, u32[]{:S(2)}, u32[]{:S(2)}) collective-permute-start(f32[100,128]{1,0:T(8,128)S(1)} %slot_bias.1.b0), channel_id=1, source_target_pairs={{0,1},{1,2},{2,3},{3,0},{4,5},{5,6},{6,7},{7,4},{8,9},{9,10},{10,1... | collective-permute-start | bytes 153608 | tf_op jit(solution)/shard_map/ppermute | solution.py:287
  56.6 5.0 %collective-permute-start.5 = (f32[100,128]{1,0:T(8,128)S(1)}, f32[100,128]{1,0:T(8,128)S(1)}, u32[]{:S(2)}, u32[]{:S(2)}) collective-permute-start(f32[100,128]{1,0:T(8,128)S(1)} %slot_bias.1.b0), channel_id=1, source_target_pairs={{0,3},{1,0},{2,1},{3,2},{4,7},{5,4},{6,5},{7,6},{8,11},{9,8},{10,9... | collective-permute-start | bytes 153608 | tf_op jit(solution)/shard_map/ppermute | solution.py:287

commit v11 on v10

--- a/solution.py
+++ b/solution.py
@@ -324,7 +324,7 @@
         compiler_params=params,
         name="slot_bias",
     )(chunks)
-    biases = around(slot_bias, (2, 1, 3))
+    biases = around(slot_bias, (1, 3, 2))
     grid = pl.pallas_call(
         join_kernel,
         out_shape=jax.ShapeDtypeStruct((levels, BLOCK, GC), F32),

time: 62.5 us -> 63.2 us (1.011)
  waiting for transfers between devices: 5.78 us -> 7.73 us
  starting transfers between devices: 17.3 us -> 16 us
    ppermute x6, waiting for transfers between devices: 3.58 us -> 5.53 us  [around(): lax.ppermute(x, 'slot', [(i, (i + d) % n_slot) for i in range(n_slot)])]
    ppermute x6, starting transfers between devices: 8.41 us -> 7.19 us  [around(): lax.ppermute(x, 'slot', [(i, (i + d) % n_slot) for i in range(n_slot)])]
  transfers between devices with their start and end apart: 8 -> 8, of which waited for: 2 -> 3; matrix products, arithmetic and copies ran while one was open for 0% -> 0% of each run, Pallas kernels for 7% -> 7%
where the time goes in v11:
time: 63.2 us; the launch traced here: 63 us
  blocking collectives  26.3 us (42%)
  starting transfers between devices  16 us (25%)
  Pallas kernels  12.1 us (19%)
  waiting for transfers between devices  7.73 us (12%)
  between operations  0.73 us (1%)
    all_to_all x1, blocking collectives, per_device(): lax.all_to_all(send.reshape(n_tile, 2 * CAP, WIDE), 'tile', 0, 0, tiled=T...  26.3 us
    ppermute x6, starting transfers between devices, around(): lax.ppermute(x, 'slot', [(i, (i + d) % n_slot) for i in range(n_slot)])  7.19 us
    pallas_call x1, Pallas kernels, per_device(): pl.pallas_call(functools.partial(send_kernel, steps=steps), out_shape=jax...  5.99 us
    all_to_all x1, starting transfers between devices, per_device(): lax.all_to_all(chunk.reshape(n_tile, CAP, 128), 'tile', 0, 0, tiled=True)  5.55 us
    ppermute x6, waiting for transfers between devices, around(): lax.ppermute(x, 'slot', [(i, (i + d) % n_slot) for i in range(n_slot)])  5.53 us
    ppermute x1, starting transfers between devices, per_device(): arrived = lax.ppermute(spill, ('tile', 'slot'), pairs)  3.29 us
    pallas_call x1, Pallas kernels, per_device(): pl.pallas_call(join_kernel, out_shape=jax.ShapeDtypeStruct((levels, BLOCK...  2.27 us
    all_to_all x1, waiting for transfers between devices, per_device(): lax.all_to_all(chunk.reshape(n_tile, CAP, 128), 'tile', 0, 0, tiled=True)  2.2 us
  transfers between devices with their start and end apart: 8, of which 3 were waited for; matrix products, arithmetic and copies ran while one was open for 0% of the time, Pallas kernels for 7%

profile of v11, /device:TPU:1, one launch (start us, length us, event | category | flops | bytes accessed | tf_op | source)
XLA Modules:
  0.0 63.0 jit_solution(18222340812101639707)
XLA Ops:
  0.6 6.0 %send.1 = bf16[512,256]{1,0:T(8,128)(2,1)} custom-call(bf16[100,96,411]{2,1,0:T(8,128)(2,1)} %bitcast.17, bf16[96,100]{1,0:T(8,128)(2,1)} %refs_1_.1, f32[1,100]{1,0:T(1,128)} %bitcast.21, s32[1,96]{1,0:T(1,128)} %bitcast.22, bf16[1,96]{1,0:T(2,128)(2,1)} %bitcast.23, bf16[1,96]{1,0:T(2,128)(2,1)} %bitcast.24, s32[1,96]{1,0:T(1,128)} %bitcast.25, ...), custom_call_target="tpu_custom_call" | custom-call | tf_op jit(solution)/shard_map/send/pallas_call | solution.py:259
  6.6 26.3 %all_to_all.10 = bf16[64,8,256]{2,1,0:T(8,128)(2,1)S(1)} all-to-all(bf16[64,8,256]{2,1,0:T(8,128)(2,1)} %bitcast.19), channel_id=1, replica_groups=mesh['tile'=64,'slot'=4] {'tile'}, dimensions={0} | all-to-all | bytes 524288 | tf_op jit(solution)/shard_map/all_to_all | solution.py:276
  33.0 1.1 %turn.1 = (bf16[416,256]{1,0:T(8,128)(2,1)S(1)}, f32[256,128]{1,0:T(8,128)}) custom-call(bf16[512,256]{1,0:T(8,128)(2,1)S(1)} %bitcast.15), custom_call_target="tpu_custom_call" | custom-call | tf_op jit(solution)/shard_map/turn/pallas_call | solution.py:277
  34.1 1.2 %collective-permute-start = (bf16[416,256]{1,0:T(8,128)(2,1)S(1)}, bf16[416,256]{1,0:T(8,128)(2,1)S(1)}, u32[]{:S(2)}, u32[]{:S(2)}) collective-permute-start(bf16[416,256]{1,0:T(8,128)(2,1)S(1)} %get-tuple-element.16.a0), channel_id=1, source_target_pairs={{0,1},{1,2},{2,3},{3,0},{4,5},{5,6},{6,7},{7,4},{8,9},{9,10},{10,1... | collective-permute-start | bytes 638984 | tf_op jit(solution)/shard_map/ppermute | solution.py:287
  35.3 1.5 %collective-permute-start.1 = (bf16[416,256]{1,0:T(8,128)(2,1)S(1)}, bf16[416,256]{1,0:T(8,128)(2,1)S(1)}, u32[]{:S(2)}, u32[]{:S(2)}) collective-permute-start(bf16[416,256]{1,0:T(8,128)(2,1)S(1)} %get-tuple-element.16.a0), channel_id=1, source_target_pairs={{0,3},{1,0},{2,1},{3,2},{4,7},{5,4},{6,5},{7,6},{8,11},{9,8},{10,9... | collective-permute-start | bytes 638984 | tf_op jit(solution)/shard_map/ppermute | solution.py:287
  36.8 1.5 %collective-permute-start.2 = (bf16[416,256]{1,0:T(8,128)(2,1)S(1)}, bf16[416,256]{1,0:T(8,128)(2,1)S(1)}, u32[]{:S(2)}, u32[]{:S(2)}) collective-permute-start(bf16[416,256]{1,0:T(8,128)(2,1)S(1)} %get-tuple-element.16.a0), channel_id=1, source_target_pairs={{0,2},{1,3},{2,0},{3,1},{4,6},{5,7},{6,4},{7,5},{8,10},{9,11},{10,... | collective-permute-start | bytes 638984 | tf_op jit(solution)/shard_map/ppermute | solution.py:287
  38.3 5.6 %all-to-all-start.1 = ((f32[64,4,128]{2,1,0:T(4,128)}), f32[64,4,128]{2,1,0:T(4,128)S(1)}, u32[]{:S(2)}, u32[]{:S(2)}) async-start(f32[64,4,128]{2,1,0:T(4,128)} %bitcast.12), calls=%async_computation.1 | async-start | bytes 262144 | tf_op jit(solution)/shard_map/all_to_all | solution.py:290
  43.9 0.0 collective-permute-done.a1
  43.9 0.0 collective-permute-done.1.a2
  43.9 3.6 %collective-permute-done.2.a3 = bf16[416,256]{1,0:T(8,128)(2,1)S(1)} collective-permute-done((bf16[416,256]{1,0:T(8,128)(2,1)S(1)}, bf16[416,256]{1,0:T(8,128)(2,1)S(1)}, u32[]{:S(2)}, u32[]{:S(2)}) %collective-permute-start.2) | collective-permute-done | bytes 213024 | tf_op jit(solution)/shard_map/ppermute | solution.py:287
  47.5 0.6 prep.1
  48.1 3.3 %collective-permute-start.6 = (bf16[416,256]{1,0:T(8,128)(2,1)S(1)}, bf16[416,256]{1,0:T(8,128)(2,1)S(1)}, u32[]{:S(2)}, u32[]{:S(2)}) collective-permute-start(bf16[416,256]{1,0:T(8,128)(2,1)S(1)} %get-tuple-element.24), channel_id=1, source_target_pairs={{0,4},{4,8},{8,12},{12,16},{16,20},{20,24},{24,28},{28,32},{32,36}... | collective-permute-start | bytes 638984 | tf_op jit(solution)/shard_map/ppermute | solution.py:309
  51.4 1.4 %grid.1 = f32[256,8,256]{2,1,0:T(8,128)S(1)} custom-call(bf16[256,1024]{1,0:T(8,128)(2,1)S(1)} %get-tuple-element.17.rows, bf16[256,1024]{1,0:T(8,128)(2,1)S(1)} %get-tuple-element.18.colw, f32[8,1024]{1,0:T(8,128)S(1)} %get-tuple-element.19.roww), custom_call_target="tpu_custom_call" | custom-call | tf_op jit(solution)/shard_map/grid/pallas_call | solution.py:310
  52.8 2.2 %all-to-all-done.1 = f32[64,4,128]{2,1,0:T(4,128)S(1)} async-done(((f32[64,4,128]{2,1,0:T(4,128)}), f32[64,4,128]{2,1,0:T(4,128)S(1)}, u32[]{:S(2)}, u32[]{:S(2)}) %all-to-all-start.1) | async-done | bytes 131104 | tf_op jit(solution)/shard_map/all_to_all | solution.py:290
  55.0 0.1 slot_bias.1.b0
  55.1 0.4 collective-permute-start.3
  55.5 2.4 %collective-permute-start.4 = (f32[100,128]{1,0:T(8,128)S(1)}, f32[100,128]{1,0:T(8,128)S(1)}, u32[]{:S(2)}, u32[]{:S(2)}) collective-permute-start(f32[100,128]{1,0:T(8,128)S(1)} %slot_bias.1.b0), channel_id=1, source_target_pairs={{0,3},{1,0},{2,1},{3,2},{4,7},{5,4},{6,5},{7,6},{8,11},{9,8},{10,9... | collective-permute-start | bytes 153608 | tf_op jit(solution)/shard_map/ppermute | solution.py:287
  57.8 0.2 collective-permute-start.5
  58.1 0.0 collective-permute-done.6.spill
  58.1 2.3 %join.1 = f32[411,8,256]{2,1,0:T(8,128)} custom-call(f32[256,8,256]{2,1,0:T(8,128)S(1)} %grid.1, bf16[160,1024]{1,0:T(8,128)(2,1)S(1)} %get-tuple-element.23.rows, bf16[256,1024]{1,0:T(8,128)(2,1)S(1)} %get-tuple-element.18.colw, f32[8,1024]{1,0:T(8,128)S(1)} %get-tuple-element.19.roww, bf16[416,256]{1,0:T(8,128)(2,1)S(1)} %collective-permute-done.6.spill), custom_call_target="tpu_custom_call" | custom-call | tf_op jit(solution)/shard_map/join/pallas_call | solution.py:328
  60.3 0.0 collective-permute-done.3.b1
  60.3 0.0 collective-permute-done.4.b2
  60.4 2.0 %collective-permute-done.5.b3 = f32[100,128]{1,0:T(8,128)S(1)} collective-permute-done((f32[100,128]{1,0:T(8,128)S(1)}, f32[100,128]{1,0:T(8,128)S(1)}, u32[]{:S(2)}, u32[]{:S(2)}) %collective-permute-start.5) | collective-permute-done | bytes 51232 | tf_op jit(solution)/shard_map/ppermute | solution.py:287
  62.3 0.6 %bias.1 = f32[100,128]{1,0:T(8,128)} custom-call(f32[100,128]{1,0:T(8,128)S(1)} %slot_bias.1.b0, f32[100,128]{1,0:T(8,128)S(1)} %collective-permute-done.3.b1, f32[100,128]{1,0:T(8,128)S(1)} %collective-permute-done.4.b2, f32[100,128]{1,0:T(8,128)S(1)} %collective-permute-done.5.b3), custom_call_target="tpu_custom_call" | custom-call | tf_op jit(solution)/shard_map/bias/pallas_call | solution.py:338
Async XLA Ops:
  34.1 9.8 %collective-permute-start = (bf16[416,256]{1,0:T(8,128)(2,1)S(1)}, bf16[416,256]{1,0:T(8,128)(2,1)S(1)}, u32[]{:S(2)}, u32[]{:S(2)}) collective-permute-start(bf16[416,256]{1,0:T(8,128)(2,1)S(1)} %get-tuple-element.16.a0), channel_id=1, source_target_pairs={{0,1},{1,2},{2,3},{3,0},{4,5},{5,6},{6,7},{7,4},{8,9},{9,10},{10,1... | collective-permute-start | bytes 638984 | tf_op jit(solution)/shard_map/ppermute | solution.py:287
  35.3 8.6 %collective-permute-start.1 = (bf16[416,256]{1,0:T(8,128)(2,1)S(1)}, bf16[416,256]{1,0:T(8,128)(2,1)S(1)}, u32[]{:S(2)}, u32[]{:S(2)}) collective-permute-start(bf16[416,256]{1,0:T(8,128)(2,1)S(1)} %get-tuple-element.16.a0), channel_id=1, source_target_pairs={{0,3},{1,0},{2,1},{3,2},{4,7},{5,4},{6,5},{7,6},{8,11},{9,8},{10,9... | collective-permute-start | bytes 638984 | tf_op jit(solution)/shard_map/ppermute | solution.py:287
  36.8 10.7 %collective-permute-start.2 = (bf16[416,256]{1,0:T(8,128)(2,1)S(1)}, bf16[416,256]{1,0:T(8,128)(2,1)S(1)}, u32[]{:S(2)}, u32[]{:S(2)}) collective-permute-start(bf16[416,256]{1,0:T(8,128)(2,1)S(1)} %get-tuple-element.16.a0), channel_id=1, source_target_pairs={{0,2},{1,3},{2,0},{3,1},{4,6},{5,7},{6,4},{7,5},{8,10},{9,11},{10,... | collective-permute-start | bytes 638984 | tf_op jit(solution)/shard_map/ppermute | solution.py:287
  38.3 16.7 %all-to-all-start.1 = ((f32[64,4,128]{2,1,0:T(4,128)}), f32[64,4,128]{2,1,0:T(4,128)S(1)}, u32[]{:S(2)}, u32[]{:S(2)}) async-start(f32[64,4,128]{2,1,0:T(4,128)} %bitcast.12), calls=%async_computation.1 | async-start | bytes 262144 | tf_op jit(solution)/shard_map/all_to_all | solution.py:290
  48.1 10.0 %collective-permute-start.6 = (bf16[416,256]{1,0:T(8,128)(2,1)S(1)}, bf16[416,256]{1,0:T(8,128)(2,1)S(1)}, u32[]{:S(2)}, u32[]{:S(2)}) collective-permute-start(bf16[416,256]{1,0:T(8,128)(2,1)S(1)} %get-tuple-element.24), channel_id=1, source_target_pairs={{0,4},{4,8},{8,12},{12,16},{16,20},{20,24},{24,28},{28,32},{32,36}... | collective-permute-start | bytes 638984 | tf_op jit(solution)/shard_map/ppermute | solution.py:309
  55.1 5.3 %collective-permute-start.3 = (f32[100,128]{1,0:T(8,128)S(1)}, f32[100,128]{1,0:T(8,128)S(1)}, u32[]{:S(2)}, u32[]{:S(2)}) collective-permute-start(f32[100,128]{1,0:T(8,128)S(1)} %slot_bias.1.b0), channel_id=1, source_target_pairs={{0,1},{1,2},{2,3},{3,0},{4,5},{5,6},{6,7},{7,4},{8,9},{9,10},{10,1... | collective-permute-start | bytes 153608 | tf_op jit(solution)/shard_map/ppermute | solution.py:287
  55.5 4.9 %collective-permute-start.4 = (f32[100,128]{1,0:T(8,128)S(1)}, f32[100,128]{1,0:T(8,128)S(1)}, u32[]{:S(2)}, u32[]{:S(2)}) collective-permute-start(f32[100,128]{1,0:T(8,128)S(1)} %slot_bias.1.b0), channel_id=1, source_target_pairs={{0,3},{1,0},{2,1},{3,2},{4,7},{5,4},{6,5},{7,6},{8,11},{9,8},{10,9... | collective-permute-start | bytes 153608 | tf_op jit(solution)/shard_map/ppermute | solution.py:287
  57.8 4.5 %collective-permute-start.5 = (f32[100,128]{1,0:T(8,128)S(1)}, f32[100,128]{1,0:T(8,128)S(1)}, u32[]{:S(2)}, u32[]{:S(2)}) collective-permute-start(f32[100,128]{1,0:T(8,128)S(1)} %slot_bias.1.b0), channel_id=1, source_target_pairs={{0,2},{1,3},{2,0},{3,1},{4,6},{5,7},{6,4},{7,5},{8,10},{9,11},{10,... | collective-permute-start | bytes 153608 | tf_op jit(solution)/shard_map/ppermute | solution.py:287
